TPU v7x, 256 devices: a whole 4x4x8 slice. The times are simulated.
256 devices in a mesh: grp: 4 (over x_hi, core), dev: 64 (over x_lo, y, z).
Axes of the slice: x: 4 (x_hi: 2, x_lo: 2; x = x_hi * 2 + x_lo), y: 4, z: 8, core: 2. Of those that a mesh axis runs over, the one named last changes fastest.
Arguments:
- hidden_in: bfloat16 [32, 5120], P('grp', 'dev'), may hold values from -6 to 6
- w_qkv: bfloat16 [5120, 7168], P(None, ('grp', 'dev')), may hold values from -0.078125 to 0.078125
- w_o: bfloat16 [5120, 5120], P(None, ('grp', 'dev')), may hold values from -0.3125 to 0.3125
- key_cache: bfloat16 [32, 8192, 1024], P('grp', 'dev'), may hold values from -144 to 144
- value_cache: bfloat16 [32, 8192, 1024], P('grp', 'dev'), may hold values from -6 to 6
- lengths: int32 [32], P('grp'), may hold values from 1 to 8192, as said below
- finished: int32 [32], P('grp'), may hold values from 0 to 1, as said below
- assignment: int32 [32], P('grp'), may hold values from 0 to 3, as said below
Outputs:
- hidden_out: float32 [32, 5120], P('grp', 'dev')
- returned: float32 [32, 5120], P('grp', 'dev')
- w_qkv_gen: bfloat16 [5120, 7168], P('dev')
- w_o_gen: bfloat16 [5120, 5120], P('dev')
Inputs may be any that keep to these rules, and one draw needn't show every extreme that they name: `lengths`: some row has exactly 8192. `assignment`: within each generator group every learner shard is named by exactly 2 rows. One learner shard, the same for all generator groups, has all its 2 rows finished in every group.
All inputs are finite; a program needn't handle non-finite values.
Results may differ from a plain program's by a relative error of at most 0.028.
Values may be sent and summed in bfloat16 or wider, within the bound.
No kernel may reach another device: no remote copies, remote signals or barrier semaphores. Data moves between devices by JAX's collectives and lax.ppermute only.
A program may use at most 64 MiB of HBM per device.

v0:
```python
import math

import jax
import jax.numpy as jnp
from jax import lax
from jax.sharding import PartitionSpec as P

QUERY_HEADS = 40
KEY_VALUE_HEADS = 8
HEAD_SIZE = 128


NEG_FILL = -1e30


def combined_all(part, axis, combine):
    gathered = jax.tree.map(lambda a: lax.all_gather(a, axis), part)

    def take(source):
        return jax.tree.map(lambda a: lax.dynamic_index_in_dim(a, source, 0, False), gathered)

    return lax.fori_loop(
        1, lax.axis_size(axis), lambda source, state: combine(state, take(source)), take(0)
    )


def reorder_columns(matrix, n_groups, n_devs):
    height = matrix.shape[0]
    each_width = matrix.shape[1] // (n_groups * n_devs)
    split_up = matrix.reshape(height, n_devs, n_groups, each_width)
    return jnp.transpose(split_up, (0, 2, 1, 3)).reshape(height, matrix.shape[1])


def combine_parts(first, second):
    highest = jnp.maximum(first[0], second[0])
    left_factor = jnp.exp(first[0] - highest)
    right_factor = jnp.exp(second[0] - highest)
    sums = first[1] * left_factor + second[1] * right_factor
    values = first[2] * left_factor[..., None] + second[2] * right_factor[..., None]
    return (highest, sums, values)


def shards(hidden_in, w_qkv, w_o, key_cache, value_cache, lengths, finished, assignment):
    n_groups = lax.axis_size("grp")
    n_devs = lax.axis_size("dev")
    copies = (
        lax.all_gather(w_qkv, "grp", axis=1, tiled=True),
        lax.all_gather(w_o, "grp", axis=1, tiled=True),
    )
    spread = (
        lax.all_to_all(copies[0], "dev", split_axis=0, concat_axis=1, tiled=True),
        lax.all_to_all(copies[1], "dev", split_axis=0, concat_axis=1, tiled=True),
    )
    qkv_rows = reorder_columns(spread[0], n_groups, n_devs)
    out_rows = reorder_columns(spread[1], n_groups, n_devs)
    partial_qkv = jnp.dot(hidden_in, qkv_rows, preferred_element_type=jnp.float32)
    query_key_value_full = lax.psum(partial_qkv, "dev").astype(jnp.bfloat16)
    row_count = hidden_in.shape[0]
    rows_per_group = QUERY_HEADS // KEY_VALUE_HEADS
    query_width = QUERY_HEADS * HEAD_SIZE
    key_value_width = KEY_VALUE_HEADS * HEAD_SIZE
    score_factor = 1.0 / math.sqrt(HEAD_SIZE)
    query_rows = query_key_value_full[:, :query_width].reshape(
        row_count, KEY_VALUE_HEADS, rows_per_group, HEAD_SIZE
    )
    fresh_keys = query_key_value_full[:, query_width : query_width + key_value_width].reshape(
        row_count, KEY_VALUE_HEADS, HEAD_SIZE
    )
    fresh_values = query_key_value_full[:, query_width + key_value_width :].reshape(
        row_count, KEY_VALUE_HEADS, HEAD_SIZE
    )
    cache_positions = key_cache.shape[1]
    offset = lax.axis_index("dev") * cache_positions
    stored_keys = key_cache.reshape(row_count, cache_positions, KEY_VALUE_HEADS, HEAD_SIZE)
    stored_values = value_cache.reshape(row_count, cache_positions, KEY_VALUE_HEADS, HEAD_SIZE)
    scores = (
        jnp.einsum("rhgd,rjhd->rhgj", query_rows, stored_keys, preferred_element_type=jnp.float32)
        * score_factor
    )
    is_valid = (offset + jnp.arange(cache_positions, dtype=jnp.int32))[None, :] < lengths[:, None]
    is_valid = is_valid[:, None, None, :]
    scores = jnp.where(is_valid, scores, NEG_FILL)
    local_max = jnp.max(scores, axis=-1)
    weights = jnp.where(is_valid, jnp.exp(scores - local_max[..., None]), 0.0)
    local_sum = jnp.sum(weights, axis=-1)
    local_values = jnp.einsum(
        "rhgj,rjhd->rhgd",
        weights.astype(jnp.bfloat16),
        stored_values,
        preferred_element_type=jnp.float32,
    )
    self_score = (
        jnp.einsum("rhgd,rhd->rhg", query_rows, fresh_keys, preferred_element_type=jnp.float32)
        * score_factor
    )
    own_values = fresh_values.astype(jnp.float32)[:, :, None, :]
    col_width = query_width // n_devs
    col_start = lax.axis_index("dev") * col_width
    merged = combined_all((local_max, local_sum, local_values), "dev", combine_parts)
    top_score = jnp.maximum(merged[0], self_score)
    old_factor = jnp.exp(merged[0] - top_score)
    self_weight = jnp.exp(self_score - top_score)
    denominator = merged[1] * old_factor + self_weight
    numerator = merged[2] * old_factor[..., None] + self_weight[..., None] * own_values
    attended = (numerator / denominator[..., None]).reshape(row_count, query_width)
    attn_cols = lax.dynamic_slice_in_dim(attended, col_start, col_width, 1).astype(jnp.bfloat16)
    partial_out = jnp.dot(attn_cols, out_rows, preferred_element_type=jnp.float32)
    hidden_out = lax.psum_scatter(partial_out, "dev", scatter_dimension=1, tiled=True)
    learners = jnp.arange(n_groups, dtype=jnp.int32)
    matches = ((assignment[:, None] == learners[None, :]) & (finished[:, None] == 1)).astype(
        jnp.int32
    )
    ranks = jnp.cumsum(matches, axis=0) - 1
    capacity = row_count // n_groups
    slots = jnp.arange(capacity, dtype=jnp.int32)
    table = (matches.T[:, None, :] == 1) & (ranks.T[:, None, :] == slots[None, :, None])
    table = table.reshape(n_groups * capacity, row_count).astype(jnp.float32)
    packed = jnp.dot(table, hidden_out, precision=lax.Precision.HIGHEST)
    packed = packed.reshape(n_groups, capacity, hidden_out.shape[1])
    arrived = lax.all_to_all(packed, "grp", split_axis=0, concat_axis=0, tiled=True)
    returned = arrived.reshape(n_groups * capacity, hidden_out.shape[1])
    return (hidden_out, returned, qkv_rows, out_rows)


def solution(mesh):
    return jax.shard_map(
        shards,
        mesh=mesh,
        in_specs=(
            P("grp", "dev"),
            P(None, ("grp", "dev")),
            P(None, ("grp", "dev")),
            P("grp", "dev", None),
            P("grp", "dev", None),
            P("grp"),
            P("grp"),
            P("grp"),
        ),
        out_specs=(P("grp", "dev"), P("grp", "dev"), P("dev", None), P("dev", None)),
        check_vma=False,
    )
```

profile of v0, /device:TPU:1, one launch (start us, length us, event | category | flops | bytes accessed | tf_op | source)
XLA Modules:
  0.0 1285.3 jit_solution(4426693414676470014)
XLA Ops:
  7.9 30.9 %all-gather.10.cloned.1.call-done = bf16[4,28,5120]{2,1,0:T(8,128)(2,1)} async-done(((bf16[1,28,5120]{2,1,0:T(8,128)(2,1)}), bf16[4,28,5120]{2,1,0:T(8,128)(2,1)}) %all-gather.10.cloned.1.call-update) | async-done | bytes 1146896 | tf_op jit(solution)/shard_map/all_gather | solution.py:47
  40.3 1.4 copy.72
  41.7 10.3 all-to-all-start
  52.2 33.0 %all-to-all-done = bf16[64,80,112]{2,1,0:T(8,128)(2,1)S(1)} async-done(((bf16[64,80,112]{2,1,0:T(8,128)(2,1)}), bf16[64,80,112]{2,1,0:T(8,128)(2,1)S(1)}, u32[]{:S(2)}, u32[]{:S(2)}) %all-to-all-start) | async-done | bytes 1146912 | tf_op jit(solution)/shard_map/all_to_all | solution.py:51
  85.2 3.5 copy.73
  88.7 4.0 copy.74
  92.7 4.0 reshape.133
  96.7 2.1 fusion.42
  98.7 250.9 %all-reduce.1 = bf16[8,7168]{1,0:T(8,128)(2,1)S(1)} all-reduce(f32[8,7168]{1,0:T(8,128)S(1)} %fusion.42), channel_id=1, replica_groups=mesh['grp'=4,'dev'=64] {'dev'}, use_global_device_ids=true, to_apply=%region_0.0 | all-reduce | flops 57344 | bytes 344064 | tf_op jit(solution)/shard_map/psum | solution.py:57
  353.1 67.8 %all-gather.4 = bf16[4,20,5120]{2,1,0:T(8,128)(2,1)S(1)} all-gather(bf16[1,20,5120]{2,1,0:T(8,128)(2,1)S(1)} %bitcast.115), channel_id=1, replica_groups=mesh['grp'=4,'dev'=64] {'grp'}, dimensions={0}, use_global_device_ids=true | all-gather | bytes 1024000 | tf_op jit(solution)/shard_map/all_gather | solution.py:48
  422.0 2.5 all_to_all.30
  424.5 1.9 copy.91
  426.4 4.8 all-to-all-start.1
  431.5 45.4 %all-to-all-done.1 = bf16[64,80,80]{1,2,0:T(8,128)(2,1)S(1)} async-done(((bf16[64,80,80]{1,2,0:T(8,128)(2,1)}), bf16[64,80,80]{1,2,0:T(8,128)(2,1)S(1)}, u32[]{:S(2)}, u32[]{:S(2)}) %all-to-all-start.1) | async-done | bytes 819232 | tf_op jit(solution)/shard_map/all_to_all | solution.py:52
  477.3 2.0 copy.93
  479.3 3.5 reshape.140
  483.4 140.0 %all-gather.1 = f32[512,8,5]{1,0,2:T(8,128)S(1)} all-gather(f32[8,8,5]{1,0,2:T(8,128)S(1)} %copy.78), channel_id=3, replica_groups=mesh['grp'=4,'dev'=64] {'dev'}, dimensions={0}, use_global_device_ids=true | all-gather | bytes 83200 | tf_op jit(solution)/shard_map/all_gather | solution.py:17
  624.4 135.7 %all-gather = f32[512,8,5]{1,0,2:T(8,128)S(1)} all-gather(f32[8,8,5]{1,0,2:T(8,128)S(1)} %copy.77), channel_id=2, replica_groups=mesh['grp'=4,'dev'=64] {'dev'}, dimensions={0}, use_global_device_ids=true | all-gather | bytes 83200 | tf_op jit(solution)/shard_map/all_gather | solution.py:17
  763.4 140.5 %while.19 = (s32[]{:T(128)}, f32[8,8,5]{1,0,2:T(8,128)S(1)}, f32[8,8,5]{1,0,2:T(8,128)S(1)}, f32[8,8,5,128]{3,2,1,0:T(8,128)S(1)}, f32[64,8,8,5]{2,1,0,3:T(8,128...) while((s32[]{:T(128)}, f32[8,8,5]{1,0,2:T(8,128)S(1)}, ...), condition=%wide.region_4.5_spmd, body=%wide.region_3.4_spmd.sunk | while | flops 124805 | bytes 837271 | solution.py:22
  904.7 3.4 convolution_bitcast_fusion
  908.1 310.8 %reduce-scatter.4.cloned.1.call-done = f32[80,8]{1,0:T(8,128)} async-done(((f32[5120,8]{1,0:T(8,128)}), f32[80,8]{1,0:T(8,128)}) %reduce-scatter.4.cloned.1.call-update) | async-done | bytes 2576
  1218.9 1.5 fusion.25
  1220.5 53.1 %all-to-all-start.2 = ((f32[4,2,80]{2,1,0:T(2,128)}), f32[4,2,80]{2,1,0:T(2,128)S(1)}, u32[]{:S(2)}, u32[]{:S(2)}) async-start(f32[4,2,80]{2,1,0:T(2,128)} %fusion.25), calls=%async_computation.2 | async-start | bytes 8192 | tf_op jit(solution)/shard_map/all_to_all | solution.py:120
  1274.9 2.6 copy.95
  (386 shorter events, 154.1 us)
Async XLA Ops:
  7.2 342.5 %copy-start = (bf16[8,128,1024]{2,1,0:T(8,128)(2,1)S(1)}, bf16[8,128,1024]{2,1,0:T(8,128)(2,1)}, u32[]{:S(2)}) copy-start(bf16[8,128,1024]{2,1,0:T(8,128)(2,1)} %param.13) | copy-start | bytes 6291460
  7.2 31.7 %all-gather.10.cloned.1.call-start = ((), (), s32[]{:S(2)}) async-start(), calls=%async_computation.5 | async-start | bytes 1638400 | tf_op jit(solution)/shard_map/all_gather | solution.py:47
  41.7 10.4 copy-start.11
  41.7 43.5 %all-to-all-start = ((bf16[64,80,112]{2,1,0:T(8,128)(2,1)}), bf16[64,80,112]{2,1,0:T(8,128)(2,1)S(1)}, u32[]{:S(2)}, u32[]{:S(2)}) async-start(bf16[64,80,112]{2,1,0:T(8,128)(2,1)} %bitcast.106), calls=%async_computation | async-start | bytes 2621440 | tf_op jit(solution)/shard_map/all_to_all | solution.py:51
  52.1 710.3 %all-gather.8.cloned.1.call-start = ((), (), s32[]{:S(2)}) async-start(), calls=%async_computation.4 | async-start | bytes 10649600 | tf_op jit(solution)/shard_map/all_gather | solution.py:17
  92.7 4.0 copy-start.10
  349.6 2.7 copy-start.7
  349.6 2.0 copy-start.4
  350.9 0.7 copy-start.2
  350.9 2.2 copy-start.8
  426.4 4.9 copy-start.13
  426.4 4.9 copy-start.12
  426.4 50.5 %all-to-all-start.1 = ((bf16[64,80,80]{1,2,0:T(8,128)(2,1)}), bf16[64,80,80]{1,2,0:T(8,128)(2,1)S(1)}, u32[]{:S(2)}, u32[]{:S(2)}) async-start(bf16[64,80,80]{1,2,0:T(8,128)(2,1)} %copy.91), calls=%async_computation.1 | async-start | bytes 2621440 | tf_op jit(solution)/shard_map/all_to_all | solution.py:52
  431.2 787.7 %reduce-scatter.4.cloned.1.call-start = ((), (), s32[]{:S(2)}) async-start(), calls=%async_computation.6 | async-start | bytes 2662400
  479.3 3.7 copy-start.3
  623.4 1.1 copy-start.5
  760.2 1.1 copy-start.6
  908.1 365.5 %copy-start.1 = (bf16[80,5120]{0,1:T(8,128)(2,1)S(1)}, bf16[80,5120]{0,1:T(8,128)(2,1)}, u32[]{:S(2)}) copy-start(bf16[80,5120]{0,1:T(8,128)(2,1)} %reshape.140) | copy-start | bytes 2457604
  1220.5 57.7 %all-to-all-start.2 = ((f32[4,2,80]{2,1,0:T(2,128)}), f32[4,2,80]{2,1,0:T(2,128)S(1)}, u32[]{:S(2)}, u32[]{:S(2)}) async-start(f32[4,2,80]{2,1,0:T(2,128)} %fusion.25), calls=%async_computation.2 | async-start | bytes 8192 | tf_op jit(solution)/shard_map/all_to_all | solution.py:120
  1274.9 2.6 copy-start.9
Sparse Core Ops, SparseCore 0:
  9.8 28.9 all-gather.9
  353.2 346.5 all-gather.7
  908.2 310.6 reduce-scatter.3
where the time goes:
time: 1290 us
  blocking collectives  594 us (46%)
  waiting for transfers between devices  421 us (33%)
  local copies, waits for them, and re-layouts  110 us (9%)
  starting transfers between devices  68.4 us (5%)
  other arithmetic  66.3 us (5%)
  between operations  14 us (1%)
    unnamed x4, waiting for transfers between devices  312 us
    all_gather x2, blocking collectives, combined_all(): gathered = jax.tree.map(lambda a: lax.all_gather(a, axis), part)  276 us
    psum x1, blocking collectives, shards(): query_key_value_full = lax.psum(partial_qkv, 'dev').astype(jnp.bfloat16)  251 us
    all_gather x1, blocking collectives, shards(): lax.all_gather(w_o, 'grp', axis=1, tiled=True)  67.8 us
    dynamic_slice x66, local copies, waits for them, and re-layouts, take(): lax.dynamic_index_in_dim(a, source, 0, False)  59.3 us
    all_to_all x1, starting transfers between devices, shards(): lax.all_to_all(packed, 'grp', split_axis=0, concat_axis=0, tiled=True)  53.1 us
    add x63, other arithmetic, combine_parts(): sums = first[1] * left_factor + second[1] * right_factor  48.8 us
    all_to_all x1, waiting for transfers between devices, shards(): lax.all_to_all(copies[1], 'dev', split_axis=0, concat_axis=1, tiled=True)  45.4 us
  transfers between devices with their start and end apart: 6, of which 4 were waited for; matrix products, arithmetic and copies ran while one was open for 1% of the time, Pallas kernels for 0%

commit v1 on v0

v1 whole, which is shorter than its diff:
```python
import functools
import math

import jax
import jax.numpy as jnp
from jax import lax
from jax.experimental import pallas as pl
from jax.experimental.pallas import tpu as pltpu
from jax.sharding import Mesh
from jax.sharding import PartitionSpec as P

N_DEV = 64
N_GRP = 4
ROWS = 8
HEADS = 40
KV_HEADS = 8
SHARE = HEADS // KV_HEADS
LANES = 128
D = 5120
FEAT = D // N_DEV
WQ = 28
WO = 20
PIECE = 48
QW = N_DEV * WQ
OW = N_DEV * WO
POS = 128
NEG = -1e30

G_AXES = ("xh", "core")
D_AXES = ("xl", "y", "z")
F32 = jnp.float32
BF16 = jnp.bfloat16
VMEM = pl.BlockSpec(memory_space=pltpu.VMEM)
SMEM = pl.BlockSpec(memory_space=pltpu.SMEM)
PARAMS = pltpu.CompilerParams(vmem_limit_bytes=48 * 1024 * 1024)


def lane_iota(rows):
    return lax.broadcasted_iota(jnp.int32, (rows, LANES), 1)


def rolled(x, shift):
    shift %= LANES
    return x if shift == 0 else pltpu.roll(x, shift, 1)


def cut(tiles, start, width, lane):
    at, off = divmod(start, LANES)
    first = rolled(tiles[at], -off)
    if off + width <= LANES:
        return first
    return jnp.where(lane < LANES - off, first, rolled(tiles[at + 1], -off))


def lay(count, pieces, lane):
    tiles = [None] * count
    for source, first, width, column in pieces:
        moved = rolled(source, column - first)
        at, off = divmod(column, LANES)
        tiles[at] = moved if tiles[at] is None else jnp.where(lane >= off, moved, tiles[at])
        if off + width > LANES:
            tiles[at + 1] = moved
    return tiles


def swapped_blocks(blocks, group):
    odd = (group & 1) == 1
    high = (group & 2) == 2
    a, b, c, d = blocks
    a, b, c, d = (
        jnp.where(odd, b, a),
        jnp.where(odd, a, b),
        jnp.where(odd, d, c),
        jnp.where(odd, c, d),
    )
    return (
        jnp.where(high, c, a),
        jnp.where(high, d, b),
        jnp.where(high, a, c),
        jnp.where(high, b, d),
    )


def pack_kernel(hidden_ref, wq_ref, wo_ref, out_ref, rows_ref):
    lane = lane_iota(PIECE)
    rows_ref[0:WQ, :] = wq_ref[...].astype(F32)
    rows_ref[WQ:PIECE, :] = wo_ref[...].astype(F32)
    hidden = jnp.concatenate(
        [hidden_ref[...].astype(F32), jnp.zeros((ROWS, LANES - FEAT), F32)], axis=1
    )
    spare = jnp.concatenate(
        [
            pltpu.roll(hidden, FEAT, 1),
            pltpu.roll(hidden, 2 * FEAT - LANES, 1),
            jnp.zeros((PIECE - 2 * ROWS, LANES), F32),
        ],
        axis=0,
    )
    for dest in range(N_DEV):
        at, off = divmod(dest * FEAT, LANES)
        tiles = {at: rows_ref[:, at * LANES : (at + 1) * LANES]}
        if off + FEAT > LANES:
            tiles[at + 1] = rows_ref[:, (at + 1) * LANES : (at + 2) * LANES]
        piece = cut(tiles, dest * FEAT, FEAT, lane)
        piece = jnp.where(lane < FEAT, piece, spare)
        out_ref[dest * PIECE : (dest + 1) * PIECE, :] = piece.astype(BF16)


def project_kernel(group_ref, recv_ref, w0_ref, w1_ref, w2_ref, w3_ref, out_ref, w_ref):
    lane = lane_iota(ROWS)
    group = group_ref[0]
    for j, ref in enumerate((w0_ref, w1_ref, w2_ref, w3_ref)):
        w_ref[32 * j + 16 : 32 * j + 32, :] = jnp.zeros((16, D), BF16)
        w_ref[32 * j : 32 * j + WQ, :] = ref[...]
    pieces = []
    for dev in range(N_DEV):
        both = recv_ref[dev * PIECE : dev * PIECE + 16, :].astype(F32)
        pieces.append((both[0:8], FEAT, LANES - FEAT, dev * FEAT))
        pieces.append((both[8:16], FEAT, 2 * FEAT - LANES, dev * FEAT + LANES - FEAT))
    tiles = lay(D // LANES, pieces, lane)
    hidden = jnp.concatenate([t.astype(BF16) for t in tiles], axis=1)
    y = lax.dot_general(hidden, w_ref[...], (((1,), (1,)), ((), ())), preferred_element_type=F32)
    up, down = pltpu.roll(y, 32, 1), pltpu.roll(y, LANES - 32, 1)
    y = jnp.where((group & 1) == 1, jnp.where((lane & 32) == 0, down, up), y)
    y = jnp.where((group & 2) == 2, pltpu.roll(y, 64, 1), y)
    two = jnp.concatenate([y, y], axis=0).astype(BF16)
    for pair in range(N_DEV // 2):
        out_ref[16 * pair : 16 * pair + 16, :] = two


def turn_kernel(recv_ref, out_ref, q_ref, o_ref):
    for dev in range(N_DEV):
        x = recv_ref[dev * PIECE : (dev + 1) * PIECE, :].astype(F32)
        q_ref[dev * WQ : (dev + 1) * WQ, :] = x[0:WQ]
        o_ref[dev * WO : (dev + 1) * WO, :] = x[WQ:PIECE]
    row = lax.broadcasted_iota(jnp.int32, (FEAT, LANES), 0)
    eye = (row == lax.broadcasted_iota(jnp.int32, (FEAT, LANES), 1)).astype(BF16)
    turn = functools.partial(
        lax.dot_general,
        dimension_numbers=(((1,), (1,)), ((), ())),
        preferred_element_type=F32,
    )
    out_ref[:, 0:QW] = turn(eye, q_ref[...].astype(BF16)).astype(BF16)
    out_ref[:, QW : QW + OW] = turn(eye, o_ref[...].astype(BF16)).astype(BF16)


def attend_kernel(dev_ref, lengths_ref, recv_ref, keys_ref, values_ref, out_ref):
    lane = lane_iota(ROWS)
    sub = lax.broadcasted_iota(jnp.int32, (ROWS, LANES), 0)
    dev = dev_ref[0]
    scale = 1.0 / math.sqrt(LANES)
    offset = dev * POS
    sources = []
    for pair in range(N_DEV // 2):
        both = recv_ref[16 * pair : 16 * pair + 16, :].astype(F32)
        sources += [both[0:8], both[8:16]]
    pieces = [
        (sources[d], 32 * g, WQ, g * QW + d * WQ) for g in range(N_GRP) for d in range(N_DEV)
    ]
    tiles = lay(N_GRP * QW // LANES, pieces, lane)
    own_rows = [sub == r for r in range(ROWS)]
    length = jnp.zeros((ROWS, LANES), jnp.int32)
    for r in range(ROWS):
        length = jnp.where(own_rows[r], lengths_ref[r], length)
    valid = offset + lane < length
    valid = jnp.concatenate([valid] * SHARE, axis=0)
    first = dev == 0
    outs, tops, sums = [], [], []
    for k in range(KV_HEADS):
        heads = tiles[k * SHARE : (k + 1) * SHARE]
        new_key, new_value = tiles[HEADS + k], tiles[HEADS + KV_HEADS + k]
        q = jnp.concatenate(heads, axis=0)
        columns = slice(k * LANES, (k + 1) * LANES)
        keys = keys_ref[:, columns]
        wide = lax.dot_general(
            q.astype(BF16), keys, (((1,), (1,)), ((), ())), preferred_element_type=F32
        )
        s = []
        for i in range(SHARE):
            line = wide[i * ROWS : (i + 1) * ROWS, 0:LANES]
            for r in range(1, ROWS):
                line = jnp.where(
                    own_rows[r],
                    wide[i * ROWS : (i + 1) * ROWS, r * LANES : (r + 1) * LANES],
                    line,
                )
            s.append(line)
        s = jnp.concatenate(s, axis=0) * scale
        s = jnp.where(valid, s, NEG)
        own = jnp.sum(q * jnp.concatenate([new_key] * SHARE, axis=0), axis=1, keepdims=True) * scale
        own = jnp.where(first, own, NEG)
        top = jnp.maximum(jnp.max(s, axis=1, keepdims=True), own)
        w = jnp.where(valid, jnp.exp(s - top), 0.0)
        own_w = jnp.where(first, jnp.exp(own - top), 0.0)
        total = jnp.sum(w, axis=1, keepdims=True) + own_w
        spread = []
        for r in range(ROWS):
            spread.append(
                jnp.concatenate(
                    [
                        jnp.where(own_rows[r], w[i * ROWS : (i + 1) * ROWS], 0.0)
                        for i in range(SHARE)
                    ],
                    axis=0,
                ).astype(BF16)
            )
        spread = jnp.concatenate(spread, axis=1)
        out = jnp.dot(spread, values_ref[:, columns], preferred_element_type=F32)
        out = out + own_w * jnp.concatenate([new_value] * SHARE, axis=0)
        for i in range(SHARE):
            rows = slice(i * ROWS, (i + 1) * ROWS)
            outs.append(out[rows])
            tops.append(jnp.broadcast_to(top[rows], (ROWS, LANES)))
            sums.append(jnp.broadcast_to(total[rows], (ROWS, LANES)))
    for dest in range(N_DEV):
        h0, h1 = dest * FEAT // LANES, (dest * FEAT + FEAT - 1) // LANES
        tile = cut(outs, dest * FEAT, FEAT, lane)
        tile = jnp.where(lane < FEAT, tile, tops[h0])
        tile = jnp.where(lane == FEAT + 1, sums[h0], tile)
        tile = jnp.where(lane == FEAT + 2, tops[h1], tile)
        tile = jnp.where(lane == FEAT + 3, sums[h1], tile)
        out_ref[dest * ROWS : (dest + 1) * ROWS, :] = tile


def finish_kernel(place_ref, recv_ref, b0_ref, b1_ref, b2_ref, b3_ref, out_ref):
    lane = lane_iota(ROWS)
    dev, group = place_ref[0], place_ref[1]
    start = dev * FEAT
    split = ((start + FEAT - 1) // LANES) * LANES - start
    split = jnp.where(split <= 0, FEAT, split)
    left = (lane < split) | (lane == FEAT) | (lane == FEAT + 1)
    parts = [recv_ref[s * ROWS : (s + 1) * ROWS, :] for s in range(N_DEV)]
    tops = parts
    while len(tops) > 1:
        tops = [jnp.maximum(a, b) for a, b in zip(tops[0::2], tops[1::2])]
    top = tops[0]
    total = [jnp.zeros((ROWS, LANES), F32) for _ in range(4)]
    for s, part in enumerate(parts):
        e = jnp.exp(part - top)
        f = jnp.where(left, e[:, FEAT : FEAT + 1], e[:, FEAT + 2 : FEAT + 3])
        total[s % 4] = total[s % 4] + f * part
    total = (total[0] + total[1]) + (total[2] + total[3])
    den = jnp.where(left, total[:, FEAT + 1 : FEAT + 2], total[:, FEAT + 3 : FEAT + 4])
    attn = (total / den)[:, 0:FEAT].astype(BF16)
    blocks = [
        jnp.dot(attn, ref[:, QW : QW + OW], preferred_element_type=F32)
        for ref in (b0_ref, b1_ref, b2_ref, b3_ref)
    ]
    blocks = swapped_blocks(blocks, group)
    tiles = [
        block[:, t * LANES : (t + 1) * LANES] for block in blocks for t in range(OW // LANES)
    ]
    for dest in range(N_DEV):
        out_ref[dest * ROWS : (dest + 1) * ROWS, :] = cut(tiles, dest * FEAT, FEAT, lane)


def total_kernel(table_ref, recv_ref, hidden_ref, r0_ref, r1_ref, r2_ref, r3_ref):
    sums = [recv_ref[s * ROWS : (s + 1) * ROWS, :] for s in range(N_DEV)]
    while len(sums) > 1:
        sums = [a + b for a, b in zip(sums[0::2], sums[1::2])]
    hidden = sums[0]
    hidden_ref[...] = hidden[:, 0:FEAT]
    table = table_ref[...]
    packed = table[:, 0:1] * hidden[0:1, :]
    for r in range(1, ROWS):
        packed = packed + table[:, r : r + 1] * hidden[r : r + 1, :]
    for j, ref in enumerate((r0_ref, r1_ref, r2_ref, r3_ref)):
        ref[...] = packed[2 * j : 2 * j + 2, 0:FEAT]


def call(kernel, outs, scratch=(), smem=0, n_in=1):
    many = isinstance(outs, (list, tuple))
    return pl.pallas_call(
        kernel,
        out_shape=outs,
        in_specs=[SMEM] * smem + [VMEM] * (n_in - smem),
        out_specs=[VMEM] * len(outs) if many else VMEM,
        scratch_shapes=list(scratch),
        compiler_params=PARAMS,
    )


def to_groups(x):
    swap = [(0, 1), (1, 0)]
    return (
        lax.ppermute(x, "core", swap),
        lax.ppermute(x, "xh", swap),
        lax.ppermute(x, G_AXES, [(g, g ^ 3) for g in range(N_GRP)]),
    )


def exchange(x):
    rows = x.shape[0] // N_DEV
    x = x.reshape(N_DEV, rows, x.shape[1])
    x = lax.all_to_all(x, D_AXES, split_axis=0, concat_axis=0, tiled=True)
    return x.reshape(N_DEV * rows, x.shape[2])


def shards(hidden_in, w_qkv, w_o, key_cache, value_cache, lengths, finished, assignment):
    struct = jax.ShapeDtypeStruct
    group = lax.axis_index(G_AXES).astype(jnp.int32)
    dev = lax.axis_index(D_AXES).astype(jnp.int32)
    group_one, dev_one = group.reshape(1), dev.reshape(1)
    place = jnp.stack([dev, group])

    wq, wo = w_qkv.T, w_o.T
    others = to_groups(wq)
    sent = call(
        pack_kernel,
        struct((N_DEV * PIECE, LANES), BF16),
        [pltpu.VMEM((PIECE, D), F32)],
        n_in=3,
    )(hidden_in, wq, wo)
    recv = exchange(sent)
    sent = call(
        project_kernel,
        struct((N_DEV * ROWS, LANES), BF16),
        [pltpu.VMEM((LANES, D), BF16)],
        smem=1,
        n_in=6,
    )(group_one, recv, wq, *others)
    got = exchange(sent)

    block = call(
        turn_kernel,
        struct((FEAT, QW + OW), BF16),
        [pltpu.VMEM((QW, LANES), F32), pltpu.VMEM((OW, LANES), F32)],
    )(recv)
    blocks = (block,) + to_groups(block)

    sent = call(
        attend_kernel, struct((N_DEV * ROWS, LANES), F32), smem=2, n_in=5
    )(
        dev_one,
        lengths,
        got,
        key_cache.reshape(ROWS * POS, KV_HEADS * LANES),
        value_cache.reshape(ROWS * POS, KV_HEADS * LANES),
    )
    got = exchange(sent)
    sent = call(finish_kernel, struct((N_DEV * ROWS, LANES), F32), smem=1, n_in=6)(
        place, got, *blocks
    )
    got = exchange(sent)

    learners = jnp.arange(N_GRP, dtype=jnp.int32) ^ group
    matches = (assignment[None, :] == learners[:, None]) & (finished[None, :] == 1)
    ranks = jnp.cumsum(matches.astype(jnp.int32), axis=1)
    slots = jnp.arange(1, 3, dtype=jnp.int32)
    table = matches[:, None, :] & (ranks[:, None, :] == slots[None, :, None])
    table = table.reshape(ROWS, ROWS).astype(F32)
    part = struct((2, FEAT), F32)
    hidden_out, r0, r1, r2, r3 = call(
        total_kernel, [struct((ROWS, FEAT), F32)] + [part] * 4, n_in=2
    )(table, got)
    swap = [(0, 1), (1, 0)]
    r1 = lax.ppermute(r1, "core", swap)
    r2 = lax.ppermute(r2, "xh", swap)
    r3 = lax.ppermute(r3, G_AXES, [(g, g ^ 3) for g in range(N_GRP)])
    returned = jnp.concatenate(swapped_blocks((r0, r1, r2, r3), group), axis=0)

    ordered = swapped_blocks(blocks, group)
    w_qkv_gen = jnp.concatenate([b[:, 0:QW] for b in ordered], axis=1)
    w_o_gen = jnp.concatenate([b[:, QW:] for b in ordered], axis=1)
    return (hidden_out, returned, w_qkv_gen, w_o_gen)


def solution(mesh):
    fine = Mesh(mesh.devices.reshape(2, 2, 2, 4, 8), G_AXES + D_AXES)
    return jax.shard_map(
        shards,
        mesh=fine,
        in_specs=(
            P(G_AXES, D_AXES),
            P(None, G_AXES + D_AXES),
            P(None, G_AXES + D_AXES),
            P(G_AXES, D_AXES, None),
            P(G_AXES, D_AXES, None),
            P(G_AXES),
            P(G_AXES),
            P(G_AXES),
        ),
        out_specs=(P(G_AXES, D_AXES), P(G_AXES, D_AXES), P(D_AXES, None), P(D_AXES, None)),
        check_vma=False,
    )
```

time: 1290 us -> 124 us (0.10)
  blocking collectives: 594 us -> 0 us
  waiting for transfers between devices: 421 us -> 52.3 us
  local copies, waits for them, and re-layouts: 110 us -> 3.51 us
  other arithmetic: 66.3 us -> 4.57 us
  starting transfers between devices: 68.4 us -> 50 us
  between operations: 14 us -> 0.81 us
    all_gather x3 -> x0, blocking collectives: 344 us -> none  [the longest x2 276 us: combined_all(): gathered = jax.tree.map(lambda a: lax.all_gather(a, axis), part)]
    unnamed x4 -> x0, waiting for transfers between devices: 312 us -> none
    psum x1 -> x0, blocking collectives: 251 us -> none  [shards(): query_key_value_full = lax.psum(partial_qkv, 'dev').astype(jnp.bfloat16)]
    add x128 -> x1, other arithmetic: 64.7 us -> 0.01 us  [shards(): slots = jnp.arange(1, 3, dtype=jnp.int32)]
    dynamic_slice x66 -> x0, local copies, waits for them, and re-layouts: 59.3 us -> none  [take(): lax.dynamic_index_in_dim(a, source, 0, False)]
    all_to_all x3 -> x4, starting transfers between devices: 68.2 us -> 34.1 us  [exchange(): x = lax.all_to_all(x, D_AXES, split_axis=0, concat_axis=0, tiled=True)]
    all_gather x2 -> x0, waiting for transfers between devices: 30.9 us -> none  [the longest x1 30.9 us: shards(): lax.all_gather(w_qkv, 'grp', axis=1, tiled=True)]
    all_to_all x3 -> x4, waiting for transfers between devices: 78.4 us -> 50.5 us  [exchange(): x = lax.all_to_all(x, D_AXES, split_axis=0, concat_axis=0, tiled=True)]
  transfers between devices with their start and end apart: 6 -> 13, of which waited for: 4 -> 5; matrix products, arithmetic and copies ran while one was open for 1% -> 3% of each run, Pallas kernels for 0% -> 6%
where the time goes in v1:
time: 124 us
  waiting for transfers between devices  52.3 us (42%)
  starting transfers between devices  50 us (40%)
  Pallas kernels  12.7 us (10%)
  other arithmetic  4.57 us (4%)
  local copies, waits for them, and re-layouts  3.51 us (3%)
    all_to_all x4, waiting for transfers between devices, exchange(): x = lax.all_to_all(x, D_AXES, split_axis=0, concat_axis=0, tiled=True)  50.5 us
    all_to_all x4, starting transfers between devices, exchange(): x = lax.all_to_all(x, D_AXES, split_axis=0, concat_axis=0, tiled=True)  34.1 us
    ppermute x2, starting transfers between devices, to_groups(): lax.ppermute(x, G_AXES, [(g, g ^ 3) for g in range(N_GRP)])  8.56 us
    ppermute x1, starting transfers between devices, shards(): r3 = lax.ppermute(r3, G_AXES, [(g, g ^ 3) for g in range(N_GRP)])  5.12 us
    pallas_call x1, Pallas kernels, shards(): call(attend_kernel, struct((N_DEV * ROWS, LANES), F32), smem=2, n_in=5)  4.15 us
    unnamed x14, local copies, waits for them, and re-layouts  3.23 us
    pallas_call x1, Pallas kernels, shards(): call(finish_kernel, struct((N_DEV * ROWS, LANES), F32), smem=1, n_in=6)  2.7 us
    pallas_call x1, Pallas kernels, shards(): call(project_kernel, struct((N_DEV * ROWS, LANES), BF16), [pltpu.VMEM((LA...  2.58 us
  transfers between devices with their start and end apart: 13, of which 5 were waited for; matrix products, arithmetic and copies ran while one was open for 3% of the time, Pallas kernels for 6%

profile of v1, /device:TPU:1, one launch (start us, length us, event | category | flops | bytes accessed | tf_op | source)
XLA Modules:
  0.0 123.8 jit_solution(5089822034575922901)
XLA Ops:
  0.7 0.9 copy-done.2
  1.6 0.7 copy-done.3
  2.3 2.2 %shard_map.111 = bf16[3072,128]{1,0:T(8,128)(2,1)} custom-call(bf16[8,80]{1,0:T(8,128)(2,1)S(1)} %copy-done.3, bf16[28,5120]{1,0:T(8,128)(2,1)} %bitcast.3.wq_ref.w0_ref, bf16[20,5120]{1,0:T(8,128)(2,1)S(1)} %bitcast.22), custom_call_target="tpu_custom_call" | custom-call | tf_op jit(solution)/shard_map/pallas_call | solution.py:308
  4.5 13.7 %all-to-all-start = ((bf16[64,48,128]{2,1,0:T(8,128)(2,1)}), bf16[64,48,128]{2,1,0:T(8,128)(2,1)S(1)}, u32[]{:S(2)}, u32[]{:S(2)}) async-start(bf16[64,48,128]{2,1,0:T(8,128)(2,1)} %bitcast.5), calls=%async_computation | async-start | bytes 1572864 | tf_op jit(solution)/shard_map/all_to_all | solution.py:295
  18.2 3.4 %collective-permute-start.2 = (bf16[28,5120]{1,0:T(8,128)(2,1)}, bf16[28,5120]{1,0:T(8,128)(2,1)}, u32[]{:S(2)}, u32[]{:S(2)}) collective-permute-start(bf16[28,5120]{1,0:T(8,128)(2,1)} %bitcast.3.wq_ref.w0_ref), channel_id=1, source_target_pairs={{0,192},{64,128},{128,64},{192,0},{1,193},{65,129},{129,65},{193,1... | collective-permute-start | bytes 860168 | tf_op jit(solution)/shard_map/ppermute | solution.py:288
  22.1 18.5 %all-to-all-done = bf16[64,48,128]{2,1,0:T(8,128)(2,1)S(1)} async-done(((bf16[64,48,128]{2,1,0:T(8,128)(2,1)}), bf16[64,48,128]{2,1,0:T(8,128)(2,1)S(1)}, u32[]{:S(2)}, u32[]{:S(2)}) %all-to-all-start) | async-done | bytes 786464 | tf_op jit(solution)/shard_map/all_to_all | solution.py:295
  41.0 5.2 %collective-permute-start.5 = (bf16[80,3072]{1,0:T(8,128)(2,1)S(1)}, bf16[80,3072]{1,0:T(8,128)(2,1)}, u32[]{:S(2)}, u32[]{:S(2)}) collective-permute-start(bf16[80,3072]{1,0:T(8,128)(2,1)S(1)} %shard_map.114.b0_ref), channel_id=1, source_target_pairs={{0,192},{64,128},{128,64},{192,0},{1,193},{65,129},{129,65},{193,1... | collective-permute-start | bytes 1474568 | tf_op jit(solution)/shard_map/ppermute | solution.py:288
  46.8 2.6 %shard_map.112 = bf16[512,128]{1,0:T(8,128)(2,1)} custom-call(s32[1]{0:T(128)} %bitcast.2.group_ref, bf16[3072,128]{1,0:T(8,128)(2,1)S(1)} %bitcast.16, bf16[28,5120]{1,0:T(8,128)(2,1)} %bitcast.3.wq_ref.w0_ref, bf16[28,5120]{1,0:T(8,128)(2,1)} %collective-permute-done.w1_ref, bf16[28,5120]{1,0:T(8,128)(2,1)} %collective-permute-done.1.w2_ref, ...), custom_call_target="tpu_custom_call" | custom-call | tf_op jit(solution)/shard_map/pallas_call | solution.py:315
  49.4 8.1 %all-to-all-start.1 = ((bf16[64,8,128]{2,1,0:T(8,128)(2,1)}), bf16[64,8,128]{2,1,0:T(8,128)(2,1)S(1)}, u32[]{:S(2)}, u32[]{:S(2)}) async-start(bf16[64,8,128]{2,1,0:T(8,128)(2,1)} %bitcast.7), calls=%async_computation.1 | async-start | bytes 262144 | tf_op jit(solution)/shard_map/all_to_all | solution.py:295
  58.0 11.3 %all-to-all-done.1 = bf16[64,8,128]{2,1,0:T(8,128)(2,1)S(1)} async-done(((bf16[64,8,128]{2,1,0:T(8,128)(2,1)}), bf16[64,8,128]{2,1,0:T(8,128)(2,1)S(1)}, u32[]{:S(2)}, u32[]{:S(2)}) %all-to-all-start.1) | async-done | bytes 131104 | tf_op jit(solution)/shard_map/all_to_all | solution.py:295
  69.3 1.6 %copy-done.1 = bf16[8,128,1024]{2,1,0:T(8,128)(2,1)S(1)} copy-done((bf16[8,128,1024]{2,1,0:T(8,128)(2,1)S(1)}, bf16[8,128,1024]{2,1,0:T(8,128)(2,1)}, u32[]{:S(2)}) %copy-start.1) | copy-done | bytes 2097176
  70.9 4.1 %shard_map.113 = f32[512,128]{1,0:T(8,128)} custom-call(s32[1]{0:T(128)} %bitcast.1.dev_ref, s32[8]{0:T(128)S(1)} %copy-done.4, bf16[512,128]{1,0:T(8,128)(2,1)S(1)} %bitcast.21, bf16[1024,1024]{1,0:T(8,128)(2,1)S(1)} %bitcast.17, bf16[1024,1024]{1,0:T(8,128)(2,1)S(1)} %bitcast.18), custom_call_target="tpu_custom_call" | custom-call | tf_op jit(solution)/shard_map/pallas_call | solution.py:331
  75.0 7.2 %all-to-all-start.2 = ((f32[64,8,128]{2,1,0:T(8,128)}), f32[64,8,128]{2,1,0:T(8,128)S(1)}, u32[]{:S(2)}, u32[]{:S(2)}) async-start(f32[64,8,128]{2,1,0:T(8,128)} %bitcast.11), calls=%async_computation.2 | async-start | bytes 524288 | tf_op jit(solution)/shard_map/all_to_all | solution.py:295
  82.3 1.5 %broadcast_select_fusion.7 = (bf16[80,3072]{1,0:T(8,128)(2,1)S(1)}, bf16[80,3072]{1,0:T(8,128)(2,1)S(1)}, bf16[80,3072]{1,0:T(8,128)(2,1)S(1)}, bf16[80,3072]{1,0:T(8,128)(2,1)S(1)}) fusion(pred[]{:T(512)S(6)} %eq.63, bf16[80,3072]{1,0:T(8,128)(2,1)} %collective-permute-done.5.b3_ref, bf16[80,3072]{1,0:T(8,128)(2,1)} %collective-permute-done.4.b2_ref, ...), kind=kLoop, calls=%fused_computation.9 | loop fusion | flops 1966080 | bytes 3932162 | tf_op jit(solution)/shard_map/jit(_where)/select_n | solution.py:77
  84.0 10.8 %all-to-all-done.2 = f32[64,8,128]{2,1,0:T(8,128)S(1)} async-done(((f32[64,8,128]{2,1,0:T(8,128)}), f32[64,8,128]{2,1,0:T(8,128)S(1)}, u32[]{:S(2)}, u32[]{:S(2)}) %all-to-all-start.2) | async-done | bytes 262176 | tf_op jit(solution)/shard_map/all_to_all | solution.py:295
  94.8 2.7 %shard_map.115 = f32[512,128]{1,0:T(8,128)} custom-call(s32[2]{0:T(128)S(1)} %pad_add_fusion.place_ref, f32[512,128]{1,0:T(8,128)S(1)} %bitcast.20, bf16[80,3072]{1,0:T(8,128)(2,1)S(1)} %shard_map.114.b0_ref, bf16[80,3072]{1,0:T(8,128)(2,1)} %collective-permute-done.3.b1_ref, bf16[80,3072]{1,0:T(8,128)(2,1)} %collective-permute-done.4.b2_ref, ...), custom_call_target="tpu_custom_call" | custom-call | tf_op jit(solution)/shard_map/pallas_call | solution.py:341
  97.5 5.0 %all-to-all-start.3 = ((f32[64,8,128]{2,1,0:T(8,128)}), f32[64,8,128]{2,1,0:T(8,128)S(1)}, u32[]{:S(2)}, u32[]{:S(2)}) async-start(f32[64,8,128]{2,1,0:T(8,128)} %bitcast.13), calls=%async_computation.3 | async-start | bytes 524288 | tf_op jit(solution)/shard_map/all_to_all | solution.py:295
  102.6 1.1 pad_maximum_fusion
  103.7 9.9 %all-to-all-done.3 = f32[64,8,128]{2,1,0:T(8,128)S(1)} async-done(((f32[64,8,128]{2,1,0:T(8,128)}), f32[64,8,128]{2,1,0:T(8,128)S(1)}, u32[]{:S(2)}, u32[]{:S(2)}) %all-to-all-start.3) | async-done | bytes 262176 | tf_op jit(solution)/shard_map/all_to_all | solution.py:295
  113.6 0.6 shard_map.116
  114.2 5.1 %collective-permute-start.6 = (f32[2,80]{1,0:T(2,128)S(1)}, f32[2,80]{1,0:T(2,128)S(1)}, u32[]{:S(2)}, u32[]{:S(2)}) collective-permute-start(f32[2,80]{1,0:T(2,128)S(1)} %get-tuple-element.10), channel_id=1, source_target_pairs={{0,192},{64,128},{128,64},{192,0},{1,193},{65,129},{129,65},{193,1... | collective-permute-start | bytes 1928 | tf_op jit(solution)/shard_map/ppermute | solution.py:359
  119.3 1.2 collective-permute-start.7
  120.5 1.0 pad_maximum_fusion.1
  121.5 1.7 %collective-permute-done.7 = f32[2,80]{1,0:T(2,128)S(1)} collective-permute-done((f32[2,80]{1,0:T(2,128)S(1)}, f32[2,80]{1,0:T(2,128)S(1)}, u32[]{:S(2)}, u32[]{:S(2)}) %collective-permute-start.7) | collective-permute-done | bytes 672 | tf_op jit(solution)/shard_map/ppermute | solution.py:358
  (47 shorter events, 2.8 us)
Async XLA Ops:
  0.6 21.5 %copy-start.6 = (s32[8]{0:T(128)S(1)}, s32[8]{0:T(128)}, u32[]{:S(2)}) copy-start(s32[8]{0:T(128)} %param.14) | copy-start | bytes 100
  0.6 1.0 copy-start.2
  1.6 0.7 copy-start.3
  4.5 42.2 %copy-start.5 = (s32[8]{0:T(128)S(1)}, s32[8]{0:T(128)}, u32[]{:S(2)}) copy-start(s32[8]{0:T(128)} %param.15) | copy-start | bytes 100
  4.5 36.1 %all-to-all-start = ((bf16[64,48,128]{2,1,0:T(8,128)(2,1)}), bf16[64,48,128]{2,1,0:T(8,128)(2,1)S(1)}, u32[]{:S(2)}, u32[]{:S(2)}) async-start(bf16[64,48,128]{2,1,0:T(8,128)(2,1)} %bitcast.5), calls=%async_computation | async-start | bytes 1572864 | tf_op jit(solution)/shard_map/all_to_all | solution.py:295
  18.2 28.5 %collective-permute-start.2 = (bf16[28,5120]{1,0:T(8,128)(2,1)}, bf16[28,5120]{1,0:T(8,128)(2,1)}, u32[]{:S(2)}, u32[]{:S(2)}) collective-permute-start(bf16[28,5120]{1,0:T(8,128)(2,1)} %bitcast.3.wq_ref.w0_ref), channel_id=1, source_target_pairs={{0,192},{64,128},{128,64},{192,0},{1,193},{65,129},{129,65},{193,1... | collective-permute-start | bytes 860168 | tf_op jit(solution)/shard_map/ppermute | solution.py:288
  21.6 25.2 %collective-permute-start.1 = (bf16[28,5120]{1,0:T(8,128)(2,1)}, bf16[28,5120]{1,0:T(8,128)(2,1)}, u32[]{:S(2)}, u32[]{:S(2)}) collective-permute-start(bf16[28,5120]{1,0:T(8,128)(2,1)} %bitcast.3.wq_ref.w0_ref), channel_id=1, source_target_pairs={{0,128},{128,0},{1,129},{129,1},{2,130},{130,2},{3,131},{131,3},{4... | collective-permute-start | bytes 860168 | tf_op jit(solution)/shard_map/ppermute | solution.py:287
  22.1 24.7 %collective-permute-start = (bf16[28,5120]{1,0:T(8,128)(2,1)}, bf16[28,5120]{1,0:T(8,128)(2,1)}, u32[]{:S(2)}, u32[]{:S(2)}) collective-permute-start(bf16[28,5120]{1,0:T(8,128)(2,1)} %bitcast.3.wq_ref.w0_ref), channel_id=1, source_target_pairs={{0,64},{64,0},{1,65},{65,1},{2,66},{66,2},{3,67},{67,3},{4,68},{68... | collective-permute-start | bytes 860168 | tf_op jit(solution)/shard_map/ppermute | solution.py:286
  40.6 28.7 %copy-start = (bf16[8,128,1024]{2,1,0:T(8,128)(2,1)S(1)}, bf16[8,128,1024]{2,1,0:T(8,128)(2,1)}, u32[]{:S(2)}) copy-start(bf16[8,128,1024]{2,1,0:T(8,128)(2,1)} %param.11) | copy-start | bytes 6291460
  40.6 28.7 %copy-start.4 = (s32[8]{0:T(128)S(1)}, s32[8]{0:T(128)}, u32[]{:S(2)}) copy-start(s32[8]{0:T(128)} %lengths_ref.1) | copy-start | bytes 100
  41.0 41.2 %collective-permute-start.5 = (bf16[80,3072]{1,0:T(8,128)(2,1)S(1)}, bf16[80,3072]{1,0:T(8,128)(2,1)}, u32[]{:S(2)}, u32[]{:S(2)}) collective-permute-start(bf16[80,3072]{1,0:T(8,128)(2,1)S(1)} %shard_map.114.b0_ref), channel_id=1, source_target_pairs={{0,192},{64,128},{128,64},{192,0},{1,193},{65,129},{129,65},{193,1... | collective-permute-start | bytes 1474568 | tf_op jit(solution)/shard_map/ppermute | solution.py:288
  46.2 36.0 %collective-permute-start.4 = (bf16[80,3072]{1,0:T(8,128)(2,1)S(1)}, bf16[80,3072]{1,0:T(8,128)(2,1)}, u32[]{:S(2)}, u32[]{:S(2)}) collective-permute-start(bf16[80,3072]{1,0:T(8,128)(2,1)S(1)} %shard_map.114.b0_ref), channel_id=1, source_target_pairs={{0,128},{128,0},{1,129},{129,1},{2,130},{130,2},{3,131},{131,3},{4... | collective-permute-start | bytes 1474568 | tf_op jit(solution)/shard_map/ppermute | solution.py:287
  46.7 35.5 %collective-permute-start.3 = (bf16[80,3072]{1,0:T(8,128)(2,1)S(1)}, bf16[80,3072]{1,0:T(8,128)(2,1)}, u32[]{:S(2)}, u32[]{:S(2)}) collective-permute-start(bf16[80,3072]{1,0:T(8,128)(2,1)S(1)} %shard_map.114.b0_ref), channel_id=1, source_target_pairs={{0,64},{64,0},{1,65},{65,1},{2,66},{66,2},{3,67},{67,3},{4,68},{68... | collective-permute-start | bytes 1474568 | tf_op jit(solution)/shard_map/ppermute | solution.py:286
  49.4 19.9 %all-to-all-start.1 = ((bf16[64,8,128]{2,1,0:T(8,128)(2,1)}), bf16[64,8,128]{2,1,0:T(8,128)(2,1)S(1)}, u32[]{:S(2)}, u32[]{:S(2)}) async-start(bf16[64,8,128]{2,1,0:T(8,128)(2,1)} %bitcast.7), calls=%async_computation.1 | async-start | bytes 262144 | tf_op jit(solution)/shard_map/all_to_all | solution.py:295
  69.3 1.6 %copy-start.1 = (bf16[8,128,1024]{2,1,0:T(8,128)(2,1)S(1)}, bf16[8,128,1024]{2,1,0:T(8,128)(2,1)}, u32[]{:S(2)}) copy-start(bf16[8,128,1024]{2,1,0:T(8,128)(2,1)} %param.12) | copy-start | bytes 6291460
  75.0 19.8 %all-to-all-start.2 = ((f32[64,8,128]{2,1,0:T(8,128)}), f32[64,8,128]{2,1,0:T(8,128)S(1)}, u32[]{:S(2)}, u32[]{:S(2)}) async-start(f32[64,8,128]{2,1,0:T(8,128)} %bitcast.11), calls=%async_computation.2 | async-start | bytes 524288 | tf_op jit(solution)/shard_map/all_to_all | solution.py:295
  97.5 16.0 %all-to-all-start.3 = ((f32[64,8,128]{2,1,0:T(8,128)}), f32[64,8,128]{2,1,0:T(8,128)S(1)}, u32[]{:S(2)}, u32[]{:S(2)}) async-start(f32[64,8,128]{2,1,0:T(8,128)} %bitcast.13), calls=%async_computation.3 | async-start | bytes 524288 | tf_op jit(solution)/shard_map/all_to_all | solution.py:295
  114.2 7.3 %collective-permute-start.6 = (f32[2,80]{1,0:T(2,128)S(1)}, f32[2,80]{1,0:T(2,128)S(1)}, u32[]{:S(2)}, u32[]{:S(2)}) collective-permute-start(f32[2,80]{1,0:T(2,128)S(1)} %get-tuple-element.10), channel_id=1, source_target_pairs={{0,192},{64,128},{128,64},{192,0},{1,193},{65,129},{129,65},{193,1... | collective-permute-start | bytes 1928 | tf_op jit(solution)/shard_map/ppermute | solution.py:359
  119.3 3.9 %collective-permute-start.7 = (f32[2,80]{1,0:T(2,128)S(1)}, f32[2,80]{1,0:T(2,128)S(1)}, u32[]{:S(2)}, u32[]{:S(2)}) collective-permute-start(f32[2,80]{1,0:T(2,128)S(1)} %get-tuple-element.11), channel_id=1, source_target_pairs={{0,128},{128,0},{1,129},{129,1},{2,130},{130,2},{3,131},{131,3},{4... | collective-permute-start | bytes 1928 | tf_op jit(solution)/shard_map/ppermute | solution.py:358
  120.5 2.7 %collective-permute-start.8 = (f32[2,80]{1,0:T(2,128)S(1)}, f32[2,80]{1,0:T(2,128)S(1)}, u32[]{:S(2)}, u32[]{:S(2)}) collective-permute-start(f32[2,80]{1,0:T(2,128)S(1)} %get-tuple-element.12), channel_id=1, source_target_pairs={{0,64},{64,0},{1,65},{65,1},{2,66},{66,2},{3,67},{67,3},{4,68},{68... | collective-permute-start | bytes 1928 | tf_op jit(solution)/shard_map/ppermute | solution.py:357

commit v2 on v1

v2 whole, which is shorter than its diff:
```python
import functools
import math

import jax
import jax.numpy as jnp
from jax import lax
from jax.experimental import pallas as pl
from jax.experimental.pallas import tpu as pltpu
from jax.sharding import Mesh
from jax.sharding import PartitionSpec as P

N_DEV = 64
N_GRP = 4
ROWS = 8
HEADS = 40
KV_HEADS = 8
SHARE = HEADS // KV_HEADS
LANES = 128
D = 5120
FEAT = D // N_DEV
WQ = 28
WO = 20
FULL = WQ + WO
PIECE = 40
MAIN = PIECE - ROWS
QW = N_DEV * WQ
OW = N_DEV * WO
POS = 128
NEG = -1e30

G_AXES = ("xh", "core")
D_AXES = ("xl", "y", "z")
F32 = jnp.float32
BF16 = jnp.bfloat16
VMEM = pl.BlockSpec(memory_space=pltpu.VMEM)
SMEM = pl.BlockSpec(memory_space=pltpu.SMEM)
ANY = pl.BlockSpec(memory_space=pl.ANY)
MIB = 1024 * 1024


def lane_iota(rows):
    return lax.broadcasted_iota(jnp.int32, (rows, LANES), 1)


def turned(lane, shift):
    return lane if shift % LANES == 0 else (lane - shift) & (LANES - 1)


def cut(tiles, start, width, lane):
    at, off = divmod(start, LANES)
    if off + width <= LANES:
        return tiles[at]
    return jnp.where(lane >= off, tiles[at], tiles[at + 1])


def lay(count, sources, width, lane):
    tiles = [None] * count
    for i, source in enumerate(sources):
        at, off = divmod(i * width, LANES)
        tiles[at] = source if tiles[at] is None else jnp.where(lane >= off, source, tiles[at])
        if off + width > LANES:
            tiles[at + 1] = source
    return tiles


def shift_of(dev, width):
    return (dev * width) & (LANES - 1)


def turned_back(x, shift):
    return pltpu.roll(x, (LANES - shift) & (LANES - 1), 1)


def halves(ref):
    parts = []
    for row in range(0, ref.shape[0], 16):
        both = ref[row : row + 16, :].astype(F32)
        parts += [both[0:8], both[8:16]]
    return parts


def swapped_blocks(blocks, group):
    odd = (group & 1) == 1
    high = (group & 2) == 2
    a, b, c, d = blocks
    a, b, c, d = (
        jnp.where(odd, b, a),
        jnp.where(odd, a, b),
        jnp.where(odd, d, c),
        jnp.where(odd, c, d),
    )
    return (
        jnp.where(high, c, a),
        jnp.where(high, d, b),
        jnp.where(high, a, c),
        jnp.where(high, b, d),
    )


def pack_kernel(
    dev_ref, hidden_hbm, wq_hbm, wo_hbm, out_ref, hidden_ref, wq_ref, wo_ref, rows_ref, spare_ref, sems
):
    copies = [
        pltpu.make_async_copy(hidden_hbm, hidden_ref, sems.at[0]),
        pltpu.make_async_copy(wq_hbm, wq_ref, sems.at[1]),
        pltpu.make_async_copy(wo_hbm, wo_ref, sems.at[2]),
    ]
    for copy in copies:
        copy.start()
    lane = lane_iota(MAIN)
    copies[0].wait()
    hidden = jnp.concatenate(
        [hidden_ref[...].astype(F32), jnp.zeros((ROWS, LANES - FEAT), F32)], axis=1
    )
    hidden = pltpu.roll(hidden, shift_of(dev_ref[0], FEAT), 1)
    copies[1].wait()
    rows_ref[0:WQ, :] = wq_ref[...].astype(F32)
    copies[2].wait()
    rows_ref[WQ:FULL, :] = wo_ref[...].astype(F32)
    for t in range(D // LANES):
        columns = slice(t * LANES, (t + 1) * LANES)
        rest = rows_ref[MAIN:FULL, columns]
        spare_ref[0:16, columns] = pltpu.roll(rest, FEAT, 1)
        spare_ref[16:32, columns] = pltpu.roll(rest, 2 * FEAT - LANES, 1)
    half = lane[0:16]
    from_spare = jnp.concatenate([turned(half, FEAT), turned(half, 2 * FEAT - LANES)], axis=0)
    pair = []
    for dest in range(N_DEV):
        at, off = divmod(dest * FEAT, LANES)
        main = {t: rows_ref[0:MAIN, t * LANES : (t + 1) * LANES] for t in (at, at + 1) if t < D // LANES}
        spare = {t: spare_ref[:, t * LANES : (t + 1) * LANES] for t in (at, at + 1) if t < D // LANES}
        piece = jnp.where(
            turned(lane, off) < FEAT,
            cut(main, dest * FEAT, FEAT, lane),
            cut(spare, dest * FEAT, FEAT, from_spare),
        )
        pair += [hidden, piece]
        if dest % 2:
            out_ref[(dest - 1) * PIECE : (dest + 1) * PIECE, :] = jnp.concatenate(
                pair, axis=0
            ).astype(BF16)
            pair = []


def project_kernel(
    dev_ref, group_ref, recv_ref, own_hbm, w1_ref, w2_ref, w3_ref, out_ref, w_ref, own_ref, sem
):
    own = pltpu.make_async_copy(own_hbm, own_ref, sem)
    own.start()
    lane = lane_iota(ROWS)
    dev, group = dev_ref[0], group_ref[0]
    for j, ref in enumerate((own_ref, w1_ref, w2_ref, w3_ref)):
        if j == 0:
            continue
        w_ref[32 * j + 16 : 32 * j + 32, :] = jnp.zeros((16, D), BF16)
        w_ref[32 * j : 32 * j + WQ, :] = ref[...]
    sources = []
    for source in range(N_DEV):
        row = source * PIECE - source * PIECE % 16
        both = recv_ref[row : row + 16, :].astype(F32)
        sources.append(both[8:16] if source % 2 else both[0:8])
    tiles = lay(D // LANES, sources, FEAT, lane)
    hidden = jnp.concatenate([t.astype(BF16) for t in tiles], axis=1)
    own.wait()
    w_ref[16:32, :] = jnp.zeros((16, D), BF16)
    w_ref[0:WQ, :] = own_ref[...]
    y = lax.dot_general(hidden, w_ref[...], (((1,), (1,)), ((), ())), preferred_element_type=F32)
    up, down = pltpu.roll(y, 32, 1), pltpu.roll(y, LANES - 32, 1)
    y = jnp.where((group & 1) == 1, jnp.where((lane & 32) == 0, down, up), y)
    y = jnp.where((group & 2) == 2, pltpu.roll(y, 64, 1), y)
    y = pltpu.roll(y, shift_of(dev, WQ), 1)
    two = jnp.concatenate([y, y], axis=0).astype(BF16)
    for pair in range(N_DEV // 2):
        out_ref[16 * pair : 16 * pair + 16, :] = two


def turn(dev, x):
    row = lax.broadcasted_iota(jnp.int32, (FEAT, LANES), 0)
    eye = (((row + shift_of(dev, FEAT)) & (LANES - 1)) == lane_iota(FEAT)).astype(BF16)
    return lax.dot_general(
        eye, x.astype(BF16), (((1,), (1,)), ((), ())), preferred_element_type=F32
    ).astype(BF16)


def turn_o_kernel(dev_ref, recv_ref, after_ref, out_ref, rows_ref):
    shift = shift_of(dev_ref[0], FEAT)
    first = ((lane_iota(16) - shift) & (LANES - 1)) < LANES - FEAT
    for source in range(N_DEV):
        if source % 2 == 0:
            both = recv_ref[source * PIECE : (source + 2) * PIECE, :].astype(F32)
        piece = both[source % 2 * PIECE + ROWS : (source % 2 + 1) * PIECE]
        rest = jnp.where(
            first,
            pltpu.roll(piece[0:16], LANES - FEAT, 1),
            pltpu.roll(piece[16:32], 2 * LANES - 2 * FEAT, 1),
        )
        rows_ref[source * WO : source * WO + MAIN - WQ, :] = piece[WQ:MAIN]
        rows_ref[source * WO + MAIN - WQ : (source + 1) * WO, :] = rest
    out_ref[...] = turn(dev_ref[0], rows_ref[...])


def turn_q_kernel(dev_ref, recv_ref, after_ref, out_ref, rows_ref):
    for source in range(N_DEV):
        if source % 2 == 0:
            both = recv_ref[source * PIECE : (source + 2) * PIECE, :].astype(F32)
        piece = both[source % 2 * PIECE + ROWS : (source % 2 + 1) * PIECE]
        rows_ref[source * WQ : (source + 1) * WQ, :] = piece[0:WQ]
    out_ref[...] = turn(dev_ref[0], rows_ref[...])


def attend_kernel(
    dev_ref, lengths_ref, recv_ref, keys_hbm, values_hbm, out_ref, keys_ref, values_ref, sems
):
    copies = []
    for i, (source, target) in enumerate(((keys_hbm, keys_ref), (values_hbm, values_ref))):
        for r in range(ROWS):
            rows = pl.ds(r * POS, POS)
            copies.append(
                pltpu.make_async_copy(source.at[rows], target.at[rows], sems.at[i, r])
            )
    for copy in copies:
        copy.start()
    lane = lane_iota(ROWS)
    sub = lax.broadcasted_iota(jnp.int32, (ROWS, LANES), 0)
    dev = dev_ref[0]
    scale = 1.0 / math.sqrt(LANES)
    sources = halves(recv_ref)
    tiles = []
    for g in range(N_GRP):
        frame = lay(QW // LANES, sources, WQ, turned(lane, 32 * g))
        tiles += [pltpu.roll(t, LANES - 32 * g, 1) for t in frame] if g else frame
    own_rows = [sub == r for r in range(ROWS)]
    valid = dev * POS + lane < lengths_ref[...]
    valid = jnp.concatenate([valid] * SHARE, axis=0)
    first = dev == 0

    for copy in copies[:ROWS]:
        copy.wait()
    weights = []
    for k in range(KV_HEADS):
        new_key = tiles[HEADS + k]
        q = jnp.concatenate(tiles[k * SHARE : (k + 1) * SHARE], axis=0)
        keys = keys_ref[:, k * LANES : (k + 1) * LANES]
        wide = lax.dot_general(
            q.astype(BF16), keys, (((1,), (1,)), ((), ())), preferred_element_type=F32
        )
        s = []
        for i in range(SHARE):
            line = wide[i * ROWS : (i + 1) * ROWS, 0:LANES]
            for r in range(1, ROWS):
                line = jnp.where(
                    own_rows[r],
                    wide[i * ROWS : (i + 1) * ROWS, r * LANES : (r + 1) * LANES],
                    line,
                )
            s.append(line)
        s = jnp.concatenate(s, axis=0) * scale
        s = jnp.where(valid, s, NEG)
        own = jnp.sum(q * jnp.concatenate([new_key] * SHARE, axis=0), axis=1, keepdims=True) * scale
        own = jnp.where(first, own, NEG)
        top = jnp.maximum(jnp.max(s, axis=1, keepdims=True), own)
        w = jnp.where(valid, jnp.exp(s - top), 0.0)
        own_w = jnp.where(first, jnp.exp(own - top), 0.0)
        weights.append((w, own_w, top, jnp.sum(w, axis=1, keepdims=True) + own_w))

    for copy in copies[ROWS:]:
        copy.wait()
    outs, tags = [], []
    at = lane & 7
    for k in range(KV_HEADS):
        w, own_w, top, total = weights[k]
        spread = []
        for r in range(ROWS):
            spread.append(
                jnp.concatenate(
                    [
                        jnp.where(own_rows[r], w[i * ROWS : (i + 1) * ROWS], 0.0)
                        for i in range(SHARE)
                    ],
                    axis=0,
                ).astype(BF16)
            )
        spread = jnp.concatenate(spread, axis=1)
        values = values_ref[:, k * LANES : (k + 1) * LANES]
        out = jnp.dot(spread, values, preferred_element_type=F32)
        out = out + own_w * jnp.concatenate([tiles[HEADS + KV_HEADS + k]] * SHARE, axis=0)
        for i in range(SHARE):
            rows = slice(i * ROWS, (i + 1) * ROWS)
            outs.append(out[rows])
            t = jnp.broadcast_to(top[rows], (ROWS, LANES))
            t0 = t.astype(BF16).astype(F32)
            t1 = (t - t0).astype(BF16).astype(F32)
            d = jnp.broadcast_to(total[rows], (ROWS, LANES))
            d0 = d.astype(BF16).astype(F32)
            tag = jnp.where(at == 0, t0, jnp.where(at == 1, t1, (t - t0) - t1))
            tags.append(jnp.where(at < 3, tag, jnp.where(at == 3, d0, d - d0)))
    pair = []
    for dest in range(N_DEV):
        h0, h1 = dest * FEAT // LANES, (dest * FEAT + FEAT - 1) // LANES
        tile = cut(outs, dest * FEAT, FEAT, lane)
        place = turned(lane, dest * FEAT)
        tile = jnp.where(place < FEAT, tile, jnp.where(place < FEAT + 8, tags[h0], tags[h1]))
        pair.append(tile)
        if dest % 2:
            out_ref[(dest - 1) * ROWS : (dest + 1) * ROWS, :] = jnp.concatenate(
                pair, axis=0
            ).astype(BF16)
            pair = []


def finish_kernel(dev_ref, group_ref, recv_ref, b0_ref, b1_ref, b2_ref, b3_ref, out_ref):
    lane = lane_iota(ROWS)
    dev, group = dev_ref[0], group_ref[0]
    start = dev * FEAT
    split = ((start + FEAT - 1) // LANES) * LANES - start
    split = jnp.where(split <= 0, FEAT, split)
    left = (lane < split) | ((lane >= FEAT) & (lane < FEAT + 8))
    shift = shift_of(dev, FEAT)
    parts = [turned_back(x, shift) for x in halves(recv_ref)]
    terms = [(x + pltpu.roll(x, LANES - 1, 1)) + pltpu.roll(x, LANES - 2, 1) for x in parts]
    tops = terms
    while len(tops) > 1:
        tops = [jnp.maximum(a, b) for a, b in zip(tops[0::2], tops[1::2])]
    top = tops[0]
    total = [jnp.zeros((ROWS, LANES), F32) for _ in range(4)]
    for s, part in enumerate(parts):
        e = jnp.exp(terms[s] - top)
        f = jnp.where(left, e[:, FEAT : FEAT + 1], e[:, FEAT + 8 : FEAT + 9])
        total[s % 4] = total[s % 4] + f * part
    total = (total[0] + total[1]) + (total[2] + total[3])
    den = total + pltpu.roll(total, LANES - 1, 1)
    den = jnp.where(left, den[:, FEAT + 3 : FEAT + 4], den[:, FEAT + 11 : FEAT + 12])
    attn = (total / den)[:, 0:FEAT].astype(BF16)
    blocks = [
        jnp.dot(attn, ref[...], preferred_element_type=F32)
        for ref in (b0_ref, b1_ref, b2_ref, b3_ref)
    ]
    blocks = swapped_blocks(blocks, group)
    tiles = [
        block[:, t * LANES : (t + 1) * LANES] for block in blocks for t in range(OW // LANES)
    ]
    for dest in range(0, N_DEV, 2):
        pair = [cut(tiles, d * FEAT, FEAT, lane) for d in (dest, dest + 1)]
        out_ref[dest * ROWS : (dest + 2) * ROWS, :] = jnp.concatenate(pair, axis=0).astype(BF16)


def total_kernel(dev_ref, table_ref, recv_ref, after_ref, hidden_ref, r0_ref, r1_ref, r2_ref, r3_ref):
    sums = halves(recv_ref)
    while len(sums) > 1:
        sums = [a + b for a, b in zip(sums[0::2], sums[1::2])]
    hidden = turned_back(sums[0], shift_of(dev_ref[0], FEAT))
    hidden_ref[...] = hidden[:, 0:FEAT]
    table = table_ref[...]
    packed = table[:, 0:1] * hidden[0:1, :]
    for r in range(1, ROWS):
        packed = packed + table[:, r : r + 1] * hidden[r : r + 1, :]
    for j, ref in enumerate((r0_ref, r1_ref, r2_ref, r3_ref)):
        ref[...] = packed[2 * j : 2 * j + 2, 0:FEAT]


def order_kernel(group_ref, after_ref, *refs):
    q_out, o_out, mark_ref = refs[8:]
    mark_ref[...] = jnp.zeros_like(mark_ref)
    for j in range(N_GRP):
        group = group_ref[0] ^ j
        q_out[:, pl.ds(pl.multiple_of(group * QW, LANES), QW)] = refs[j][...]
        o_out[:, pl.ds(pl.multiple_of(group * OW, LANES), OW)] = refs[N_GRP + j][...]


def call(kernel, outs, specs, scratch=(), vmem=32, flops=None):
    many = isinstance(outs, (list, tuple))
    return pl.pallas_call(
        kernel,
        out_shape=outs,
        in_specs=specs,
        out_specs=[VMEM] * len(outs) if many else VMEM,
        scratch_shapes=list(scratch),
        compiler_params=pltpu.CompilerParams(vmem_limit_bytes=vmem * MIB),
        cost_estimate=flops
        and pl.CostEstimate(flops=flops, bytes_accessed=4 * MIB, transcendentals=0),
    )


SWAP = [(0, 1), (1, 0)]


def to_groups(x):
    far = lax.ppermute(x, "xh", SWAP)
    return lax.ppermute(x, "core", SWAP), far, lax.ppermute(far, "core", SWAP)


def to_groups_at_once(x):
    return (
        lax.ppermute(x, "core", SWAP),
        lax.ppermute(x, "xh", SWAP),
        lax.ppermute(x, G_AXES, [(g, g ^ 3) for g in range(N_GRP)]),
    )


def exchange(x):
    rows = x.shape[0] // N_DEV
    x = x.reshape(N_DEV, rows, x.shape[1])
    x = lax.all_to_all(x, D_AXES, split_axis=0, concat_axis=0, tiled=True)
    return x.reshape(N_DEV * rows, x.shape[2])


def shards(hidden_in, w_qkv, w_o, key_cache, value_cache, lengths, finished, assignment):
    struct = jax.ShapeDtypeStruct
    group = lax.axis_index(G_AXES).astype(jnp.int32)
    dev = lax.axis_index(D_AXES).astype(jnp.int32)
    dev, group_one = dev.reshape(1), group.reshape(1)
    lengths = jnp.broadcast_to(lengths[:, None], (ROWS, LANES))

    wq, wo = w_qkv.T, w_o.T
    others = to_groups(wq)
    part = struct((N_DEV * ROWS, LANES), BF16)
    sent = call(
        pack_kernel,
        struct((N_DEV * PIECE, LANES), BF16),
        [SMEM] + [ANY] * 3,
        [
            pltpu.VMEM((ROWS, FEAT), BF16),
            pltpu.VMEM((WQ, D), BF16),
            pltpu.VMEM((WO, D), BF16),
            pltpu.VMEM((FULL, D), F32),
            pltpu.VMEM((MAIN, D), F32),
            pltpu.SemaphoreType.DMA((3,)),
        ],
        vmem=60,
    )(dev, hidden_in, wq, wo)
    recv = exchange(sent)
    sent = call(
        project_kernel,
        part,
        [SMEM, SMEM, VMEM, ANY] + [VMEM] * 3,
        [
            pltpu.VMEM((LANES, D), BF16),
            pltpu.VMEM((WQ, D), BF16),
            pltpu.SemaphoreType.DMA,
        ],
    )(dev, group_one, recv, wq, *others)
    got = exchange(sent)

    o_block = call(
        turn_o_kernel,
        struct((FEAT, OW), BF16),
        [SMEM, VMEM, ANY],
        [pltpu.VMEM((OW, LANES), F32)],
    )(dev, recv, sent)
    o_blocks = (o_block,) + to_groups(o_block)

    q_block = call(
        turn_q_kernel,
        struct((FEAT, QW), BF16),
        [SMEM, VMEM, ANY],
        [pltpu.VMEM((QW, LANES), F32)],
    )(dev, recv, sent)
    q_blocks = (q_block,) + to_groups(q_block)
    cache = (ROWS * POS, KV_HEADS * LANES)
    sent = call(
        attend_kernel,
        part,
        [SMEM, VMEM, VMEM, ANY, ANY],
        [pltpu.VMEM(cache, BF16)] * 2 + [pltpu.SemaphoreType.DMA((2, ROWS))],
        vmem=54,
        flops=10**11,
    )(dev, lengths, got, key_cache.reshape(cache), value_cache.reshape(cache))
    got = exchange(sent)
    sent = call(finish_kernel, part, [SMEM, SMEM] + [VMEM] * 5)(
        dev, group_one, got, *o_blocks
    )
    w_qkv_gen, w_o_gen, mark = call(
        order_kernel,
        [
            struct((FEAT, N_GRP * QW), BF16),
            struct((FEAT, N_GRP * OW), BF16),
            struct((ROWS, LANES), F32),
        ],
        [SMEM, ANY] + [VMEM] * 8,
    )(group_one, sent, *q_blocks, *o_blocks)
    got = exchange(sent)

    learners = jnp.arange(N_GRP, dtype=jnp.int32) ^ group
    matches = (assignment[None, :] == learners[:, None]) & (finished[None, :] == 1)
    ranks = jnp.cumsum(matches.astype(jnp.int32), axis=1)
    slots = jnp.arange(1, 3, dtype=jnp.int32)
    table = matches[:, None, :] & (ranks[:, None, :] == slots[None, :, None])
    table = table.reshape(ROWS, ROWS).astype(F32)
    few = struct((2, FEAT), F32)
    hidden_out, r0, r1, r2, r3 = call(
        total_kernel, [struct((ROWS, FEAT), F32)] + [few] * 4, [SMEM, VMEM, VMEM, ANY]
    )(dev, table, got, mark)
    r1 = lax.ppermute(r1, "core", SWAP)
    r2 = lax.ppermute(r2, "xh", SWAP)
    r3 = lax.ppermute(r3, G_AXES, [(g, g ^ 3) for g in range(N_GRP)])
    returned = jnp.concatenate(swapped_blocks((r0, r1, r2, r3), group), axis=0)
    return (hidden_out, returned, w_qkv_gen, w_o_gen)


def solution(mesh):
    fine = Mesh(mesh.devices.reshape(2, 2, 2, 4, 8), G_AXES + D_AXES)
    return jax.shard_map(
        shards,
        mesh=fine,
        in_specs=(
            P(G_AXES, D_AXES),
            P(None, G_AXES + D_AXES),
            P(None, G_AXES + D_AXES),
            P(G_AXES, D_AXES, None),
            P(G_AXES, D_AXES, None),
            P(G_AXES),
            P(G_AXES),
            P(G_AXES),
        ),
        out_specs=(P(G_AXES, D_AXES), P(G_AXES, D_AXES), P(D_AXES, None), P(D_AXES, None)),
        check_vma=False,
    )
```

time: 124 us -> 107 us (0.86)
  waiting for transfers between devices: 52.3 us -> 39.3 us
  other arithmetic: 4.57 us -> 0.95 us
  local copies, waits for them, and re-layouts: 3.51 us -> 0.8 us
  starting transfers between devices: 50 us -> 51.9 us
    all_to_all x4, waiting for transfers between devices: 50.5 us -> 22.4 us  [exchange(): x = lax.all_to_all(x, D_AXES, split_axis=0, concat_axis=0, tiled=True)]
    ppermute x8 -> x11, waiting for transfers between devices: 1.75 us -> 13.6 us  [the longest x3 11.6 us: to_groups(): far = lax.ppermute(x, 'xh', SWAP)]
    ppermute x8 -> x11, starting transfers between devices: 10.8 us -> 17.3 us  [the longest x3 5.59 us: to_groups(): far = lax.ppermute(x, 'xh', SWAP)]
    ppermute x1, starting transfers between devices: 5.12 us -> 1.15 us  [shards(): r3 = lax.ppermute(r3, G_AXES, [(g, g ^ 3) for g in range(N_GRP)])]
    ppermute x1, waiting for transfers between devices: 0.01 us -> 3.34 us  [shards(): r3 = lax.ppermute(r3, G_AXES, [(g, g ^ 3) for g in range(N_GRP)])]
    unnamed x14 -> x10, local copies, waits for them, and re-layouts: 3.23 us -> 0.02 us
    concatenate x2 -> x0, other arithmetic: 2.05 us -> none  [the longest x1 1.09 us: shards(): w_qkv_gen = jnp.concatenate([b[:, 0:QW] for b in ordered], axis=1)]
    select_n x2 -> x1, other arithmetic: 1.5 us -> 0.01 us  [swapped_blocks(): jnp.where(high, c, a)]
  transfers between devices with their start and end apart: 13 -> 16, of which waited for: 5 -> 9; matrix products, arithmetic and copies ran while one was open for 3% -> 1% of each run, Pallas kernels for 6% -> 8%
where the time goes in v2:
time: 107 us
  starting transfers between devices  51.9 us (49%)
  waiting for transfers between devices  39.3 us (37%)
  Pallas kernels  13 us (12%)
    all_to_all x4, starting transfers between devices, exchange(): x = lax.all_to_all(x, D_AXES, split_axis=0, concat_axis=0, tiled=True)  33.4 us
    all_to_all x4, waiting for transfers between devices, exchange(): x = lax.all_to_all(x, D_AXES, split_axis=0, concat_axis=0, tiled=True)  22.4 us
    ppermute x3, waiting for transfers between devices, to_groups(): far = lax.ppermute(x, 'xh', SWAP)  11.6 us
    ppermute x3, starting transfers between devices, to_groups(): far = lax.ppermute(x, 'xh', SWAP)  5.59 us
    ppermute x6, starting transfers between devices, to_groups(): return (lax.ppermute(x, 'core', SWAP), far, lax.ppermute(far, 'core', SWAP))  5.55 us
    pallas_call x1, Pallas kernels, shards(): call(attend_kernel, part, [SMEM, VMEM, VMEM, ANY, ANY], [pltpu.VMEM(cache...  5.02 us
    ppermute x1, starting transfers between devices, shards(): r1 = lax.ppermute(r1, 'core', SWAP)  4.39 us
    ppermute x1, waiting for transfers between devices, shards(): r3 = lax.ppermute(r3, G_AXES, [(g, g ^ 3) for g in range(N_GRP)])  3.34 us
  transfers between devices with their start and end apart: 16, of which 9 were waited for; matrix products, arithmetic and copies ran while one was open for 1% of the time, Pallas kernels for 8%

profile of v2, /device:TPU:1, one launch (start us, length us, event | category | flops | bytes accessed | tf_op | source)
XLA Modules:
  0.0 106.7 jit_solution(4957886218407650476)
XLA Ops:
  0.7 2.1 %shard_map.111 = bf16[2560,128]{1,0:T(8,128)(2,1)} custom-call(s32[1]{0:T(128)} %bitcast.dev_ref, bf16[8,80]{1,0:T(8,128)(2,1)} %hidden_hbm.1, bf16[28,5120]{1,0:T(8,128)(2,1)} %bitcast.18, bf16[20,5120]{1,0:T(8,128)(2,1)} %bitcast.25), custom_call_target="tpu_custom_call" | custom-call | tf_op jit(solution)/shard_map/pallas_call | solution.py:417
  2.8 13.6 %all-to-all-start = ((bf16[64,40,128]{2,1,0:T(8,128)(2,1)}), bf16[64,40,128]{2,1,0:T(8,128)(2,1)S(1)}, u32[]{:S(2)}, u32[]{:S(2)}) async-start(bf16[64,40,128]{2,1,0:T(8,128)(2,1)} %bitcast.24), calls=%async_computation | async-start | bytes 1310720 | tf_op jit(solution)/shard_map/all_to_all | solution.py:403
  16.4 2.5 %collective-permute-start.1 = (bf16[28,5120]{1,0:T(8,128)(2,1)S(1)}, bf16[28,5120]{1,0:T(8,128)(2,1)S(1)}, u32[]{:S(2)}, u32[]{:S(2)}) collective-permute-start(bf16[28,5120]{1,0:T(8,128)(2,1)S(1)} %bitcast.19), channel_id=1, source_target_pairs={{0,128},{128,0},{1,129},{129,1},{2,130},{130,2},{3,131},{131,3},{4... | collective-permute-start | bytes 860168 | tf_op jit(solution)/shard_map/ppermute | solution.py:388
  19.0 1.2 %collective-permute-start = (bf16[28,5120]{1,0:T(8,128)(2,1)S(1)}, bf16[28,5120]{1,0:T(8,128)(2,1)S(1)}, u32[]{:S(2)}, u32[]{:S(2)}) collective-permute-start(bf16[28,5120]{1,0:T(8,128)(2,1)S(1)} %bitcast.20), channel_id=1, source_target_pairs={{0,64},{64,0},{1,65},{65,1},{2,66},{66,2},{3,67},{67,3},{4,68},{68... | collective-permute-start | bytes 860168 | tf_op jit(solution)/shard_map/ppermute | solution.py:389
  20.2 11.6 %collective-permute-done.1.w2_ref = bf16[28,5120]{1,0:T(8,128)(2,1)S(1)} collective-permute-done((bf16[28,5120]{1,0:T(8,128)(2,1)S(1)}, bf16[28,5120]{1,0:T(8,128)(2,1)S(1)}, u32[]{:S(2)}, u32[]{:S(2)}) %collective-permute-start.1) | collective-permute-done | bytes 286752 | tf_op jit(solution)/shard_map/ppermute | solution.py:388
  31.8 1.8 %collective-permute-start.2 = (bf16[28,5120]{1,0:T(8,128)(2,1)S(1)}, bf16[28,5120]{1,0:T(8,128)(2,1)S(1)}, u32[]{:S(2)}, u32[]{:S(2)}) collective-permute-start(bf16[28,5120]{1,0:T(8,128)(2,1)S(1)} %collective-permute-done.1.w2_ref), channel_id=1, source_target_pairs={{0,64},{64,0},{1,65},{65,1},{2,66},{66,2},{3,67},{67,3},{4,68},{68... | collective-permute-start | bytes 860168 | tf_op jit(solution)/shard_map/ppermute | solution.py:389
  33.6 1.3 %collective-permute-done.2.w3_ref = bf16[28,5120]{1,0:T(8,128)(2,1)S(1)} collective-permute-done((bf16[28,5120]{1,0:T(8,128)(2,1)S(1)}, bf16[28,5120]{1,0:T(8,128)(2,1)S(1)}, u32[]{:S(2)}, u32[]{:S(2)}) %collective-permute-start.2) | collective-permute-done | bytes 286752 | tf_op jit(solution)/shard_map/ppermute | solution.py:389
  35.9 1.5 %shard_map.112.after_ref = bf16[512,128]{1,0:T(8,128)(2,1)} custom-call(s32[1]{0:T(128)} %bitcast.dev_ref, s32[1]{0:T(128)} %bitcast.2.group_ref, bf16[2560,128]{1,0:T(8,128)(2,1)S(1)} %bitcast.15, bf16[28,5120]{1,0:T(8,128)(2,1)S(1)} %bitcast.21, bf16[28,5120]{1,0:T(8,128)(2,1)S(1)} %collective-permute-done.w1_ref, ...), custom_call_target="tpu_custom_call" | custom-call | tf_op jit(solution)/shard_map/pallas_call | solution.py:432
  37.4 10.5 %all-to-all-start.1 = ((bf16[64,8,128]{2,1,0:T(8,128)(2,1)}), bf16[64,8,128]{2,1,0:T(8,128)(2,1)S(1)}, u32[]{:S(2)}, u32[]{:S(2)}) async-start(bf16[64,8,128]{2,1,0:T(8,128)(2,1)} %bitcast.7), calls=%async_computation.1 | async-start | bytes 262144 | tf_op jit(solution)/shard_map/all_to_all | solution.py:403
  48.7 1.8 %collective-permute-start.4 = (bf16[80,1280]{1,0:T(8,128)(2,1)S(1)}, bf16[80,1280]{1,0:T(8,128)(2,1)S(1)}, u32[]{:S(2)}, u32[]{:S(2)}) collective-permute-start(bf16[80,1280]{1,0:T(8,128)(2,1)S(1)} %shard_map.114.b0_ref.refs_4_), channel_id=1, source_target_pairs={{0,128},{128,0},{1,129},{129,1},{2,130},{130,2},{3,131},{131,3},{4... | collective-permute-start | bytes 614408 | tf_op jit(solution)/shard_map/ppermute | solution.py:388
  50.5 1.2 %collective-permute-start.7 = (bf16[80,1792]{1,0:T(8,128)(2,1)S(1)}, bf16[80,1792]{1,0:T(8,128)(2,1)S(1)}, u32[]{:S(2)}, u32[]{:S(2)}) collective-permute-start(bf16[80,1792]{1,0:T(8,128)(2,1)S(1)} %shard_map.116.refs_0_), channel_id=1, source_target_pairs={{0,128},{128,0},{1,129},{129,1},{2,130},{130,2},{3,131},{131,3},{4... | collective-permute-start | bytes 860168 | tf_op jit(solution)/shard_map/ppermute | solution.py:388
  51.7 6.5 %all-to-all-done.1 = bf16[64,8,128]{2,1,0:T(8,128)(2,1)S(1)} async-done(((bf16[64,8,128]{2,1,0:T(8,128)(2,1)}), bf16[64,8,128]{2,1,0:T(8,128)(2,1)S(1)}, u32[]{:S(2)}, u32[]{:S(2)}) %all-to-all-start.1) | async-done | bytes 131104 | tf_op jit(solution)/shard_map/all_to_all | solution.py:403
  58.9 5.0 %shard_map.113 = bf16[512,128]{1,0:T(8,128)(2,1)} custom-call(s32[1]{0:T(128)} %bitcast.dev_ref, s32[8,128]{1,0:T(8,128)} %broadcast_in_dim.2.lengths_ref, bf16[512,128]{1,0:T(8,128)(2,1)} %bitcast.27, bf16[1024,1024]{1,0:T(8,128)(2,1)} %bitcast.29, bf16[1024,1024]{1,0:T(8,128)(2,1)} %bitcast.30), custom_call_target="tpu_custom_call" | custom-call | flops 99999997952 | bytes 4194304 | tf_op jit(solution)/shard_map/pallas_call | solution.py:460
  63.9 4.7 %all-to-all-start.2 = ((bf16[64,8,128]{2,1,0:T(8,128)(2,1)}), bf16[64,8,128]{2,1,0:T(8,128)(2,1)S(1)}, u32[]{:S(2)}, u32[]{:S(2)}) async-start(bf16[64,8,128]{2,1,0:T(8,128)(2,1)} %bitcast.26), calls=%async_computation.2 | async-start | bytes 262144 | tf_op jit(solution)/shard_map/all_to_all | solution.py:403
  68.6 1.9 %collective-permute-start.3 = (bf16[80,1280]{1,0:T(8,128)(2,1)S(1)}, bf16[80,1280]{1,0:T(8,128)(2,1)S(1)}, u32[]{:S(2)}, u32[]{:S(2)}) collective-permute-start(bf16[80,1280]{1,0:T(8,128)(2,1)S(1)} %shard_map.114.b0_ref.refs_4_), channel_id=1, source_target_pairs={{0,64},{64,0},{1,65},{65,1},{2,66},{66,2},{3,67},{67,3},{4,68},{68... | collective-permute-start | bytes 614408 | tf_op jit(solution)/shard_map/ppermute | solution.py:389
  71.9 6.7 %all-to-all-done.2 = bf16[64,8,128]{2,1,0:T(8,128)(2,1)S(1)} async-done(((bf16[64,8,128]{2,1,0:T(8,128)(2,1)}), bf16[64,8,128]{2,1,0:T(8,128)(2,1)S(1)}, u32[]{:S(2)}, u32[]{:S(2)}) %all-to-all-start.2) | async-done | bytes 131104 | tf_op jit(solution)/shard_map/all_to_all | solution.py:403
  78.6 1.5 %shard_map.115.after_ref = bf16[512,128]{1,0:T(8,128)(2,1)} custom-call(s32[1]{0:T(128)} %bitcast.dev_ref, s32[1]{0:T(128)} %bitcast.2.group_ref, bf16[512,128]{1,0:T(8,128)(2,1)S(1)} %bitcast.22, bf16[80,1280]{1,0:T(8,128)(2,1)S(1)} %shard_map.114.b0_ref.refs_4_, bf16[80,1280]{1,0:T(8,128)(2,1)S(1)} %collective-permute-done.3.b1_ref.refs_5_, ...), custom_call_target="tpu_custom_call" | custom-call | tf_op jit(solution)/shard_map/pallas_call | solution.py:469
  80.1 4.6 %all-to-all-start.3 = ((bf16[64,8,128]{2,1,0:T(8,128)(2,1)}), bf16[64,8,128]{2,1,0:T(8,128)(2,1)S(1)}, u32[]{:S(2)}, u32[]{:S(2)}) async-start(bf16[64,8,128]{2,1,0:T(8,128)(2,1)} %bitcast.13), calls=%async_computation.3 | async-start | bytes 262144 | tf_op jit(solution)/shard_map/all_to_all | solution.py:403
  85.1 1.4 %shard_map.117 = (bf16[80,7168]{1,0:T(8,128)(2,1)}, bf16[80,5120]{1,0:T(8,128)(2,1)}, f32[8,128]{1,0:T(8,128)S(1)}) custom-call(s32[1]{0:T(128)} %bitcast.2.group_ref, bf16[512,128]{1,0:T(8,128)(2,1)} %shard_map.115.after_ref, bf16[80,1792]{1,0:T(8,128)(2,1)S(1)} %shard_map.116.refs_0_, bf16[80,1792]{1,0:T(8,128)(2,1)S(1)} %collective-permute-done.6.refs_1_, ...), custom_call_target="tpu_custom_call" | custom-call | tf_op jit(solution)/shard_map/pallas_call | solution.py:472
  86.5 8.2 %all-to-all-done.3 = bf16[64,8,128]{2,1,0:T(8,128)(2,1)S(1)} async-done(((bf16[64,8,128]{2,1,0:T(8,128)(2,1)}), bf16[64,8,128]{2,1,0:T(8,128)(2,1)S(1)}, u32[]{:S(2)}, u32[]{:S(2)}) %all-to-all-start.3) | async-done | bytes 131104 | tf_op jit(solution)/shard_map/all_to_all | solution.py:403
  95.4 1.8 %collective-permute-start.10 = (f32[2,80]{1,0:T(2,128)S(1)}, f32[2,80]{1,0:T(2,128)S(1)}, u32[]{:S(2)}, u32[]{:S(2)}) collective-permute-start(f32[2,80]{1,0:T(2,128)S(1)} %get-tuple-element.15), channel_id=1, source_target_pairs={{0,128},{128,0},{1,129},{129,1},{2,130},{130,2},{3,131},{131,3},{4... | collective-permute-start | bytes 1928 | tf_op jit(solution)/shard_map/ppermute | solution.py:494
  97.2 4.4 %collective-permute-start.11 = (f32[2,80]{1,0:T(2,128)S(1)}, f32[2,80]{1,0:T(2,128)S(1)}, u32[]{:S(2)}, u32[]{:S(2)}) collective-permute-start(f32[2,80]{1,0:T(2,128)S(1)} %get-tuple-element.16), channel_id=1, source_target_pairs={{0,64},{64,0},{1,65},{65,1},{2,66},{66,2},{3,67},{67,3},{4,68},{68... | collective-permute-start | bytes 1928 | tf_op jit(solution)/shard_map/ppermute | solution.py:493
  101.6 1.1 %collective-permute-start.9 = (f32[2,80]{1,0:T(2,128)S(1)}, f32[2,80]{1,0:T(2,128)S(1)}, u32[]{:S(2)}, u32[]{:S(2)}) collective-permute-start(f32[2,80]{1,0:T(2,128)S(1)} %get-tuple-element.14), channel_id=1, source_target_pairs={{0,192},{64,128},{128,64},{192,0},{1,193},{65,129},{129,65},{193,1... | collective-permute-start | bytes 1928 | tf_op jit(solution)/shard_map/ppermute | solution.py:495
  102.7 3.3 %collective-permute-done.9 = f32[2,80]{1,0:T(2,128)S(1)} collective-permute-done((f32[2,80]{1,0:T(2,128)S(1)}, f32[2,80]{1,0:T(2,128)S(1)}, u32[]{:S(2)}, u32[]{:S(2)}) %collective-permute-start.9) | collective-permute-done | bytes 672 | tf_op jit(solution)/shard_map/ppermute | solution.py:495
  (40 shorter events, 5.5 us)
Async XLA Ops:
  0.6 15.8 %copy-start = (bf16[5120,28]{0,1:T(8,128)(2,1)S(1)}, bf16[5120,28]{0,1:T(8,128)(2,1)}, u32[]{:S(2)}) copy-start(bf16[5120,28]{0,1:T(8,128)(2,1)} %param.9) | copy-start | bytes 860164
  2.8 45.1 %copy-start.4 = (s32[8]{0:T(128)S(1)}, s32[8]{0:T(128)}, u32[]{:S(2)}) copy-start(s32[8]{0:T(128)} %param.14) | copy-start | bytes 100
  2.8 33.1 %all-to-all-start = ((bf16[64,40,128]{2,1,0:T(8,128)(2,1)}), bf16[64,40,128]{2,1,0:T(8,128)(2,1)S(1)}, u32[]{:S(2)}, u32[]{:S(2)}) async-start(bf16[64,40,128]{2,1,0:T(8,128)(2,1)} %bitcast.24), calls=%async_computation | async-start | bytes 1310720 | tf_op jit(solution)/shard_map/all_to_all | solution.py:403
  16.4 15.3 %collective-permute-start.1 = (bf16[28,5120]{1,0:T(8,128)(2,1)S(1)}, bf16[28,5120]{1,0:T(8,128)(2,1)S(1)}, u32[]{:S(2)}, u32[]{:S(2)}) collective-permute-start(bf16[28,5120]{1,0:T(8,128)(2,1)S(1)} %bitcast.19), channel_id=1, source_target_pairs={{0,128},{128,0},{1,129},{129,1},{2,130},{130,2},{3,131},{131,3},{4... | collective-permute-start | bytes 860168 | tf_op jit(solution)/shard_map/ppermute | solution.py:388
  19.0 14.6 %collective-permute-start = (bf16[28,5120]{1,0:T(8,128)(2,1)S(1)}, bf16[28,5120]{1,0:T(8,128)(2,1)S(1)}, u32[]{:S(2)}, u32[]{:S(2)}) collective-permute-start(bf16[28,5120]{1,0:T(8,128)(2,1)S(1)} %bitcast.20), channel_id=1, source_target_pairs={{0,64},{64,0},{1,65},{65,1},{2,66},{66,2},{3,67},{67,3},{4,68},{68... | collective-permute-start | bytes 860168 | tf_op jit(solution)/shard_map/ppermute | solution.py:389
  31.8 3.1 %collective-permute-start.2 = (bf16[28,5120]{1,0:T(8,128)(2,1)S(1)}, bf16[28,5120]{1,0:T(8,128)(2,1)S(1)}, u32[]{:S(2)}, u32[]{:S(2)}) collective-permute-start(bf16[28,5120]{1,0:T(8,128)(2,1)S(1)} %collective-permute-done.1.w2_ref), channel_id=1, source_target_pairs={{0,64},{64,0},{1,65},{65,1},{2,66},{66,2},{3,67},{67,3},{4,68},{68... | collective-permute-start | bytes 860168 | tf_op jit(solution)/shard_map/ppermute | solution.py:389
  35.9 22.3 %copy-start.2 = (s32[8]{0:T(128)S(1)}, s32[8]{0:T(128)}, u32[]{:S(2)}) copy-start(s32[8]{0:T(128)} %param.13) | copy-start | bytes 100
  37.4 20.8 %all-to-all-start.1 = ((bf16[64,8,128]{2,1,0:T(8,128)(2,1)}), bf16[64,8,128]{2,1,0:T(8,128)(2,1)S(1)}, u32[]{:S(2)}, u32[]{:S(2)}) async-start(bf16[64,8,128]{2,1,0:T(8,128)(2,1)} %bitcast.7), calls=%async_computation.1 | async-start | bytes 262144 | tf_op jit(solution)/shard_map/all_to_all | solution.py:403
  48.7 21.8 %collective-permute-start.4 = (bf16[80,1280]{1,0:T(8,128)(2,1)S(1)}, bf16[80,1280]{1,0:T(8,128)(2,1)S(1)}, u32[]{:S(2)}, u32[]{:S(2)}) collective-permute-start(bf16[80,1280]{1,0:T(8,128)(2,1)S(1)} %shard_map.114.b0_ref.refs_4_), channel_id=1, source_target_pairs={{0,128},{128,0},{1,129},{129,1},{2,130},{130,2},{3,131},{131,3},{4... | collective-permute-start | bytes 614408 | tf_op jit(solution)/shard_map/ppermute | solution.py:388
  50.5 20.6 %collective-permute-start.7 = (bf16[80,1792]{1,0:T(8,128)(2,1)S(1)}, bf16[80,1792]{1,0:T(8,128)(2,1)S(1)}, u32[]{:S(2)}, u32[]{:S(2)}) collective-permute-start(bf16[80,1792]{1,0:T(8,128)(2,1)S(1)} %shard_map.116.refs_0_), channel_id=1, source_target_pairs={{0,128},{128,0},{1,129},{129,1},{2,130},{130,2},{3,131},{131,3},{4... | collective-permute-start | bytes 860168 | tf_op jit(solution)/shard_map/ppermute | solution.py:388
  58.2 0.7 copy-start.1
  58.9 11.7 %copy-start.3 = (s32[8]{0:T(128)S(1)}, s32[8]{0:T(128)}, u32[]{:S(2)}) copy-start(s32[8]{0:T(128)} %param.15) | copy-start | bytes 100
  63.9 14.7 %all-to-all-start.2 = ((bf16[64,8,128]{2,1,0:T(8,128)(2,1)}), bf16[64,8,128]{2,1,0:T(8,128)(2,1)S(1)}, u32[]{:S(2)}, u32[]{:S(2)}) async-start(bf16[64,8,128]{2,1,0:T(8,128)(2,1)} %bitcast.26), calls=%async_computation.2 | async-start | bytes 262144 | tf_op jit(solution)/shard_map/all_to_all | solution.py:403
  68.6 2.9 %collective-permute-start.3 = (bf16[80,1280]{1,0:T(8,128)(2,1)S(1)}, bf16[80,1280]{1,0:T(8,128)(2,1)S(1)}, u32[]{:S(2)}, u32[]{:S(2)}) collective-permute-start(bf16[80,1280]{1,0:T(8,128)(2,1)S(1)} %shard_map.114.b0_ref.refs_4_), channel_id=1, source_target_pairs={{0,64},{64,0},{1,65},{65,1},{2,66},{66,2},{3,67},{67,3},{4,68},{68... | collective-permute-start | bytes 614408 | tf_op jit(solution)/shard_map/ppermute | solution.py:389
  70.5 1.5 %collective-permute-start.5 = (bf16[80,1280]{1,0:T(8,128)(2,1)S(1)}, bf16[80,1280]{1,0:T(8,128)(2,1)S(1)}, u32[]{:S(2)}, u32[]{:S(2)}) collective-permute-start(bf16[80,1280]{1,0:T(8,128)(2,1)S(1)} %collective-permute-done.4.b2_ref.refs_6_), channel_id=1, source_target_pairs={{0,64},{64,0},{1,65},{65,1},{2,66},{66,2},{3,67},{67,3},{4,68},{68... | collective-permute-start | bytes 614408 | tf_op jit(solution)/shard_map/ppermute | solution.py:389
  70.7 14.5 %collective-permute-start.6 = (bf16[80,1792]{1,0:T(8,128)(2,1)S(1)}, bf16[80,1792]{1,0:T(8,128)(2,1)S(1)}, u32[]{:S(2)}, u32[]{:S(2)}) collective-permute-start(bf16[80,1792]{1,0:T(8,128)(2,1)S(1)} %shard_map.116.refs_0_), channel_id=1, source_target_pairs={{0,64},{64,0},{1,65},{65,1},{2,66},{66,2},{3,67},{67,3},{4,68},{68... | collective-permute-start | bytes 860168 | tf_op jit(solution)/shard_map/ppermute | solution.py:389
  71.1 14.0 %collective-permute-start.8 = (bf16[80,1792]{1,0:T(8,128)(2,1)S(1)}, bf16[80,1792]{1,0:T(8,128)(2,1)S(1)}, u32[]{:S(2)}, u32[]{:S(2)}) collective-permute-start(bf16[80,1792]{1,0:T(8,128)(2,1)S(1)} %collective-permute-done.7.refs_2_), channel_id=1, source_target_pairs={{0,64},{64,0},{1,65},{65,1},{2,66},{66,2},{3,67},{67,3},{4,68},{68... | collective-permute-start | bytes 860168 | tf_op jit(solution)/shard_map/ppermute | solution.py:389
  80.1 14.6 %all-to-all-start.3 = ((bf16[64,8,128]{2,1,0:T(8,128)(2,1)}), bf16[64,8,128]{2,1,0:T(8,128)(2,1)S(1)}, u32[]{:S(2)}, u32[]{:S(2)}) async-start(bf16[64,8,128]{2,1,0:T(8,128)(2,1)} %bitcast.13), calls=%async_computation.3 | async-start | bytes 262144 | tf_op jit(solution)/shard_map/all_to_all | solution.py:403
  95.4 7.3 %collective-permute-start.10 = (f32[2,80]{1,0:T(2,128)S(1)}, f32[2,80]{1,0:T(2,128)S(1)}, u32[]{:S(2)}, u32[]{:S(2)}) collective-permute-start(f32[2,80]{1,0:T(2,128)S(1)} %get-tuple-element.15), channel_id=1, source_target_pairs={{0,128},{128,0},{1,129},{129,1},{2,130},{130,2},{3,131},{131,3},{4... | collective-permute-start | bytes 1928 | tf_op jit(solution)/shard_map/ppermute | solution.py:494
  97.2 5.5 %collective-permute-start.11 = (f32[2,80]{1,0:T(2,128)S(1)}, f32[2,80]{1,0:T(2,128)S(1)}, u32[]{:S(2)}, u32[]{:S(2)}) collective-permute-start(f32[2,80]{1,0:T(2,128)S(1)} %get-tuple-element.16), channel_id=1, source_target_pairs={{0,64},{64,0},{1,65},{65,1},{2,66},{66,2},{3,67},{67,3},{4,68},{68... | collective-permute-start | bytes 1928 | tf_op jit(solution)/shard_map/ppermute | solution.py:493
  101.6 4.5 %collective-permute-start.9 = (f32[2,80]{1,0:T(2,128)S(1)}, f32[2,80]{1,0:T(2,128)S(1)}, u32[]{:S(2)}, u32[]{:S(2)}) collective-permute-start(f32[2,80]{1,0:T(2,128)S(1)} %get-tuple-element.14), channel_id=1, source_target_pairs={{0,192},{64,128},{128,64},{192,0},{1,193},{65,129},{129,65},{193,1... | collective-permute-start | bytes 1928 | tf_op jit(solution)/shard_map/ppermute | solution.py:495

commit v3 on v2

--- a/solution.py
+++ b/solution.py
@@ -25,6 +25,7 @@
 MAIN = PIECE - ROWS
 QW = N_DEV * WQ
 OW = N_DEV * WO
+GROUP = ROWS * SHARE
 POS = 128
 NEG = -1e30
 
@@ -143,13 +144,13 @@
 
 
 def project_kernel(
-    dev_ref, group_ref, recv_ref, own_hbm, w1_ref, w2_ref, w3_ref, out_ref, w_ref, own_ref, sem
+    dev_ref, group_ref, recv_ref, own_hbm, w2_ref, both_ref, out_ref, w_ref, own_ref, sem
 ):
     own = pltpu.make_async_copy(own_hbm, own_ref, sem)
     own.start()
     lane = lane_iota(ROWS)
     dev, group = dev_ref[0], group_ref[0]
-    for j, ref in enumerate((own_ref, w1_ref, w2_ref, w3_ref)):
+    for j, ref in enumerate((own_ref, both_ref.at[0], w2_ref, both_ref.at[1])):
         if j == 0:
             continue
         w_ref[32 * j + 16 : 32 * j + 32, :] = jnp.zeros((16, D), BF16)
@@ -182,7 +183,9 @@
     ).astype(BF16)
 
 
-def turn_o_kernel(dev_ref, recv_ref, after_ref, out_ref, rows_ref):
+def turn_o_kernel(dev_ref, lengths_ref, recv_ref, after_ref, out_ref, wide_ref, rows_ref):
+    for r in range(ROWS):
+        wide_ref[r : r + 1, :] = jnp.full((1, LANES), lengths_ref[r], jnp.int32)
     shift = shift_of(dev_ref[0], FEAT)
     first = ((lane_iota(16) - shift) & (LANES - 1)) < LANES - FEAT
     for source in range(N_DEV):
@@ -208,18 +211,7 @@
     out_ref[...] = turn(dev_ref[0], rows_ref[...])
 
 
-def attend_kernel(
-    dev_ref, lengths_ref, recv_ref, keys_hbm, values_hbm, out_ref, keys_ref, values_ref, sems
-):
-    copies = []
-    for i, (source, target) in enumerate(((keys_hbm, keys_ref), (values_hbm, values_ref))):
-        for r in range(ROWS):
-            rows = pl.ds(r * POS, POS)
-            copies.append(
-                pltpu.make_async_copy(source.at[rows], target.at[rows], sems.at[i, r])
-            )
-    for copy in copies:
-        copy.start()
+def score_kernel(dev_ref, lengths_ref, recv_ref, keys_ref, w_ref, own_ref, tag_ref, fresh_ref):
     lane = lane_iota(ROWS)
     sub = lax.broadcasted_iota(jnp.int32, (ROWS, LANES), 0)
     dev = dev_ref[0]
@@ -233,10 +225,7 @@
     valid = dev * POS + lane < lengths_ref[...]
     valid = jnp.concatenate([valid] * SHARE, axis=0)
     first = dev == 0
-
-    for copy in copies[:ROWS]:
-        copy.wait()
-    weights = []
+    at = lane_iota(GROUP) & 7
     for k in range(KV_HEADS):
         new_key = tiles[HEADS + k]
         q = jnp.concatenate(tiles[k * SHARE : (k + 1) * SHARE], axis=0)
@@ -261,39 +250,41 @@
         top = jnp.maximum(jnp.max(s, axis=1, keepdims=True), own)
         w = jnp.where(valid, jnp.exp(s - top), 0.0)
         own_w = jnp.where(first, jnp.exp(own - top), 0.0)
-        weights.append((w, own_w, top, jnp.sum(w, axis=1, keepdims=True) + own_w))
-
-    for copy in copies[ROWS:]:
-        copy.wait()
+        total = jnp.sum(w, axis=1, keepdims=True) + own_w
+        rows = slice(k * GROUP, (k + 1) * GROUP)
+        w_ref[rows, :] = w
+        own_ref[rows, :] = jnp.broadcast_to(own_w, (GROUP, LANES))
+        t = jnp.broadcast_to(top, (GROUP, LANES))
+        t0 = t.astype(BF16).astype(F32)
+        t1 = (t - t0).astype(BF16).astype(F32)
+        d = jnp.broadcast_to(total, (GROUP, LANES))
+        d0 = d.astype(BF16).astype(F32)
+        tag = jnp.where(at == 0, t0, jnp.where(at == 1, t1, (t - t0) - t1))
+        tag_ref[rows, :] = jnp.where(at < 3, tag, jnp.where(at == 3, d0, d - d0))
+        fresh_ref[k * ROWS : (k + 1) * ROWS, :] = tiles[HEADS + KV_HEADS + k]
+
+
+def value_kernel(w_ref, own_ref, tag_ref, fresh_ref, values_ref, out_ref):
+    lane = lane_iota(ROWS)
+    sub = lax.broadcasted_iota(jnp.int32, (ROWS, LANES), 0)
+    own_rows = [sub == r for r in range(ROWS)]
     outs, tags = [], []
-    at = lane & 7
     for k in range(KV_HEADS):
-        w, own_w, top, total = weights[k]
+        heads = [slice(k * GROUP + i * ROWS, k * GROUP + (i + 1) * ROWS) for i in range(SHARE)]
         spread = []
         for r in range(ROWS):
             spread.append(
                 jnp.concatenate(
-                    [
-                        jnp.where(own_rows[r], w[i * ROWS : (i + 1) * ROWS], 0.0)
-                        for i in range(SHARE)
-                    ],
-                    axis=0,
+                    [jnp.where(own_rows[r], w_ref[h, :], 0.0) for h in heads], axis=0
                 ).astype(BF16)
             )
         spread = jnp.concatenate(spread, axis=1)
         values = values_ref[:, k * LANES : (k + 1) * LANES]
         out = jnp.dot(spread, values, preferred_element_type=F32)
-        out = out + own_w * jnp.concatenate([tiles[HEADS + KV_HEADS + k]] * SHARE, axis=0)
-        for i in range(SHARE):
-            rows = slice(i * ROWS, (i + 1) * ROWS)
-            outs.append(out[rows])
-            t = jnp.broadcast_to(top[rows], (ROWS, LANES))
-            t0 = t.astype(BF16).astype(F32)
-            t1 = (t - t0).astype(BF16).astype(F32)
-            d = jnp.broadcast_to(total[rows], (ROWS, LANES))
-            d0 = d.astype(BF16).astype(F32)
-            tag = jnp.where(at == 0, t0, jnp.where(at == 1, t1, (t - t0) - t1))
-            tags.append(jnp.where(at < 3, tag, jnp.where(at == 3, d0, d - d0)))
+        fresh = fresh_ref[k * ROWS : (k + 1) * ROWS, :]
+        for i, h in enumerate(heads):
+            outs.append(out[i * ROWS : (i + 1) * ROWS] + own_ref[h, :] * fresh)
+            tags.append(tag_ref[h, :])
     pair = []
     for dest in range(N_DEV):
         h0, h1 = dest * FEAT // LANES, (dest * FEAT + FEAT - 1) // LANES
@@ -409,10 +400,10 @@
     group = lax.axis_index(G_AXES).astype(jnp.int32)
     dev = lax.axis_index(D_AXES).astype(jnp.int32)
     dev, group_one = dev.reshape(1), group.reshape(1)
-    lengths = jnp.broadcast_to(lengths[:, None], (ROWS, LANES))
 
     wq, wo = w_qkv.T, w_o.T
-    others = to_groups(wq)
+    far = lax.ppermute(wq, "xh", SWAP)
+    both = lax.ppermute(jnp.stack([wq, far]), "core", SWAP)
     part = struct((N_DEV * ROWS, LANES), BF16)
     sent = call(
         pack_kernel,
@@ -432,21 +423,21 @@
     sent = call(
         project_kernel,
         part,
-        [SMEM, SMEM, VMEM, ANY] + [VMEM] * 3,
+        [SMEM, SMEM, VMEM, ANY] + [VMEM] * 2,
         [
             pltpu.VMEM((LANES, D), BF16),
             pltpu.VMEM((WQ, D), BF16),
             pltpu.SemaphoreType.DMA,
         ],
-    )(dev, group_one, recv, wq, *others)
+    )(dev, group_one, recv, wq, far, both)
     got = exchange(sent)
 
-    o_block = call(
+    o_block, lengths = call(
         turn_o_kernel,
-        struct((FEAT, OW), BF16),
-        [SMEM, VMEM, ANY],
+        [struct((FEAT, OW), BF16), struct((ROWS, LANES), jnp.int32)],
+        [SMEM, SMEM, VMEM, ANY],
         [pltpu.VMEM((OW, LANES), F32)],
-    )(dev, recv, sent)
+    )(dev, lengths, recv, sent)
     o_blocks = (o_block,) + to_groups(o_block)
 
     q_block = call(
@@ -457,14 +448,14 @@
     )(dev, recv, sent)
     q_blocks = (q_block,) + to_groups(q_block)
     cache = (ROWS * POS, KV_HEADS * LANES)
-    sent = call(
-        attend_kernel,
-        part,
-        [SMEM, VMEM, VMEM, ANY, ANY],
-        [pltpu.VMEM(cache, BF16)] * 2 + [pltpu.SemaphoreType.DMA((2, ROWS))],
-        vmem=54,
-        flops=10**11,
-    )(dev, lengths, got, key_cache.reshape(cache), value_cache.reshape(cache))
+    tall = struct((KV_HEADS * GROUP, LANES), F32)
+    scored = call(
+        score_kernel,
+        [tall] * 3 + [struct((KV_HEADS * ROWS, LANES), F32)],
+        [SMEM] + [VMEM] * 3,
+        flops=10**10,
+    )(dev, lengths, got, key_cache.reshape(cache))
+    sent = call(value_kernel, part, [VMEM] * 5, flops=10**10)(*scored, value_cache.reshape(cache))
     got = exchange(sent)
     sent = call(finish_kernel, part, [SMEM, SMEM] + [VMEM] * 5)(
         dev, group_one, got, *o_blocks

time: 107 us -> 104 us (0.972)
  starting transfers between devices: 51.9 us -> 48.5 us
  local copies, waits for them, and re-layouts: 0.8 us -> 2.95 us
  Pallas kernels: 13 us -> 10.9 us
    all_to_all x4, waiting for transfers between devices: 22.4 us -> 34.2 us  [exchange(): x = lax.all_to_all(x, D_AXES, split_axis=0, concat_axis=0, tiled=True)]
    ppermute x3 -> x2, waiting for transfers between devices: 11.6 us -> 0.01 us  [to_groups(): far = lax.ppermute(x, 'xh', SWAP)]
    ppermute x0 -> x2, starting transfers between devices: none -> 4.98 us  [the longest x1 3.66 us: shards(): far = lax.ppermute(wq, 'xh', SWAP)]
    all_to_all x4, starting transfers between devices: 33.4 us -> 29.3 us  [exchange(): x = lax.all_to_all(x, D_AXES, split_axis=0, concat_axis=0, tiled=True)]
    ppermute x3 -> x2, starting transfers between devices: 5.59 us -> 3.06 us  [to_groups(): far = lax.ppermute(x, 'xh', SWAP)]
    unnamed x10 -> x12, local copies, waits for them, and re-layouts: 0.02 us -> 2.15 us
    pallas_call x3 -> x4, Pallas kernels: 6.94 us -> 4.85 us  [the longest x1 1.52 us: shards(): call(project_kernel, part, [SMEM, SMEM, VMEM, ANY] + [VMEM] * 2, [pltpu.V...]
    ppermute x1, waiting for transfers between devices: 3.34 us -> 1.64 us  [shards(): r3 = lax.ppermute(r3, G_AXES, [(g, g ^ 3) for g in range(N_GRP)])]
  transfers between devices with their start and end apart: 16 -> 15, of which waited for: 9 -> 9; matrix products, arithmetic and copies ran while one was open for 1% -> 1% of each run, Pallas kernels for 8% -> 8%
where the time goes in v3:
time: 104 us; the launch traced here: 103 us
  starting transfers between devices  48.5 us (47%)
  waiting for transfers between devices  39.2 us (38%)
  Pallas kernels  10.9 us (10%)
  local copies, waits for them, and re-layouts  2.95 us (3%)
    all_to_all x4, waiting for transfers between devices, exchange(): x = lax.all_to_all(x, D_AXES, split_axis=0, concat_axis=0, tiled=True)  34.2 us
    all_to_all x4, starting transfers between devices, exchange(): x = lax.all_to_all(x, D_AXES, split_axis=0, concat_axis=0, tiled=True)  29.3 us
    ppermute x1, starting transfers between devices, shards(): r1 = lax.ppermute(r1, 'core', SWAP)  4.38 us
    ppermute x4, starting transfers between devices, to_groups(): return (lax.ppermute(x, 'core', SWAP), far, lax.ppermute(far, 'core', SWAP))  3.9 us
    ppermute x1, starting transfers between devices, shards(): far = lax.ppermute(wq, 'xh', SWAP)  3.66 us
    ppermute x2, starting transfers between devices, to_groups(): far = lax.ppermute(x, 'xh', SWAP)  3.06 us
    unnamed x12, local copies, waits for them, and re-layouts  2.15 us
    pallas_call x1, Pallas kernels, shards(): call(pack_kernel, struct((N_DEV * PIECE, LANES), BF16), [SMEM] + [ANY] *...  2.1 us
  transfers between devices with their start and end apart: 15, of which 9 were waited for; matrix products, arithmetic and copies ran while one was open for 1% of the time, Pallas kernels for 8%

profile of v3, /device:TPU:1, one launch (start us, length us, event | category | flops | bytes accessed | tf_op | source)
XLA Modules:
  0.0 103.4 jit_solution(8347418896369993160)
XLA Ops:
  0.6 3.7 %collective-permute-start = (bf16[28,5120]{1,0:T(8,128)(2,1)}, bf16[28,5120]{1,0:T(8,128)(2,1)S(1)}, u32[]{:S(2)}, u32[]{:S(2)}) collective-permute-start(bf16[28,5120]{1,0:T(8,128)(2,1)} %bitcast.21), channel_id=1, source_target_pairs={{0,128},{128,0},{1,129},{129,1},{2,130},{130,2},{3,131},{131,3},{4... | collective-permute-start | bytes 860168 | tf_op jit(solution)/shard_map/ppermute | solution.py:405
  4.3 2.1 %shard_map.111 = bf16[2560,128]{1,0:T(8,128)(2,1)} custom-call(s32[1]{0:T(128)} %bitcast.dev_ref, bf16[8,80]{1,0:T(8,128)(2,1)} %hidden_hbm.1, bf16[28,5120]{1,0:T(8,128)(2,1)} %bitcast.22, bf16[20,5120]{1,0:T(8,128)(2,1)} %bitcast.32), custom_call_target="tpu_custom_call" | custom-call | tf_op jit(solution)/shard_map/pallas_call | solution.py:408
  6.4 11.9 %all-to-all-start = ((bf16[64,40,128]{2,1,0:T(8,128)(2,1)}), bf16[64,40,128]{2,1,0:T(8,128)(2,1)S(1)}, u32[]{:S(2)}, u32[]{:S(2)}) async-start(bf16[64,40,128]{2,1,0:T(8,128)(2,1)} %bitcast.31), calls=%async_computation | async-start | bytes 1310720 | tf_op jit(solution)/shard_map/all_to_all | solution.py:394
  19.0 1.3 %collective-permute-start.1 = (bf16[2,28,5120]{2,0,1:T(2,128)(2,1)S(1)}, bf16[2,28,5120]{2,0,1:T(2,128)(2,1)S(1)}, u32[]{:S(2)}, u32[]{:S(2)}) collective-permute-start(bf16[2,28,5120]{2,0,1:T(2,128)(2,1)S(1)} %copy.12), channel_id=1, source_target_pairs={{0,64},{64,0},{1,65},{65,1},{2,66},{66,2},{3,67},{67,3},{4,68},{68... | collective-permute-start | bytes 1720328 | tf_op jit(solution)/shard_map/ppermute | solution.py:406
  20.3 1.6 %collective-permute-done.1 = bf16[2,28,5120]{2,0,1:T(2,128)(2,1)S(1)} collective-permute-done((bf16[2,28,5120]{2,0,1:T(2,128)(2,1)S(1)}, bf16[2,28,5120]{2,0,1:T(2,128)(2,1)S(1)}, u32[]{:S(2)}, u32[]{:S(2)}) %collective-permute-start.1) | collective-permute-done | bytes 573472 | tf_op jit(solution)/shard_map/ppermute | solution.py:406
  22.0 15.1 %all-to-all-done = bf16[64,40,128]{2,1,0:T(8,128)(2,1)S(1)} async-done(((bf16[64,40,128]{2,1,0:T(8,128)(2,1)}), bf16[64,40,128]{2,1,0:T(8,128)(2,1)S(1)}, u32[]{:S(2)}, u32[]{:S(2)}) %all-to-all-start) | async-done | bytes 655392 | tf_op jit(solution)/shard_map/all_to_all | solution.py:394
  37.1 1.5 %shard_map.112.after_ref = bf16[512,128]{1,0:T(8,128)(2,1)} custom-call(s32[1]{0:T(128)} %bitcast.dev_ref, s32[1]{0:T(128)} %bitcast.2.group_ref, bf16[2560,128]{1,0:T(8,128)(2,1)S(1)} %bitcast.18, bf16[28,5120]{1,0:T(8,128)(2,1)S(1)} %bitcast.24, bf16[28,5120]{1,0:T(8,128)(2,1)S(1)} %collective-permute-done.w2_ref, bf16[2,28,5120]{2,1,0:T(8,128)(2,1)S(1)} %copy.13.both_ref), custom_call_target="tpu_custom_call" | custom-call | tf_op jit(solution)/shard_map/pallas_call | solution.py:423
  38.7 6.6 %all-to-all-start.1 = ((bf16[64,8,128]{2,1,0:T(8,128)(2,1)}), bf16[64,8,128]{2,1,0:T(8,128)(2,1)S(1)}, u32[]{:S(2)}, u32[]{:S(2)}) async-start(bf16[64,8,128]{2,1,0:T(8,128)(2,1)} %bitcast.9), calls=%async_computation.1 | async-start | bytes 262144 | tf_op jit(solution)/shard_map/all_to_all | solution.py:394
  46.6 1.8 %collective-permute-start.3 = (bf16[80,1280]{1,0:T(8,128)(2,1)S(1)}, bf16[80,1280]{1,0:T(8,128)(2,1)S(1)}, u32[]{:S(2)}, u32[]{:S(2)}) collective-permute-start(bf16[80,1280]{1,0:T(8,128)(2,1)S(1)} %get-tuple-element.23.b0_ref.refs_4_), channel_id=1, source_target_pairs={{0,128},{128,0},{1,129},{129,1},{2,130},{130,2},{3,131},{131,3},{4... | collective-permute-start | bytes 614408 | tf_op jit(solution)/shard_map/ppermute | solution.py:379
  48.4 1.2 %collective-permute-start.6 = (bf16[80,1792]{1,0:T(8,128)(2,1)S(1)}, bf16[80,1792]{1,0:T(8,128)(2,1)S(1)}, u32[]{:S(2)}, u32[]{:S(2)}) collective-permute-start(bf16[80,1792]{1,0:T(8,128)(2,1)S(1)} %shard_map.117.refs_0_), channel_id=1, source_target_pairs={{0,128},{128,0},{1,129},{129,1},{2,130},{130,2},{3,131},{131,3},{4... | collective-permute-start | bytes 860168 | tf_op jit(solution)/shard_map/ppermute | solution.py:379
  49.6 5.7 %all-to-all-done.1 = bf16[64,8,128]{2,1,0:T(8,128)(2,1)S(1)} async-done(((bf16[64,8,128]{2,1,0:T(8,128)(2,1)}), bf16[64,8,128]{2,1,0:T(8,128)(2,1)S(1)}, u32[]{:S(2)}, u32[]{:S(2)}) %all-to-all-start.1) | async-done | bytes 131104 | tf_op jit(solution)/shard_map/all_to_all | solution.py:394
  55.3 1.6 %copy-done.2 = bf16[8,128,1024]{2,1,0:T(8,128)(2,1)S(1)} copy-done((bf16[8,128,1024]{2,1,0:T(8,128)(2,1)S(1)}, bf16[8,128,1024]{2,1,0:T(8,128)(2,1)}, u32[]{:S(2)}) %copy-start.2) | copy-done | bytes 2097176
  58.5 1.4 %shard_map.115 = bf16[512,128]{1,0:T(8,128)(2,1)} custom-call(f32[320,128]{1,0:T(8,128)S(1)} %get-tuple-element.19.w_ref, f32[320,128]{1,0:T(8,128)S(1)} %get-tuple-element.20.own_ref, f32[320,128]{1,0:T(8,128)S(1)} %get-tuple-element.21.tag_ref, f32[64,128]{1,0:T(8,128)S(1)} %get-tuple-element.22.fresh_ref, bf16[1024,1024]{1,0:T(8,128)(2,1)S(1)} %bitcast.30), custom_call_target="tpu_custom_call" | custom-call | flops 10000000000 | bytes 4194304 | tf_op jit(solution)/shard_map/pallas_call | solution.py:458
  59.8 5.1 %all-to-all-start.2 = ((bf16[64,8,128]{2,1,0:T(8,128)(2,1)}), bf16[64,8,128]{2,1,0:T(8,128)(2,1)S(1)}, u32[]{:S(2)}, u32[]{:S(2)}) async-start(bf16[64,8,128]{2,1,0:T(8,128)(2,1)} %bitcast.13), calls=%async_computation.2 | async-start | bytes 262144 | tf_op jit(solution)/shard_map/all_to_all | solution.py:394
  64.9 3.3 %collective-permute-start.2 = (bf16[80,1280]{1,0:T(8,128)(2,1)S(1)}, bf16[80,1280]{1,0:T(8,128)(2,1)S(1)}, u32[]{:S(2)}, u32[]{:S(2)}) collective-permute-start(bf16[80,1280]{1,0:T(8,128)(2,1)S(1)} %get-tuple-element.23.b0_ref.refs_4_), channel_id=1, source_target_pairs={{0,64},{64,0},{1,65},{65,1},{2,66},{66,2},{3,67},{67,3},{4,68},{68... | collective-permute-start | bytes 614408 | tf_op jit(solution)/shard_map/ppermute | solution.py:380
  69.6 5.3 %all-to-all-done.2 = bf16[64,8,128]{2,1,0:T(8,128)(2,1)S(1)} async-done(((bf16[64,8,128]{2,1,0:T(8,128)(2,1)}), bf16[64,8,128]{2,1,0:T(8,128)(2,1)S(1)}, u32[]{:S(2)}, u32[]{:S(2)}) %all-to-all-start.2) | async-done | bytes 131104 | tf_op jit(solution)/shard_map/all_to_all | solution.py:394
  74.9 1.5 %shard_map.116.after_ref = bf16[512,128]{1,0:T(8,128)(2,1)} custom-call(s32[1]{0:T(128)} %bitcast.dev_ref, s32[1]{0:T(128)} %bitcast.2.group_ref, bf16[512,128]{1,0:T(8,128)(2,1)S(1)} %bitcast.26, bf16[80,1280]{1,0:T(8,128)(2,1)S(1)} %get-tuple-element.23.b0_ref.refs_4_, bf16[80,1280]{1,0:T(8,128)(2,1)S(1)} %collective-permute-done.2.b1_ref.refs_5_, ...), custom_call_target="tpu_custom_call" | custom-call | tf_op jit(solution)/shard_map/pallas_call | solution.py:460
  76.4 5.8 %all-to-all-start.3 = ((bf16[64,8,128]{2,1,0:T(8,128)(2,1)}), bf16[64,8,128]{2,1,0:T(8,128)(2,1)S(1)}, u32[]{:S(2)}, u32[]{:S(2)}) async-start(bf16[64,8,128]{2,1,0:T(8,128)(2,1)} %bitcast.15), calls=%async_computation.3 | async-start | bytes 262144 | tf_op jit(solution)/shard_map/all_to_all | solution.py:394
  82.6 1.4 %shard_map.118 = (bf16[80,7168]{1,0:T(8,128)(2,1)}, bf16[80,5120]{1,0:T(8,128)(2,1)}, f32[8,128]{1,0:T(8,128)S(1)}) custom-call(s32[1]{0:T(128)} %bitcast.2.group_ref, bf16[512,128]{1,0:T(8,128)(2,1)} %shard_map.116.after_ref, bf16[80,1792]{1,0:T(8,128)(2,1)S(1)} %shard_map.117.refs_0_, bf16[80,1792]{1,0:T(8,128)(2,1)S(1)} %collective-permute-done.5.refs_1_, ...), custom_call_target="tpu_custom_call" | custom-call | tf_op jit(solution)/shard_map/pallas_call | solution.py:463
  84.0 8.2 %all-to-all-done.3 = bf16[64,8,128]{2,1,0:T(8,128)(2,1)S(1)} async-done(((bf16[64,8,128]{2,1,0:T(8,128)(2,1)}), bf16[64,8,128]{2,1,0:T(8,128)(2,1)S(1)}, u32[]{:S(2)}, u32[]{:S(2)}) %all-to-all-start.3) | async-done | bytes 131104 | tf_op jit(solution)/shard_map/all_to_all | solution.py:394
  92.9 4.4 %collective-permute-start.10 = (f32[2,80]{1,0:T(2,128)S(1)}, f32[2,80]{1,0:T(2,128)S(1)}, u32[]{:S(2)}, u32[]{:S(2)}) collective-permute-start(f32[2,80]{1,0:T(2,128)S(1)} %get-tuple-element.28), channel_id=1, source_target_pairs={{0,64},{64,0},{1,65},{65,1},{2,66},{66,2},{3,67},{67,3},{4,68},{68... | collective-permute-start | bytes 1928 | tf_op jit(solution)/shard_map/ppermute | solution.py:484
  97.2 1.6 %collective-permute-start.8 = (f32[2,80]{1,0:T(2,128)S(1)}, f32[2,80]{1,0:T(2,128)S(1)}, u32[]{:S(2)}, u32[]{:S(2)}) collective-permute-start(f32[2,80]{1,0:T(2,128)S(1)} %get-tuple-element.26), channel_id=1, source_target_pairs={{0,192},{64,128},{128,64},{192,0},{1,193},{65,129},{129,65},{193,1... | collective-permute-start | bytes 1928 | tf_op jit(solution)/shard_map/ppermute | solution.py:486
  98.8 1.3 %collective-permute-start.9 = (f32[2,80]{1,0:T(2,128)S(1)}, f32[2,80]{1,0:T(2,128)S(1)}, u32[]{:S(2)}, u32[]{:S(2)}) collective-permute-start(f32[2,80]{1,0:T(2,128)S(1)} %get-tuple-element.27), channel_id=1, source_target_pairs={{0,128},{128,0},{1,129},{129,1},{2,130},{130,2},{3,131},{131,3},{4... | collective-permute-start | bytes 1928 | tf_op jit(solution)/shard_map/ppermute | solution.py:485
  100.1 1.6 %collective-permute-done.8 = f32[2,80]{1,0:T(2,128)S(1)} collective-permute-done((f32[2,80]{1,0:T(2,128)S(1)}, f32[2,80]{1,0:T(2,128)S(1)}, u32[]{:S(2)}, u32[]{:S(2)}) %collective-permute-start.8) | collective-permute-done | bytes 672 | tf_op jit(solution)/shard_map/ppermute | solution.py:486
  (43 shorter events, 7.8 us)
Async XLA Ops:
  0.6 17.7 %copy-start = (bf16[5120,28]{0,1:T(8,128)(2,1)S(1)}, bf16[5120,28]{0,1:T(8,128)(2,1)}, u32[]{:S(2)}) copy-start(bf16[5120,28]{0,1:T(8,128)(2,1)} %param.9) | copy-start | bytes 860164
  0.6 17.6 %collective-permute-start = (bf16[28,5120]{1,0:T(8,128)(2,1)}, bf16[28,5120]{1,0:T(8,128)(2,1)S(1)}, u32[]{:S(2)}, u32[]{:S(2)}) collective-permute-start(bf16[28,5120]{1,0:T(8,128)(2,1)} %bitcast.21), channel_id=1, source_target_pairs={{0,128},{128,0},{1,129},{129,1},{2,130},{130,2},{3,131},{131,3},{4... | collective-permute-start | bytes 860168 | tf_op jit(solution)/shard_map/ppermute | solution.py:405
  6.4 30.7 %all-to-all-start = ((bf16[64,40,128]{2,1,0:T(8,128)(2,1)}), bf16[64,40,128]{2,1,0:T(8,128)(2,1)S(1)}, u32[]{:S(2)}, u32[]{:S(2)}) async-start(bf16[64,40,128]{2,1,0:T(8,128)(2,1)} %bitcast.31), calls=%async_computation | async-start | bytes 1310720 | tf_op jit(solution)/shard_map/all_to_all | solution.py:394
  19.0 26.3 %copy-start.5 = (s32[8]{0:T(128)S(1)}, s32[8]{0:T(128)}, u32[]{:S(2)}) copy-start(s32[8]{0:T(128)} %param.14) | copy-start | bytes 100
  19.0 2.9 %collective-permute-start.1 = (bf16[2,28,5120]{2,0,1:T(2,128)(2,1)S(1)}, bf16[2,28,5120]{2,0,1:T(2,128)(2,1)S(1)}, u32[]{:S(2)}, u32[]{:S(2)}) collective-permute-start(bf16[2,28,5120]{2,0,1:T(2,128)(2,1)S(1)} %copy.12), channel_id=1, source_target_pairs={{0,64},{64,0},{1,65},{65,1},{2,66},{66,2},{3,67},{67,3},{4,68},{68... | collective-permute-start | bytes 1720328 | tf_op jit(solution)/shard_map/ppermute | solution.py:406
  20.3 25.3 %copy-start.1 = (s32[8]{0:T(128)S(1)}, s32[8]{0:T(128)}, u32[]{:S(2)}) copy-start(s32[8]{0:T(128)} %lengths_ref.1) | copy-start | bytes 100
  38.7 16.6 %all-to-all-start.1 = ((bf16[64,8,128]{2,1,0:T(8,128)(2,1)}), bf16[64,8,128]{2,1,0:T(8,128)(2,1)S(1)}, u32[]{:S(2)}, u32[]{:S(2)}) async-start(bf16[64,8,128]{2,1,0:T(8,128)(2,1)} %bitcast.9), calls=%async_computation.1 | async-start | bytes 262144 | tf_op jit(solution)/shard_map/all_to_all | solution.py:394
  46.6 21.6 %collective-permute-start.3 = (bf16[80,1280]{1,0:T(8,128)(2,1)S(1)}, bf16[80,1280]{1,0:T(8,128)(2,1)S(1)}, u32[]{:S(2)}, u32[]{:S(2)}) collective-permute-start(bf16[80,1280]{1,0:T(8,128)(2,1)S(1)} %get-tuple-element.23.b0_ref.refs_4_), channel_id=1, source_target_pairs={{0,128},{128,0},{1,129},{129,1},{2,130},{130,2},{3,131},{131,3},{4... | collective-permute-start | bytes 614408 | tf_op jit(solution)/shard_map/ppermute | solution.py:379
  48.4 20.4 %collective-permute-start.6 = (bf16[80,1792]{1,0:T(8,128)(2,1)S(1)}, bf16[80,1792]{1,0:T(8,128)(2,1)S(1)}, u32[]{:S(2)}, u32[]{:S(2)}) collective-permute-start(bf16[80,1792]{1,0:T(8,128)(2,1)S(1)} %shard_map.117.refs_0_), channel_id=1, source_target_pairs={{0,128},{128,0},{1,129},{129,1},{2,130},{130,2},{3,131},{131,3},{4... | collective-permute-start | bytes 860168 | tf_op jit(solution)/shard_map/ppermute | solution.py:379
  55.3 1.6 %copy-start.2 = (bf16[8,128,1024]{2,1,0:T(8,128)(2,1)S(1)}, bf16[8,128,1024]{2,1,0:T(8,128)(2,1)}, u32[]{:S(2)}) copy-start(bf16[8,128,1024]{2,1,0:T(8,128)(2,1)} %param.11) | copy-start | bytes 6291460
  56.9 1.6 %copy-start.3 = (bf16[8,128,1024]{2,1,0:T(8,128)(2,1)S(1)}, bf16[8,128,1024]{2,1,0:T(8,128)(2,1)}, u32[]{:S(2)}) copy-start(bf16[8,128,1024]{2,1,0:T(8,128)(2,1)} %param.12) | copy-start | bytes 6291460
  58.5 9.8 %copy-start.4 = (s32[8]{0:T(128)S(1)}, s32[8]{0:T(128)}, u32[]{:S(2)}) copy-start(s32[8]{0:T(128)} %param.15) | copy-start | bytes 100
  59.8 15.1 %all-to-all-start.2 = ((bf16[64,8,128]{2,1,0:T(8,128)(2,1)}), bf16[64,8,128]{2,1,0:T(8,128)(2,1)S(1)}, u32[]{:S(2)}, u32[]{:S(2)}) async-start(bf16[64,8,128]{2,1,0:T(8,128)(2,1)} %bitcast.13), calls=%async_computation.2 | async-start | bytes 262144 | tf_op jit(solution)/shard_map/all_to_all | solution.py:394
  64.9 4.3 %collective-permute-start.2 = (bf16[80,1280]{1,0:T(8,128)(2,1)S(1)}, bf16[80,1280]{1,0:T(8,128)(2,1)S(1)}, u32[]{:S(2)}, u32[]{:S(2)}) collective-permute-start(bf16[80,1280]{1,0:T(8,128)(2,1)S(1)} %get-tuple-element.23.b0_ref.refs_4_), channel_id=1, source_target_pairs={{0,64},{64,0},{1,65},{65,1},{2,66},{66,2},{3,67},{67,3},{4,68},{68... | collective-permute-start | bytes 614408 | tf_op jit(solution)/shard_map/ppermute | solution.py:380
  68.2 1.5 %collective-permute-start.4 = (bf16[80,1280]{1,0:T(8,128)(2,1)S(1)}, bf16[80,1280]{1,0:T(8,128)(2,1)S(1)}, u32[]{:S(2)}, u32[]{:S(2)}) collective-permute-start(bf16[80,1280]{1,0:T(8,128)(2,1)S(1)} %collective-permute-done.3.b2_ref.refs_6_), channel_id=1, source_target_pairs={{0,64},{64,0},{1,65},{65,1},{2,66},{66,2},{3,67},{67,3},{4,68},{68... | collective-permute-start | bytes 614408 | tf_op jit(solution)/shard_map/ppermute | solution.py:380
  68.4 14.2 %collective-permute-start.5 = (bf16[80,1792]{1,0:T(8,128)(2,1)S(1)}, bf16[80,1792]{1,0:T(8,128)(2,1)S(1)}, u32[]{:S(2)}, u32[]{:S(2)}) collective-permute-start(bf16[80,1792]{1,0:T(8,128)(2,1)S(1)} %shard_map.117.refs_0_), channel_id=1, source_target_pairs={{0,64},{64,0},{1,65},{65,1},{2,66},{66,2},{3,67},{67,3},{4,68},{68... | collective-permute-start | bytes 860168 | tf_op jit(solution)/shard_map/ppermute | solution.py:380
  68.8 13.8 %collective-permute-start.7 = (bf16[80,1792]{1,0:T(8,128)(2,1)S(1)}, bf16[80,1792]{1,0:T(8,128)(2,1)S(1)}, u32[]{:S(2)}, u32[]{:S(2)}) collective-permute-start(bf16[80,1792]{1,0:T(8,128)(2,1)S(1)} %collective-permute-done.6.refs_2_), channel_id=1, source_target_pairs={{0,64},{64,0},{1,65},{65,1},{2,66},{66,2},{3,67},{67,3},{4,68},{68... | collective-permute-start | bytes 860168 | tf_op jit(solution)/shard_map/ppermute | solution.py:380
  76.4 15.8 %all-to-all-start.3 = ((bf16[64,8,128]{2,1,0:T(8,128)(2,1)}), bf16[64,8,128]{2,1,0:T(8,128)(2,1)S(1)}, u32[]{:S(2)}, u32[]{:S(2)}) async-start(bf16[64,8,128]{2,1,0:T(8,128)(2,1)} %bitcast.15), calls=%async_computation.3 | async-start | bytes 262144 | tf_op jit(solution)/shard_map/all_to_all | solution.py:394
  92.9 7.2 %collective-permute-start.10 = (f32[2,80]{1,0:T(2,128)S(1)}, f32[2,80]{1,0:T(2,128)S(1)}, u32[]{:S(2)}, u32[]{:S(2)}) collective-permute-start(f32[2,80]{1,0:T(2,128)S(1)} %get-tuple-element.28), channel_id=1, source_target_pairs={{0,64},{64,0},{1,65},{65,1},{2,66},{66,2},{3,67},{67,3},{4,68},{68... | collective-permute-start | bytes 1928 | tf_op jit(solution)/shard_map/ppermute | solution.py:484
  97.2 4.5 %collective-permute-start.8 = (f32[2,80]{1,0:T(2,128)S(1)}, f32[2,80]{1,0:T(2,128)S(1)}, u32[]{:S(2)}, u32[]{:S(2)}) collective-permute-start(f32[2,80]{1,0:T(2,128)S(1)} %get-tuple-element.26), channel_id=1, source_target_pairs={{0,192},{64,128},{128,64},{192,0},{1,193},{65,129},{129,65},{193,1... | collective-permute-start | bytes 1928 | tf_op jit(solution)/shard_map/ppermute | solution.py:486
  98.8 3.9 %collective-permute-start.9 = (f32[2,80]{1,0:T(2,128)S(1)}, f32[2,80]{1,0:T(2,128)S(1)}, u32[]{:S(2)}, u32[]{:S(2)}) collective-permute-start(f32[2,80]{1,0:T(2,128)S(1)} %get-tuple-element.27), channel_id=1, source_target_pairs={{0,128},{128,0},{1,129},{129,1},{2,130},{130,2},{3,131},{131,3},{4... | collective-permute-start | bytes 1928 | tf_op jit(solution)/shard_map/ppermute | solution.py:485

commit v4 on v3

--- a/solution.py
+++ b/solution.py
@@ -26,6 +26,7 @@
 QW = N_DEV * WQ
 OW = N_DEV * WO
 GROUP = ROWS * SHARE
+WIDE = 48
 POS = 128
 NEG = -1e30
 
@@ -78,6 +79,10 @@
         both = ref[row : row + 16, :].astype(F32)
         parts += [both[0:8], both[8:16]]
     return parts
+
+
+def pick(x, lanes):
+    return jnp.take_along_axis(x, lanes, axis=1)
 
 
 def swapped_blocks(blocks, group):
@@ -101,11 +106,15 @@
 def pack_kernel(
     dev_ref, hidden_hbm, wq_hbm, wo_hbm, out_ref, hidden_ref, wq_ref, wo_ref, rows_ref, spare_ref, sems
 ):
-    copies = [
-        pltpu.make_async_copy(hidden_hbm, hidden_ref, sems.at[0]),
-        pltpu.make_async_copy(wq_hbm, wq_ref, sems.at[1]),
-        pltpu.make_async_copy(wo_hbm, wo_ref, sems.at[2]),
-    ]
+    copies = [pltpu.make_async_copy(hidden_hbm, hidden_ref, sems.at[0])]
+    for h in range(2):
+        half = pl.ds(h * D // 2, D // 2)
+        for i, (source, target) in enumerate(((wq_hbm, wq_ref), (wo_hbm, wo_ref))):
+            copies.append(
+                pltpu.make_async_copy(
+                    source.at[:, half], target.at[:, half], sems.at[1 + 2 * h + i]
+                )
+            )
     for copy in copies:
         copy.start()
     lane = lane_iota(MAIN)
@@ -114,19 +123,22 @@
         [hidden_ref[...].astype(F32), jnp.zeros((ROWS, LANES - FEAT), F32)], axis=1
     )
     hidden = pltpu.roll(hidden, shift_of(dev_ref[0], FEAT), 1)
-    copies[1].wait()
-    rows_ref[0:WQ, :] = wq_ref[...].astype(F32)
-    copies[2].wait()
-    rows_ref[WQ:FULL, :] = wo_ref[...].astype(F32)
-    for t in range(D // LANES):
-        columns = slice(t * LANES, (t + 1) * LANES)
-        rest = rows_ref[MAIN:FULL, columns]
-        spare_ref[0:16, columns] = pltpu.roll(rest, FEAT, 1)
-        spare_ref[16:32, columns] = pltpu.roll(rest, 2 * FEAT - LANES, 1)
     half = lane[0:16]
     from_spare = jnp.concatenate([turned(half, FEAT), turned(half, 2 * FEAT - LANES)], axis=0)
     pair = []
     for dest in range(N_DEV):
+        if dest % (N_DEV // 2) == 0:
+            h = dest // (N_DEV // 2)
+            columns = slice(h * D // 2, (h + 1) * D // 2)
+            copies[1 + 2 * h].wait()
+            rows_ref[0:WQ, columns] = wq_ref[:, columns].astype(F32)
+            copies[2 + 2 * h].wait()
+            rows_ref[WQ:FULL, columns] = wo_ref[:, columns].astype(F32)
+            for t in range(h * D // 2 // LANES, (h + 1) * D // 2 // LANES):
+                columns = slice(t * LANES, (t + 1) * LANES)
+                rest = rows_ref[MAIN:FULL, columns]
+                spare_ref[0:16, columns] = pltpu.roll(rest, FEAT, 1)
+                spare_ref[16:32, columns] = pltpu.roll(rest, 2 * FEAT - LANES, 1)
         at, off = divmod(dest * FEAT, LANES)
         main = {t: rows_ref[0:MAIN, t * LANES : (t + 1) * LANES] for t in (at, at + 1) if t < D // LANES}
         spare = {t: spare_ref[:, t * LANES : (t + 1) * LANES] for t in (at, at + 1) if t < D // LANES}
@@ -143,18 +155,15 @@
             pair = []
 
 
-def project_kernel(
-    dev_ref, group_ref, recv_ref, own_hbm, w2_ref, both_ref, out_ref, w_ref, own_ref, sem
-):
-    own = pltpu.make_async_copy(own_hbm, own_ref, sem)
-    own.start()
+def merge_kernel(own_ref, far_ref, both_ref, out_ref):
+    for j, ref in enumerate((own_ref, both_ref.at[0], far_ref, both_ref.at[1])):
+        out_ref[32 * j + 16 : 32 * j + 32, :] = jnp.zeros((16, D), BF16)
+        out_ref[32 * j : 32 * j + WQ, :] = ref[...]
+
+
+def project_kernel(dev_ref, group_ref, recv_ref, w_ref, out_ref):
     lane = lane_iota(ROWS)
     dev, group = dev_ref[0], group_ref[0]
-    for j, ref in enumerate((own_ref, both_ref.at[0], w2_ref, both_ref.at[1])):
-        if j == 0:
-            continue
-        w_ref[32 * j + 16 : 32 * j + 32, :] = jnp.zeros((16, D), BF16)
-        w_ref[32 * j : 32 * j + WQ, :] = ref[...]
     sources = []
     for source in range(N_DEV):
         row = source * PIECE - source * PIECE % 16
@@ -162,9 +171,6 @@
         sources.append(both[8:16] if source % 2 else both[0:8])
     tiles = lay(D // LANES, sources, FEAT, lane)
     hidden = jnp.concatenate([t.astype(BF16) for t in tiles], axis=1)
-    own.wait()
-    w_ref[16:32, :] = jnp.zeros((16, D), BF16)
-    w_ref[0:WQ, :] = own_ref[...]
     y = lax.dot_general(hidden, w_ref[...], (((1,), (1,)), ((), ())), preferred_element_type=F32)
     up, down = pltpu.roll(y, 32, 1), pltpu.roll(y, LANES - 32, 1)
     y = jnp.where((group & 1) == 1, jnp.where((lane & 32) == 0, down, up), y)
@@ -211,7 +217,9 @@
     out_ref[...] = turn(dev_ref[0], rows_ref[...])
 
 
-def score_kernel(dev_ref, lengths_ref, recv_ref, keys_ref, w_ref, own_ref, tag_ref, fresh_ref):
+def score_kernel(
+    dev_ref, lengths_ref, recv_ref, keys_ref, spread_ref, own_ref, tag_ref, fresh_ref
+):
     lane = lane_iota(ROWS)
     sub = lax.broadcasted_iota(jnp.int32, (ROWS, LANES), 0)
     dev = dev_ref[0]
@@ -252,7 +260,14 @@
         own_w = jnp.where(first, jnp.exp(own - top), 0.0)
         total = jnp.sum(w, axis=1, keepdims=True) + own_w
         rows = slice(k * GROUP, (k + 1) * GROUP)
-        w_ref[rows, :] = w
+        for r in range(ROWS):
+            spread_ref[k * WIDE : k * WIDE + GROUP, r * LANES : (r + 1) * LANES] = jnp.concatenate(
+                [
+                    jnp.where(own_rows[r], w[i * ROWS : (i + 1) * ROWS], 0.0)
+                    for i in range(SHARE)
+                ],
+                axis=0,
+            ).astype(BF16)
         own_ref[rows, :] = jnp.broadcast_to(own_w, (GROUP, LANES))
         t = jnp.broadcast_to(top, (GROUP, LANES))
         t0 = t.astype(BF16).astype(F32)
@@ -264,23 +279,15 @@
         fresh_ref[k * ROWS : (k + 1) * ROWS, :] = tiles[HEADS + KV_HEADS + k]
 
 
-def value_kernel(w_ref, own_ref, tag_ref, fresh_ref, values_ref, out_ref):
+def value_kernel(spread_ref, own_ref, tag_ref, fresh_ref, values_ref, out_ref):
     lane = lane_iota(ROWS)
-    sub = lax.broadcasted_iota(jnp.int32, (ROWS, LANES), 0)
-    own_rows = [sub == r for r in range(ROWS)]
     outs, tags = [], []
     for k in range(KV_HEADS):
         heads = [slice(k * GROUP + i * ROWS, k * GROUP + (i + 1) * ROWS) for i in range(SHARE)]
-        spread = []
-        for r in range(ROWS):
-            spread.append(
-                jnp.concatenate(
-                    [jnp.where(own_rows[r], w_ref[h, :], 0.0) for h in heads], axis=0
-                ).astype(BF16)
-            )
-        spread = jnp.concatenate(spread, axis=1)
         values = values_ref[:, k * LANES : (k + 1) * LANES]
-        out = jnp.dot(spread, values, preferred_element_type=F32)
+        out = jnp.dot(
+            spread_ref[k * WIDE : (k + 1) * WIDE, :], values, preferred_element_type=F32
+        )
         fresh = fresh_ref[k * ROWS : (k + 1) * ROWS, :]
         for i, h in enumerate(heads):
             outs.append(out[i * ROWS : (i + 1) * ROWS] + own_ref[h, :] * fresh)
@@ -305,23 +312,22 @@
     start = dev * FEAT
     split = ((start + FEAT - 1) // LANES) * LANES - start
     split = jnp.where(split <= 0, FEAT, split)
-    left = (lane < split) | ((lane >= FEAT) & (lane < FEAT + 8))
     shift = shift_of(dev, FEAT)
-    parts = [turned_back(x, shift) for x in halves(recv_ref)]
-    terms = [(x + pltpu.roll(x, LANES - 1, 1)) + pltpu.roll(x, LANES - 2, 1) for x in parts]
-    tops = terms
-    while len(tops) > 1:
-        tops = [jnp.maximum(a, b) for a, b in zip(tops[0::2], tops[1::2])]
-    top = tops[0]
+    spot = (lane - shift) & (LANES - 1)
+    left = (spot < split) | ((spot >= FEAT) & (spot < FEAT + 8))
+    tag = jnp.where(left, FEAT, FEAT + 8) + shift
+    at = [(tag + i) & (LANES - 1) for i in range(5)]
+    parts = halves(recv_ref)
+    tops = [(pick(x, at[0]) + pick(x, at[1])) + pick(x, at[2]) for x in parts]
+    top = tops
+    while len(top) > 1:
+        top = [jnp.maximum(a, b) for a, b in zip(top[0::2], top[1::2])]
     total = [jnp.zeros((ROWS, LANES), F32) for _ in range(4)]
     for s, part in enumerate(parts):
-        e = jnp.exp(terms[s] - top)
-        f = jnp.where(left, e[:, FEAT : FEAT + 1], e[:, FEAT + 8 : FEAT + 9])
-        total[s % 4] = total[s % 4] + f * part
+        total[s % 4] = total[s % 4] + jnp.exp(tops[s] - top[0]) * part
     total = (total[0] + total[1]) + (total[2] + total[3])
-    den = total + pltpu.roll(total, LANES - 1, 1)
-    den = jnp.where(left, den[:, FEAT + 3 : FEAT + 4], den[:, FEAT + 11 : FEAT + 12])
-    attn = (total / den)[:, 0:FEAT].astype(BF16)
+    den = pick(total, at[3]) + pick(total, at[4])
+    attn = turned_back(total / den, shift)[:, 0:FEAT].astype(BF16)
     blocks = [
         jnp.dot(attn, ref[...], preferred_element_type=F32)
         for ref in (b0_ref, b1_ref, b2_ref, b3_ref)
@@ -415,21 +421,13 @@
             pltpu.VMEM((WO, D), BF16),
             pltpu.VMEM((FULL, D), F32),
             pltpu.VMEM((MAIN, D), F32),
-            pltpu.SemaphoreType.DMA((3,)),
+            pltpu.SemaphoreType.DMA((5,)),
         ],
         vmem=60,
     )(dev, hidden_in, wq, wo)
     recv = exchange(sent)
-    sent = call(
-        project_kernel,
-        part,
-        [SMEM, SMEM, VMEM, ANY] + [VMEM] * 2,
-        [
-            pltpu.VMEM((LANES, D), BF16),
-            pltpu.VMEM((WQ, D), BF16),
-            pltpu.SemaphoreType.DMA,
-        ],
-    )(dev, group_one, recv, wq, far, both)
+    merged = call(merge_kernel, struct((LANES, D), BF16), [VMEM] * 3)(wq, far, both)
+    sent = call(project_kernel, part, [SMEM, SMEM, VMEM, VMEM])(dev, group_one, recv, merged)
     got = exchange(sent)
 
     o_block, lengths = call(
@@ -451,7 +449,8 @@
     tall = struct((KV_HEADS * GROUP, LANES), F32)
     scored = call(
         score_kernel,
-        [tall] * 3 + [struct((KV_HEADS * ROWS, LANES), F32)],
+        [struct((KV_HEADS * WIDE, ROWS * POS), BF16), tall, tall]
+        + [struct((KV_HEADS * ROWS, LANES), F32)],
         [SMEM] + [VMEM] * 3,
         flops=10**10,
     )(dev, lengths, got, key_cache.reshape(cache))

time: 104 us -> 103 us (level)
    pallas_call x2 -> x3, Pallas kernels: 2.57 us -> 2.49 us  [the longest x1 1.32 us: shards(): call(project_kernel, part, [SMEM, SMEM, VMEM, VMEM])]
where the time goes in v4:
time: 103 us
  starting transfers between devices  48.4 us (47%)
  waiting for transfers between devices  39.2 us (38%)
  Pallas kernels  10.6 us (10%)
  local copies, waits for them, and re-layouts  2.94 us (3%)
  other arithmetic  1.03 us (1%)
    all_to_all x4, waiting for transfers between devices, exchange(): x = lax.all_to_all(x, D_AXES, split_axis=0, concat_axis=0, tiled=True)  34.2 us
    all_to_all x4, starting transfers between devices, exchange(): x = lax.all_to_all(x, D_AXES, split_axis=0, concat_axis=0, tiled=True)  29.2 us
    ppermute x1, starting transfers between devices, shards(): r1 = lax.ppermute(r1, 'core', SWAP)  4.37 us
    ppermute x4, starting transfers between devices, to_groups(): return (lax.ppermute(x, 'core', SWAP), far, lax.ppermute(far, 'core', SWAP))  3.89 us
    ppermute x1, starting transfers between devices, shards(): far = lax.ppermute(wq, 'xh', SWAP)  3.66 us
    ppermute x2, starting transfers between devices, to_groups(): far = lax.ppermute(x, 'xh', SWAP)  3.06 us
    pallas_call x1, Pallas kernels, shards(): call(pack_kernel, struct((N_DEV * PIECE, LANES), BF16), [SMEM] + [ANY] *...  2.15 us
    unnamed x12, local copies, waits for them, and re-layouts  2.14 us
  transfers between devices with their start and end apart: 15, of which 9 were waited for; matrix products, arithmetic and copies ran while one was open for 1% of the time, Pallas kernels for 8%

profile of v4, /device:TPU:1, one launch (start us, length us, event | category | flops | bytes accessed | tf_op | source)
XLA Modules:
  0.0 103.0 jit_solution(895805503524234724)
XLA Ops:
  0.6 3.7 %collective-permute-start = (bf16[28,5120]{1,0:T(8,128)(2,1)}, bf16[28,5120]{1,0:T(8,128)(2,1)S(1)}, u32[]{:S(2)}, u32[]{:S(2)}) collective-permute-start(bf16[28,5120]{1,0:T(8,128)(2,1)} %bitcast.21), channel_id=1, source_target_pairs={{0,128},{128,0},{1,129},{129,1},{2,130},{130,2},{3,131},{131,3},{4... | collective-permute-start | bytes 860168 | tf_op jit(solution)/shard_map/ppermute | solution.py:411
  4.3 2.1 %shard_map.111 = bf16[2560,128]{1,0:T(8,128)(2,1)} custom-call(s32[1]{0:T(128)} %bitcast.dev_ref, bf16[8,80]{1,0:T(8,128)(2,1)} %hidden_hbm.1, bf16[28,5120]{1,0:T(8,128)(2,1)} %bitcast.22, bf16[20,5120]{1,0:T(8,128)(2,1)} %bitcast.32), custom_call_target="tpu_custom_call" | custom-call | tf_op jit(solution)/shard_map/pallas_call | solution.py:414
  6.5 11.9 %all-to-all-start = ((bf16[64,40,128]{2,1,0:T(8,128)(2,1)}), bf16[64,40,128]{2,1,0:T(8,128)(2,1)S(1)}, u32[]{:S(2)}, u32[]{:S(2)}) async-start(bf16[64,40,128]{2,1,0:T(8,128)(2,1)} %bitcast.31), calls=%async_computation | async-start | bytes 1310720 | tf_op jit(solution)/shard_map/all_to_all | solution.py:400
  19.0 1.3 %collective-permute-start.1 = (bf16[2,28,5120]{2,0,1:T(2,128)(2,1)S(1)}, bf16[2,28,5120]{2,0,1:T(2,128)(2,1)S(1)}, u32[]{:S(2)}, u32[]{:S(2)}) collective-permute-start(bf16[2,28,5120]{2,0,1:T(2,128)(2,1)S(1)} %copy.12), channel_id=1, source_target_pairs={{0,64},{64,0},{1,65},{65,1},{2,66},{66,2},{3,67},{67,3},{4,68},{68... | collective-permute-start | bytes 1720328 | tf_op jit(solution)/shard_map/ppermute | solution.py:412
  20.4 1.6 %collective-permute-done.1 = bf16[2,28,5120]{2,0,1:T(2,128)(2,1)S(1)} collective-permute-done((bf16[2,28,5120]{2,0,1:T(2,128)(2,1)S(1)}, bf16[2,28,5120]{2,0,1:T(2,128)(2,1)S(1)}, u32[]{:S(2)}, u32[]{:S(2)}) %collective-permute-start.1) | collective-permute-done | bytes 573472 | tf_op jit(solution)/shard_map/ppermute | solution.py:412
  22.2 15.0 %all-to-all-done = bf16[64,40,128]{2,1,0:T(8,128)(2,1)S(1)} async-done(((bf16[64,40,128]{2,1,0:T(8,128)(2,1)}), bf16[64,40,128]{2,1,0:T(8,128)(2,1)S(1)}, u32[]{:S(2)}, u32[]{:S(2)}) %all-to-all-start) | async-done | bytes 655392 | tf_op jit(solution)/shard_map/all_to_all | solution.py:400
  37.2 1.3 %shard_map.113.after_ref = bf16[512,128]{1,0:T(8,128)(2,1)} custom-call(s32[1]{0:T(128)} %bitcast.dev_ref, s32[1]{0:T(128)} %bitcast.2.group_ref, bf16[2560,128]{1,0:T(8,128)(2,1)S(1)} %bitcast.18, bf16[128,5120]{1,0:T(8,128)(2,1)S(1)} %shard_map.112.w_ref), custom_call_target="tpu_custom_call" | custom-call | tf_op jit(solution)/shard_map/pallas_call | solution.py:430
  38.5 6.6 %all-to-all-start.1 = ((bf16[64,8,128]{2,1,0:T(8,128)(2,1)}), bf16[64,8,128]{2,1,0:T(8,128)(2,1)S(1)}, u32[]{:S(2)}, u32[]{:S(2)}) async-start(bf16[64,8,128]{2,1,0:T(8,128)(2,1)} %bitcast.9), calls=%async_computation.1 | async-start | bytes 262144 | tf_op jit(solution)/shard_map/all_to_all | solution.py:400
  46.4 1.8 %collective-permute-start.3 = (bf16[80,1280]{1,0:T(8,128)(2,1)S(1)}, bf16[80,1280]{1,0:T(8,128)(2,1)S(1)}, u32[]{:S(2)}, u32[]{:S(2)}) collective-permute-start(bf16[80,1280]{1,0:T(8,128)(2,1)S(1)} %get-tuple-element.23.b0_ref.refs_4_), channel_id=1, source_target_pairs={{0,128},{128,0},{1,129},{129,1},{2,130},{130,2},{3,131},{131,3},{4... | collective-permute-start | bytes 614408 | tf_op jit(solution)/shard_map/ppermute | solution.py:385
  48.2 1.2 %collective-permute-start.6 = (bf16[80,1792]{1,0:T(8,128)(2,1)S(1)}, bf16[80,1792]{1,0:T(8,128)(2,1)S(1)}, u32[]{:S(2)}, u32[]{:S(2)}) collective-permute-start(bf16[80,1792]{1,0:T(8,128)(2,1)S(1)} %shard_map.118.refs_0_), channel_id=1, source_target_pairs={{0,128},{128,0},{1,129},{129,1},{2,130},{130,2},{3,131},{131,3},{4... | collective-permute-start | bytes 860168 | tf_op jit(solution)/shard_map/ppermute | solution.py:385
  49.4 5.7 %all-to-all-done.1 = bf16[64,8,128]{2,1,0:T(8,128)(2,1)S(1)} async-done(((bf16[64,8,128]{2,1,0:T(8,128)(2,1)}), bf16[64,8,128]{2,1,0:T(8,128)(2,1)S(1)}, u32[]{:S(2)}, u32[]{:S(2)}) %all-to-all-start.1) | async-done | bytes 131104 | tf_op jit(solution)/shard_map/all_to_all | solution.py:400
  55.1 1.6 %copy-done.2 = bf16[8,128,1024]{2,1,0:T(8,128)(2,1)S(1)} copy-done((bf16[8,128,1024]{2,1,0:T(8,128)(2,1)S(1)}, bf16[8,128,1024]{2,1,0:T(8,128)(2,1)}, u32[]{:S(2)}) %copy-start.2) | copy-done | bytes 2097176
  58.3 1.3 %shard_map.116 = bf16[512,128]{1,0:T(8,128)(2,1)} custom-call(bf16[384,1024]{1,0:T(8,128)(2,1)S(1)} %get-tuple-element.19.spread_ref, f32[320,128]{1,0:T(8,128)S(1)} %get-tuple-element.20.own_ref, f32[320,128]{1,0:T(8,128)S(1)} %get-tuple-element.21.tag_ref, f32[64,128]{1,0:T(8,128)S(1)} %get-tuple-element.22.fresh_ref, bf16[1024,1024]{1,0:T(8,128)(2,1)S(1)} %bitcast.30), custom_call_target="tpu_custom_call" | custom-call | flops 10000000000 | bytes 4194304 | tf_op jit(solution)/shard_map/pallas_call | solution.py:457
  59.6 5.1 %all-to-all-start.2 = ((bf16[64,8,128]{2,1,0:T(8,128)(2,1)}), bf16[64,8,128]{2,1,0:T(8,128)(2,1)S(1)}, u32[]{:S(2)}, u32[]{:S(2)}) async-start(bf16[64,8,128]{2,1,0:T(8,128)(2,1)} %bitcast.13), calls=%async_computation.2 | async-start | bytes 262144 | tf_op jit(solution)/shard_map/all_to_all | solution.py:400
  64.7 3.3 %collective-permute-start.2 = (bf16[80,1280]{1,0:T(8,128)(2,1)S(1)}, bf16[80,1280]{1,0:T(8,128)(2,1)S(1)}, u32[]{:S(2)}, u32[]{:S(2)}) collective-permute-start(bf16[80,1280]{1,0:T(8,128)(2,1)S(1)} %get-tuple-element.23.b0_ref.refs_4_), channel_id=1, source_target_pairs={{0,64},{64,0},{1,65},{65,1},{2,66},{66,2},{3,67},{67,3},{4,68},{68... | collective-permute-start | bytes 614408 | tf_op jit(solution)/shard_map/ppermute | solution.py:386
  69.4 5.4 %all-to-all-done.2 = bf16[64,8,128]{2,1,0:T(8,128)(2,1)S(1)} async-done(((bf16[64,8,128]{2,1,0:T(8,128)(2,1)}), bf16[64,8,128]{2,1,0:T(8,128)(2,1)S(1)}, u32[]{:S(2)}, u32[]{:S(2)}) %all-to-all-start.2) | async-done | bytes 131104 | tf_op jit(solution)/shard_map/all_to_all | solution.py:400
  74.8 1.3 %shard_map.117.after_ref = bf16[512,128]{1,0:T(8,128)(2,1)} custom-call(s32[1]{0:T(128)} %bitcast.dev_ref, s32[1]{0:T(128)} %bitcast.2.group_ref, bf16[512,128]{1,0:T(8,128)(2,1)S(1)} %bitcast.26, bf16[80,1280]{1,0:T(8,128)(2,1)S(1)} %get-tuple-element.23.b0_ref.refs_4_, bf16[80,1280]{1,0:T(8,128)(2,1)S(1)} %collective-permute-done.2.b1_ref.refs_5_, ...), custom_call_target="tpu_custom_call" | custom-call | tf_op jit(solution)/shard_map/pallas_call | solution.py:459
  76.1 5.7 %all-to-all-start.3 = ((bf16[64,8,128]{2,1,0:T(8,128)(2,1)}), bf16[64,8,128]{2,1,0:T(8,128)(2,1)S(1)}, u32[]{:S(2)}, u32[]{:S(2)}) async-start(bf16[64,8,128]{2,1,0:T(8,128)(2,1)} %bitcast.15), calls=%async_computation.3 | async-start | bytes 262144 | tf_op jit(solution)/shard_map/all_to_all | solution.py:400
  82.2 1.4 %shard_map.119 = (bf16[80,7168]{1,0:T(8,128)(2,1)}, bf16[80,5120]{1,0:T(8,128)(2,1)}, f32[8,128]{1,0:T(8,128)S(1)}) custom-call(s32[1]{0:T(128)} %bitcast.2.group_ref, bf16[512,128]{1,0:T(8,128)(2,1)} %shard_map.117.after_ref, bf16[80,1792]{1,0:T(8,128)(2,1)S(1)} %shard_map.118.refs_0_, bf16[80,1792]{1,0:T(8,128)(2,1)S(1)} %collective-permute-done.5.refs_1_, ...), custom_call_target="tpu_custom_call" | custom-call | tf_op jit(solution)/shard_map/pallas_call | solution.py:462
  83.6 8.2 %all-to-all-done.3 = bf16[64,8,128]{2,1,0:T(8,128)(2,1)S(1)} async-done(((bf16[64,8,128]{2,1,0:T(8,128)(2,1)}), bf16[64,8,128]{2,1,0:T(8,128)(2,1)S(1)}, u32[]{:S(2)}, u32[]{:S(2)}) %all-to-all-start.3) | async-done | bytes 131104 | tf_op jit(solution)/shard_map/all_to_all | solution.py:400
  92.4 4.4 %collective-permute-start.10 = (f32[2,80]{1,0:T(2,128)S(1)}, f32[2,80]{1,0:T(2,128)S(1)}, u32[]{:S(2)}, u32[]{:S(2)}) collective-permute-start(f32[2,80]{1,0:T(2,128)S(1)} %get-tuple-element.28), channel_id=1, source_target_pairs={{0,64},{64,0},{1,65},{65,1},{2,66},{66,2},{3,67},{67,3},{4,68},{68... | collective-permute-start | bytes 1928 | tf_op jit(solution)/shard_map/ppermute | solution.py:483
  96.8 1.6 %collective-permute-start.8 = (f32[2,80]{1,0:T(2,128)S(1)}, f32[2,80]{1,0:T(2,128)S(1)}, u32[]{:S(2)}, u32[]{:S(2)}) collective-permute-start(f32[2,80]{1,0:T(2,128)S(1)} %get-tuple-element.26), channel_id=1, source_target_pairs={{0,192},{64,128},{128,64},{192,0},{1,193},{65,129},{129,65},{193,1... | collective-permute-start | bytes 1928 | tf_op jit(solution)/shard_map/ppermute | solution.py:485
  98.4 1.2 %collective-permute-start.9 = (f32[2,80]{1,0:T(2,128)S(1)}, f32[2,80]{1,0:T(2,128)S(1)}, u32[]{:S(2)}, u32[]{:S(2)}) collective-permute-start(f32[2,80]{1,0:T(2,128)S(1)} %get-tuple-element.27), channel_id=1, source_target_pairs={{0,128},{128,0},{1,129},{129,1},{2,130},{130,2},{3,131},{131,3},{4... | collective-permute-start | bytes 1928 | tf_op jit(solution)/shard_map/ppermute | solution.py:484
  99.7 1.6 %collective-permute-done.8 = f32[2,80]{1,0:T(2,128)S(1)} collective-permute-done((f32[2,80]{1,0:T(2,128)S(1)}, f32[2,80]{1,0:T(2,128)S(1)}, u32[]{:S(2)}, u32[]{:S(2)}) %collective-permute-start.8) | collective-permute-done | bytes 672 | tf_op jit(solution)/shard_map/ppermute | solution.py:485
  (44 shorter events, 7.9 us)
Async XLA Ops:
  0.6 17.7 %copy-start = (bf16[5120,28]{0,1:T(8,128)(2,1)S(1)}, bf16[5120,28]{0,1:T(8,128)(2,1)}, u32[]{:S(2)}) copy-start(bf16[5120,28]{0,1:T(8,128)(2,1)} %param.9) | copy-start | bytes 860164
  0.6 17.7 %collective-permute-start = (bf16[28,5120]{1,0:T(8,128)(2,1)}, bf16[28,5120]{1,0:T(8,128)(2,1)S(1)}, u32[]{:S(2)}, u32[]{:S(2)}) collective-permute-start(bf16[28,5120]{1,0:T(8,128)(2,1)} %bitcast.21), channel_id=1, source_target_pairs={{0,128},{128,0},{1,129},{129,1},{2,130},{130,2},{3,131},{131,3},{4... | collective-permute-start | bytes 860168 | tf_op jit(solution)/shard_map/ppermute | solution.py:411
  6.5 30.7 %all-to-all-start = ((bf16[64,40,128]{2,1,0:T(8,128)(2,1)}), bf16[64,40,128]{2,1,0:T(8,128)(2,1)S(1)}, u32[]{:S(2)}, u32[]{:S(2)}) async-start(bf16[64,40,128]{2,1,0:T(8,128)(2,1)} %bitcast.31), calls=%async_computation | async-start | bytes 1310720 | tf_op jit(solution)/shard_map/all_to_all | solution.py:400
  19.0 2.9 %collective-permute-start.1 = (bf16[2,28,5120]{2,0,1:T(2,128)(2,1)S(1)}, bf16[2,28,5120]{2,0,1:T(2,128)(2,1)S(1)}, u32[]{:S(2)}, u32[]{:S(2)}) collective-permute-start(bf16[2,28,5120]{2,0,1:T(2,128)(2,1)S(1)} %copy.12), channel_id=1, source_target_pairs={{0,64},{64,0},{1,65},{65,1},{2,66},{66,2},{3,67},{67,3},{4,68},{68... | collective-permute-start | bytes 1720328 | tf_op jit(solution)/shard_map/ppermute | solution.py:412
  22.1 23.0 %copy-start.5 = (s32[8]{0:T(128)S(1)}, s32[8]{0:T(128)}, u32[]{:S(2)}) copy-start(s32[8]{0:T(128)} %param.14) | copy-start | bytes 100
  22.2 23.2 %copy-start.1 = (s32[8]{0:T(128)S(1)}, s32[8]{0:T(128)}, u32[]{:S(2)}) copy-start(s32[8]{0:T(128)} %lengths_ref.1) | copy-start | bytes 100
  38.5 16.6 %all-to-all-start.1 = ((bf16[64,8,128]{2,1,0:T(8,128)(2,1)}), bf16[64,8,128]{2,1,0:T(8,128)(2,1)S(1)}, u32[]{:S(2)}, u32[]{:S(2)}) async-start(bf16[64,8,128]{2,1,0:T(8,128)(2,1)} %bitcast.9), calls=%async_computation.1 | async-start | bytes 262144 | tf_op jit(solution)/shard_map/all_to_all | solution.py:400
  46.4 21.6 %collective-permute-start.3 = (bf16[80,1280]{1,0:T(8,128)(2,1)S(1)}, bf16[80,1280]{1,0:T(8,128)(2,1)S(1)}, u32[]{:S(2)}, u32[]{:S(2)}) collective-permute-start(bf16[80,1280]{1,0:T(8,128)(2,1)S(1)} %get-tuple-element.23.b0_ref.refs_4_), channel_id=1, source_target_pairs={{0,128},{128,0},{1,129},{129,1},{2,130},{130,2},{3,131},{131,3},{4... | collective-permute-start | bytes 614408 | tf_op jit(solution)/shard_map/ppermute | solution.py:385
  48.2 20.4 %collective-permute-start.6 = (bf16[80,1792]{1,0:T(8,128)(2,1)S(1)}, bf16[80,1792]{1,0:T(8,128)(2,1)S(1)}, u32[]{:S(2)}, u32[]{:S(2)}) collective-permute-start(bf16[80,1792]{1,0:T(8,128)(2,1)S(1)} %shard_map.118.refs_0_), channel_id=1, source_target_pairs={{0,128},{128,0},{1,129},{129,1},{2,130},{130,2},{3,131},{131,3},{4... | collective-permute-start | bytes 860168 | tf_op jit(solution)/shard_map/ppermute | solution.py:385
  55.1 1.6 %copy-start.2 = (bf16[8,128,1024]{2,1,0:T(8,128)(2,1)S(1)}, bf16[8,128,1024]{2,1,0:T(8,128)(2,1)}, u32[]{:S(2)}) copy-start(bf16[8,128,1024]{2,1,0:T(8,128)(2,1)} %param.11) | copy-start | bytes 6291460
  56.7 1.6 %copy-start.3 = (bf16[8,128,1024]{2,1,0:T(8,128)(2,1)S(1)}, bf16[8,128,1024]{2,1,0:T(8,128)(2,1)}, u32[]{:S(2)}) copy-start(bf16[8,128,1024]{2,1,0:T(8,128)(2,1)} %param.12) | copy-start | bytes 6291460
  58.3 9.8 %copy-start.4 = (s32[8]{0:T(128)S(1)}, s32[8]{0:T(128)}, u32[]{:S(2)}) copy-start(s32[8]{0:T(128)} %param.15) | copy-start | bytes 100
  59.6 15.2 %all-to-all-start.2 = ((bf16[64,8,128]{2,1,0:T(8,128)(2,1)}), bf16[64,8,128]{2,1,0:T(8,128)(2,1)S(1)}, u32[]{:S(2)}, u32[]{:S(2)}) async-start(bf16[64,8,128]{2,1,0:T(8,128)(2,1)} %bitcast.13), calls=%async_computation.2 | async-start | bytes 262144 | tf_op jit(solution)/shard_map/all_to_all | solution.py:400
  64.7 4.3 %collective-permute-start.2 = (bf16[80,1280]{1,0:T(8,128)(2,1)S(1)}, bf16[80,1280]{1,0:T(8,128)(2,1)S(1)}, u32[]{:S(2)}, u32[]{:S(2)}) collective-permute-start(bf16[80,1280]{1,0:T(8,128)(2,1)S(1)} %get-tuple-element.23.b0_ref.refs_4_), channel_id=1, source_target_pairs={{0,64},{64,0},{1,65},{65,1},{2,66},{66,2},{3,67},{67,3},{4,68},{68... | collective-permute-start | bytes 614408 | tf_op jit(solution)/shard_map/ppermute | solution.py:386
  68.0 1.5 %collective-permute-start.4 = (bf16[80,1280]{1,0:T(8,128)(2,1)S(1)}, bf16[80,1280]{1,0:T(8,128)(2,1)S(1)}, u32[]{:S(2)}, u32[]{:S(2)}) collective-permute-start(bf16[80,1280]{1,0:T(8,128)(2,1)S(1)} %collective-permute-done.3.b2_ref.refs_6_), channel_id=1, source_target_pairs={{0,64},{64,0},{1,65},{65,1},{2,66},{66,2},{3,67},{67,3},{4,68},{68... | collective-permute-start | bytes 614408 | tf_op jit(solution)/shard_map/ppermute | solution.py:386
  68.2 14.0 %collective-permute-start.5 = (bf16[80,1792]{1,0:T(8,128)(2,1)S(1)}, bf16[80,1792]{1,0:T(8,128)(2,1)S(1)}, u32[]{:S(2)}, u32[]{:S(2)}) collective-permute-start(bf16[80,1792]{1,0:T(8,128)(2,1)S(1)} %shard_map.118.refs_0_), channel_id=1, source_target_pairs={{0,64},{64,0},{1,65},{65,1},{2,66},{66,2},{3,67},{67,3},{4,68},{68... | collective-permute-start | bytes 860168 | tf_op jit(solution)/shard_map/ppermute | solution.py:386
  68.6 13.6 %collective-permute-start.7 = (bf16[80,1792]{1,0:T(8,128)(2,1)S(1)}, bf16[80,1792]{1,0:T(8,128)(2,1)S(1)}, u32[]{:S(2)}, u32[]{:S(2)}) collective-permute-start(bf16[80,1792]{1,0:T(8,128)(2,1)S(1)} %collective-permute-done.6.refs_2_), channel_id=1, source_target_pairs={{0,64},{64,0},{1,65},{65,1},{2,66},{66,2},{3,67},{67,3},{4,68},{68... | collective-permute-start | bytes 860168 | tf_op jit(solution)/shard_map/ppermute | solution.py:386
  76.1 15.7 %all-to-all-start.3 = ((bf16[64,8,128]{2,1,0:T(8,128)(2,1)}), bf16[64,8,128]{2,1,0:T(8,128)(2,1)S(1)}, u32[]{:S(2)}, u32[]{:S(2)}) async-start(bf16[64,8,128]{2,1,0:T(8,128)(2,1)} %bitcast.15), calls=%async_computation.3 | async-start | bytes 262144 | tf_op jit(solution)/shard_map/all_to_all | solution.py:400
  92.4 7.2 %collective-permute-start.10 = (f32[2,80]{1,0:T(2,128)S(1)}, f32[2,80]{1,0:T(2,128)S(1)}, u32[]{:S(2)}, u32[]{:S(2)}) collective-permute-start(f32[2,80]{1,0:T(2,128)S(1)} %get-tuple-element.28), channel_id=1, source_target_pairs={{0,64},{64,0},{1,65},{65,1},{2,66},{66,2},{3,67},{67,3},{4,68},{68... | collective-permute-start | bytes 1928 | tf_op jit(solution)/shard_map/ppermute | solution.py:483
  96.8 4.5 %collective-permute-start.8 = (f32[2,80]{1,0:T(2,128)S(1)}, f32[2,80]{1,0:T(2,128)S(1)}, u32[]{:S(2)}, u32[]{:S(2)}) collective-permute-start(f32[2,80]{1,0:T(2,128)S(1)} %get-tuple-element.26), channel_id=1, source_target_pairs={{0,192},{64,128},{128,64},{192,0},{1,193},{65,129},{129,65},{193,1... | collective-permute-start | bytes 1928 | tf_op jit(solution)/shard_map/ppermute | solution.py:485
  98.4 3.9 %collective-permute-start.9 = (f32[2,80]{1,0:T(2,128)S(1)}, f32[2,80]{1,0:T(2,128)S(1)}, u32[]{:S(2)}, u32[]{:S(2)}) collective-permute-start(f32[2,80]{1,0:T(2,128)S(1)} %get-tuple-element.27), channel_id=1, source_target_pairs={{0,128},{128,0},{1,129},{129,1},{2,130},{130,2},{3,131},{131,3},{4... | collective-permute-start | bytes 1928 | tf_op jit(solution)/shard_map/ppermute | solution.py:484

commit v5 on v4

--- a/solution.py
+++ b/solution.py
@@ -217,18 +217,24 @@
     out_ref[...] = turn(dev_ref[0], rows_ref[...])
 
 
+def query_kernel(recv_ref, out_ref):
+    lane = lane_iota(ROWS)
+    sources = halves(recv_ref)
+    for g in range(N_GRP):
+        frame = lay(QW // LANES, sources, WQ, turned(lane, 32 * g))
+        for t, tile in enumerate(frame):
+            row = (g * len(frame) + t) * ROWS
+            out_ref[row : row + ROWS, :] = pltpu.roll(tile, LANES - 32 * g, 1) if g else tile
+
+
 def score_kernel(
-    dev_ref, lengths_ref, recv_ref, keys_ref, spread_ref, own_ref, tag_ref, fresh_ref
+    dev_ref, lengths_ref, tiles_ref, keys_ref, spread_ref, own_ref, tag_ref, fresh_ref
 ):
     lane = lane_iota(ROWS)
     sub = lax.broadcasted_iota(jnp.int32, (ROWS, LANES), 0)
     dev = dev_ref[0]
     scale = 1.0 / math.sqrt(LANES)
-    sources = halves(recv_ref)
-    tiles = []
-    for g in range(N_GRP):
-        frame = lay(QW // LANES, sources, WQ, turned(lane, 32 * g))
-        tiles += [pltpu.roll(t, LANES - 32 * g, 1) for t in frame] if g else frame
+    tiles = [tiles_ref[h * ROWS : (h + 1) * ROWS, :] for h in range(HEADS + 2 * KV_HEADS)]
     own_rows = [sub == r for r in range(ROWS)]
     valid = dev * POS + lane < lengths_ref[...]
     valid = jnp.concatenate([valid] * SHARE, axis=0)
@@ -447,13 +453,16 @@
     q_blocks = (q_block,) + to_groups(q_block)
     cache = (ROWS * POS, KV_HEADS * LANES)
     tall = struct((KV_HEADS * GROUP, LANES), F32)
+    tiles = call(
+        query_kernel, struct(((HEADS + 2 * KV_HEADS) * ROWS, LANES), F32), [VMEM], flops=10**10
+    )(got)
     scored = call(
         score_kernel,
         [struct((KV_HEADS * WIDE, ROWS * POS), BF16), tall, tall]
         + [struct((KV_HEADS * ROWS, LANES), F32)],
         [SMEM] + [VMEM] * 3,
         flops=10**10,
-    )(dev, lengths, got, key_cache.reshape(cache))
+    )(dev, lengths, tiles, key_cache.reshape(cache))
     sent = call(value_kernel, part, [VMEM] * 5, flops=10**10)(*scored, value_cache.reshape(cache))
     got = exchange(sent)
     sent = call(finish_kernel, part, [SMEM, SMEM] + [VMEM] * 5)(

time: 103 us -> 103 us (level)
  no operation moved by 1% of the time
where the time goes in v5:
time: 103 us
  starting transfers between devices  48.4 us (47%)
  waiting for transfers between devices  39.2 us (38%)
  Pallas kernels  10.7 us (10%)
  local copies, waits for them, and re-layouts  2.82 us (3%)
  other arithmetic  1.03 us (1%)
    all_to_all x4, waiting for transfers between devices, exchange(): x = lax.all_to_all(x, D_AXES, split_axis=0, concat_axis=0, tiled=True)  34.2 us
    all_to_all x4, starting transfers between devices, exchange(): x = lax.all_to_all(x, D_AXES, split_axis=0, concat_axis=0, tiled=True)  29.2 us
    ppermute x1, starting transfers between devices, shards(): r1 = lax.ppermute(r1, 'core', SWAP)  4.37 us
    ppermute x4, starting transfers between devices, to_groups(): return (lax.ppermute(x, 'core', SWAP), far, lax.ppermute(far, 'core', SWAP))  3.89 us
    ppermute x1, starting transfers between devices, shards(): far = lax.ppermute(wq, 'xh', SWAP)  3.66 us
    ppermute x2, starting transfers between devices, to_groups(): far = lax.ppermute(x, 'xh', SWAP)  3.06 us
    pallas_call x1, Pallas kernels, shards(): call(pack_kernel, struct((N_DEV * PIECE, LANES), BF16), [SMEM] + [ANY] *...  2.15 us
  transfers between devices with their start and end apart: 15, of which 9 were waited for; matrix products, arithmetic and copies ran while one was open for 1% of the time, Pallas kernels for 8%

profile of v5, /device:TPU:1, one launch (start us, length us, event | category | flops | bytes accessed | tf_op | source)
XLA Modules:
  0.0 103.0 jit_solution(14374185259396256973)
XLA Ops:
  0.6 3.7 %collective-permute-start = (bf16[28,5120]{1,0:T(8,128)(2,1)}, bf16[28,5120]{1,0:T(8,128)(2,1)S(1)}, u32[]{:S(2)}, u32[]{:S(2)}) collective-permute-start(bf16[28,5120]{1,0:T(8,128)(2,1)} %bitcast.21), channel_id=1, source_target_pairs={{0,128},{128,0},{1,129},{129,1},{2,130},{130,2},{3,131},{131,3},{4... | collective-permute-start | bytes 860168 | tf_op jit(solution)/shard_map/ppermute | solution.py:417
  4.3 2.1 %shard_map.111 = bf16[2560,128]{1,0:T(8,128)(2,1)} custom-call(s32[1]{0:T(128)} %bitcast.dev_ref, bf16[8,80]{1,0:T(8,128)(2,1)} %hidden_hbm.1, bf16[28,5120]{1,0:T(8,128)(2,1)} %bitcast.22, bf16[20,5120]{1,0:T(8,128)(2,1)} %bitcast.32), custom_call_target="tpu_custom_call" | custom-call | tf_op jit(solution)/shard_map/pallas_call | solution.py:420
  6.5 11.9 %all-to-all-start = ((bf16[64,40,128]{2,1,0:T(8,128)(2,1)}), bf16[64,40,128]{2,1,0:T(8,128)(2,1)S(1)}, u32[]{:S(2)}, u32[]{:S(2)}) async-start(bf16[64,40,128]{2,1,0:T(8,128)(2,1)} %bitcast.31), calls=%async_computation | async-start | bytes 1310720 | tf_op jit(solution)/shard_map/all_to_all | solution.py:406
  19.0 1.3 %collective-permute-start.1 = (bf16[2,28,5120]{2,0,1:T(2,128)(2,1)S(1)}, bf16[2,28,5120]{2,0,1:T(2,128)(2,1)S(1)}, u32[]{:S(2)}, u32[]{:S(2)}) collective-permute-start(bf16[2,28,5120]{2,0,1:T(2,128)(2,1)S(1)} %copy.12), channel_id=1, source_target_pairs={{0,64},{64,0},{1,65},{65,1},{2,66},{66,2},{3,67},{67,3},{4,68},{68... | collective-permute-start | bytes 1720328 | tf_op jit(solution)/shard_map/ppermute | solution.py:418
  20.4 1.6 %collective-permute-done.1 = bf16[2,28,5120]{2,0,1:T(2,128)(2,1)S(1)} collective-permute-done((bf16[2,28,5120]{2,0,1:T(2,128)(2,1)S(1)}, bf16[2,28,5120]{2,0,1:T(2,128)(2,1)S(1)}, u32[]{:S(2)}, u32[]{:S(2)}) %collective-permute-start.1) | collective-permute-done | bytes 573472 | tf_op jit(solution)/shard_map/ppermute | solution.py:418
  22.2 15.0 %all-to-all-done = bf16[64,40,128]{2,1,0:T(8,128)(2,1)S(1)} async-done(((bf16[64,40,128]{2,1,0:T(8,128)(2,1)}), bf16[64,40,128]{2,1,0:T(8,128)(2,1)S(1)}, u32[]{:S(2)}, u32[]{:S(2)}) %all-to-all-start) | async-done | bytes 655392 | tf_op jit(solution)/shard_map/all_to_all | solution.py:406
  37.2 1.3 %shard_map.113.after_ref = bf16[512,128]{1,0:T(8,128)(2,1)} custom-call(s32[1]{0:T(128)} %bitcast.dev_ref, s32[1]{0:T(128)} %bitcast.2.group_ref, bf16[2560,128]{1,0:T(8,128)(2,1)S(1)} %bitcast.18, bf16[128,5120]{1,0:T(8,128)(2,1)S(1)} %shard_map.112.w_ref), custom_call_target="tpu_custom_call" | custom-call | tf_op jit(solution)/shard_map/pallas_call | solution.py:436
  38.5 6.6 %all-to-all-start.1 = ((bf16[64,8,128]{2,1,0:T(8,128)(2,1)}), bf16[64,8,128]{2,1,0:T(8,128)(2,1)S(1)}, u32[]{:S(2)}, u32[]{:S(2)}) async-start(bf16[64,8,128]{2,1,0:T(8,128)(2,1)} %bitcast.9), calls=%async_computation.1 | async-start | bytes 262144 | tf_op jit(solution)/shard_map/all_to_all | solution.py:406
  46.4 1.8 %collective-permute-start.3 = (bf16[80,1280]{1,0:T(8,128)(2,1)S(1)}, bf16[80,1280]{1,0:T(8,128)(2,1)S(1)}, u32[]{:S(2)}, u32[]{:S(2)}) collective-permute-start(bf16[80,1280]{1,0:T(8,128)(2,1)S(1)} %get-tuple-element.23.b0_ref.refs_4_), channel_id=1, source_target_pairs={{0,128},{128,0},{1,129},{129,1},{2,130},{130,2},{3,131},{131,3},{4... | collective-permute-start | bytes 614408 | tf_op jit(solution)/shard_map/ppermute | solution.py:391
  48.2 1.2 %collective-permute-start.6 = (bf16[80,1792]{1,0:T(8,128)(2,1)S(1)}, bf16[80,1792]{1,0:T(8,128)(2,1)S(1)}, u32[]{:S(2)}, u32[]{:S(2)}) collective-permute-start(bf16[80,1792]{1,0:T(8,128)(2,1)S(1)} %shard_map.119.refs_0_), channel_id=1, source_target_pairs={{0,128},{128,0},{1,129},{129,1},{2,130},{130,2},{3,131},{131,3},{4... | collective-permute-start | bytes 860168 | tf_op jit(solution)/shard_map/ppermute | solution.py:391
  49.4 5.7 %all-to-all-done.1 = bf16[64,8,128]{2,1,0:T(8,128)(2,1)S(1)} async-done(((bf16[64,8,128]{2,1,0:T(8,128)(2,1)}), bf16[64,8,128]{2,1,0:T(8,128)(2,1)S(1)}, u32[]{:S(2)}, u32[]{:S(2)}) %all-to-all-start.1) | async-done | bytes 131104 | tf_op jit(solution)/shard_map/all_to_all | solution.py:406
  55.2 1.4 %copy-done.2 = bf16[8,128,1024]{2,1,0:T(8,128)(2,1)S(1)} copy-done((bf16[8,128,1024]{2,1,0:T(8,128)(2,1)S(1)}, bf16[8,128,1024]{2,1,0:T(8,128)(2,1)}, u32[]{:S(2)}) %copy-start.2) | copy-done | bytes 2097176
  58.3 1.3 %shard_map.117 = bf16[512,128]{1,0:T(8,128)(2,1)} custom-call(bf16[384,1024]{1,0:T(8,128)(2,1)S(1)} %get-tuple-element.19.spread_ref, f32[320,128]{1,0:T(8,128)S(1)} %get-tuple-element.20.own_ref, f32[320,128]{1,0:T(8,128)S(1)} %get-tuple-element.21.tag_ref, f32[64,128]{1,0:T(8,128)S(1)} %get-tuple-element.22.fresh_ref, bf16[1024,1024]{1,0:T(8,128)(2,1)S(1)} %bitcast.30), custom_call_target="tpu_custom_call" | custom-call | flops 10000000000 | bytes 4194304 | tf_op jit(solution)/shard_map/pallas_call | solution.py:466
  59.6 5.1 %all-to-all-start.2 = ((bf16[64,8,128]{2,1,0:T(8,128)(2,1)}), bf16[64,8,128]{2,1,0:T(8,128)(2,1)S(1)}, u32[]{:S(2)}, u32[]{:S(2)}) async-start(bf16[64,8,128]{2,1,0:T(8,128)(2,1)} %bitcast.13), calls=%async_computation.2 | async-start | bytes 262144 | tf_op jit(solution)/shard_map/all_to_all | solution.py:406
  64.7 3.3 %collective-permute-start.2 = (bf16[80,1280]{1,0:T(8,128)(2,1)S(1)}, bf16[80,1280]{1,0:T(8,128)(2,1)S(1)}, u32[]{:S(2)}, u32[]{:S(2)}) collective-permute-start(bf16[80,1280]{1,0:T(8,128)(2,1)S(1)} %get-tuple-element.23.b0_ref.refs_4_), channel_id=1, source_target_pairs={{0,64},{64,0},{1,65},{65,1},{2,66},{66,2},{3,67},{67,3},{4,68},{68... | collective-permute-start | bytes 614408 | tf_op jit(solution)/shard_map/ppermute | solution.py:392
  69.4 5.4 %all-to-all-done.2 = bf16[64,8,128]{2,1,0:T(8,128)(2,1)S(1)} async-done(((bf16[64,8,128]{2,1,0:T(8,128)(2,1)}), bf16[64,8,128]{2,1,0:T(8,128)(2,1)S(1)}, u32[]{:S(2)}, u32[]{:S(2)}) %all-to-all-start.2) | async-done | bytes 131104 | tf_op jit(solution)/shard_map/all_to_all | solution.py:406
  74.8 1.3 %shard_map.118.after_ref = bf16[512,128]{1,0:T(8,128)(2,1)} custom-call(s32[1]{0:T(128)} %bitcast.dev_ref, s32[1]{0:T(128)} %bitcast.2.group_ref, bf16[512,128]{1,0:T(8,128)(2,1)S(1)} %bitcast.26, bf16[80,1280]{1,0:T(8,128)(2,1)S(1)} %get-tuple-element.23.b0_ref.refs_4_, bf16[80,1280]{1,0:T(8,128)(2,1)S(1)} %collective-permute-done.2.b1_ref.refs_5_, ...), custom_call_target="tpu_custom_call" | custom-call | tf_op jit(solution)/shard_map/pallas_call | solution.py:468
  76.1 5.7 %all-to-all-start.3 = ((bf16[64,8,128]{2,1,0:T(8,128)(2,1)}), bf16[64,8,128]{2,1,0:T(8,128)(2,1)S(1)}, u32[]{:S(2)}, u32[]{:S(2)}) async-start(bf16[64,8,128]{2,1,0:T(8,128)(2,1)} %bitcast.15), calls=%async_computation.3 | async-start | bytes 262144 | tf_op jit(solution)/shard_map/all_to_all | solution.py:406
  82.2 1.4 %shard_map.120 = (bf16[80,7168]{1,0:T(8,128)(2,1)}, bf16[80,5120]{1,0:T(8,128)(2,1)}, f32[8,128]{1,0:T(8,128)S(1)}) custom-call(s32[1]{0:T(128)} %bitcast.2.group_ref, bf16[512,128]{1,0:T(8,128)(2,1)} %shard_map.118.after_ref, bf16[80,1792]{1,0:T(8,128)(2,1)S(1)} %shard_map.119.refs_0_, bf16[80,1792]{1,0:T(8,128)(2,1)S(1)} %collective-permute-done.5.refs_1_, ...), custom_call_target="tpu_custom_call" | custom-call | tf_op jit(solution)/shard_map/pallas_call | solution.py:471
  83.6 8.2 %all-to-all-done.3 = bf16[64,8,128]{2,1,0:T(8,128)(2,1)S(1)} async-done(((bf16[64,8,128]{2,1,0:T(8,128)(2,1)}), bf16[64,8,128]{2,1,0:T(8,128)(2,1)S(1)}, u32[]{:S(2)}, u32[]{:S(2)}) %all-to-all-start.3) | async-done | bytes 131104 | tf_op jit(solution)/shard_map/all_to_all | solution.py:406
  92.5 4.4 %collective-permute-start.10 = (f32[2,80]{1,0:T(2,128)S(1)}, f32[2,80]{1,0:T(2,128)S(1)}, u32[]{:S(2)}, u32[]{:S(2)}) collective-permute-start(f32[2,80]{1,0:T(2,128)S(1)} %get-tuple-element.28), channel_id=1, source_target_pairs={{0,64},{64,0},{1,65},{65,1},{2,66},{66,2},{3,67},{67,3},{4,68},{68... | collective-permute-start | bytes 1928 | tf_op jit(solution)/shard_map/ppermute | solution.py:492
  96.8 1.6 %collective-permute-start.8 = (f32[2,80]{1,0:T(2,128)S(1)}, f32[2,80]{1,0:T(2,128)S(1)}, u32[]{:S(2)}, u32[]{:S(2)}) collective-permute-start(f32[2,80]{1,0:T(2,128)S(1)} %get-tuple-element.26), channel_id=1, source_target_pairs={{0,192},{64,128},{128,64},{192,0},{1,193},{65,129},{129,65},{193,1... | collective-permute-start | bytes 1928 | tf_op jit(solution)/shard_map/ppermute | solution.py:494
  98.4 1.2 %collective-permute-start.9 = (f32[2,80]{1,0:T(2,128)S(1)}, f32[2,80]{1,0:T(2,128)S(1)}, u32[]{:S(2)}, u32[]{:S(2)}) collective-permute-start(f32[2,80]{1,0:T(2,128)S(1)} %get-tuple-element.27), channel_id=1, source_target_pairs={{0,128},{128,0},{1,129},{129,1},{2,130},{130,2},{3,131},{131,3},{4... | collective-permute-start | bytes 1928 | tf_op jit(solution)/shard_map/ppermute | solution.py:493
  99.7 1.6 %collective-permute-done.8 = f32[2,80]{1,0:T(2,128)S(1)} collective-permute-done((f32[2,80]{1,0:T(2,128)S(1)}, f32[2,80]{1,0:T(2,128)S(1)}, u32[]{:S(2)}, u32[]{:S(2)}) %collective-permute-start.8) | collective-permute-done | bytes 672 | tf_op jit(solution)/shard_map/ppermute | solution.py:494
  (45 shorter events, 8.0 us)
Async XLA Ops:
  0.6 17.7 %copy-start = (bf16[5120,28]{0,1:T(8,128)(2,1)S(1)}, bf16[5120,28]{0,1:T(8,128)(2,1)}, u32[]{:S(2)}) copy-start(bf16[5120,28]{0,1:T(8,128)(2,1)} %param.9) | copy-start | bytes 860164
  0.6 17.7 %collective-permute-start = (bf16[28,5120]{1,0:T(8,128)(2,1)}, bf16[28,5120]{1,0:T(8,128)(2,1)S(1)}, u32[]{:S(2)}, u32[]{:S(2)}) collective-permute-start(bf16[28,5120]{1,0:T(8,128)(2,1)} %bitcast.21), channel_id=1, source_target_pairs={{0,128},{128,0},{1,129},{129,1},{2,130},{130,2},{3,131},{131,3},{4... | collective-permute-start | bytes 860168 | tf_op jit(solution)/shard_map/ppermute | solution.py:417
  6.5 30.7 %all-to-all-start = ((bf16[64,40,128]{2,1,0:T(8,128)(2,1)}), bf16[64,40,128]{2,1,0:T(8,128)(2,1)S(1)}, u32[]{:S(2)}, u32[]{:S(2)}) async-start(bf16[64,40,128]{2,1,0:T(8,128)(2,1)} %bitcast.31), calls=%async_computation | async-start | bytes 1310720 | tf_op jit(solution)/shard_map/all_to_all | solution.py:406
  19.0 2.9 %collective-permute-start.1 = (bf16[2,28,5120]{2,0,1:T(2,128)(2,1)S(1)}, bf16[2,28,5120]{2,0,1:T(2,128)(2,1)S(1)}, u32[]{:S(2)}, u32[]{:S(2)}) collective-permute-start(bf16[2,28,5120]{2,0,1:T(2,128)(2,1)S(1)} %copy.12), channel_id=1, source_target_pairs={{0,64},{64,0},{1,65},{65,1},{2,66},{66,2},{3,67},{67,3},{4,68},{68... | collective-permute-start | bytes 1720328 | tf_op jit(solution)/shard_map/ppermute | solution.py:418
  22.1 23.0 %copy-start.5 = (s32[8]{0:T(128)S(1)}, s32[8]{0:T(128)}, u32[]{:S(2)}) copy-start(s32[8]{0:T(128)} %param.14) | copy-start | bytes 100
  22.2 23.2 %copy-start.1 = (s32[8]{0:T(128)S(1)}, s32[8]{0:T(128)}, u32[]{:S(2)}) copy-start(s32[8]{0:T(128)} %lengths_ref.1) | copy-start | bytes 100
  38.5 16.6 %all-to-all-start.1 = ((bf16[64,8,128]{2,1,0:T(8,128)(2,1)}), bf16[64,8,128]{2,1,0:T(8,128)(2,1)S(1)}, u32[]{:S(2)}, u32[]{:S(2)}) async-start(bf16[64,8,128]{2,1,0:T(8,128)(2,1)} %bitcast.9), calls=%async_computation.1 | async-start | bytes 262144 | tf_op jit(solution)/shard_map/all_to_all | solution.py:406
  46.4 21.6 %collective-permute-start.3 = (bf16[80,1280]{1,0:T(8,128)(2,1)S(1)}, bf16[80,1280]{1,0:T(8,128)(2,1)S(1)}, u32[]{:S(2)}, u32[]{:S(2)}) collective-permute-start(bf16[80,1280]{1,0:T(8,128)(2,1)S(1)} %get-tuple-element.23.b0_ref.refs_4_), channel_id=1, source_target_pairs={{0,128},{128,0},{1,129},{129,1},{2,130},{130,2},{3,131},{131,3},{4... | collective-permute-start | bytes 614408 | tf_op jit(solution)/shard_map/ppermute | solution.py:391
  48.2 20.4 %collective-permute-start.6 = (bf16[80,1792]{1,0:T(8,128)(2,1)S(1)}, bf16[80,1792]{1,0:T(8,128)(2,1)S(1)}, u32[]{:S(2)}, u32[]{:S(2)}) collective-permute-start(bf16[80,1792]{1,0:T(8,128)(2,1)S(1)} %shard_map.119.refs_0_), channel_id=1, source_target_pairs={{0,128},{128,0},{1,129},{129,1},{2,130},{130,2},{3,131},{131,3},{4... | collective-permute-start | bytes 860168 | tf_op jit(solution)/shard_map/ppermute | solution.py:391
  55.1 1.6 %copy-start.2 = (bf16[8,128,1024]{2,1,0:T(8,128)(2,1)S(1)}, bf16[8,128,1024]{2,1,0:T(8,128)(2,1)}, u32[]{:S(2)}) copy-start(bf16[8,128,1024]{2,1,0:T(8,128)(2,1)} %param.11) | copy-start | bytes 6291460
  56.7 1.6 %copy-start.3 = (bf16[8,128,1024]{2,1,0:T(8,128)(2,1)S(1)}, bf16[8,128,1024]{2,1,0:T(8,128)(2,1)}, u32[]{:S(2)}) copy-start(bf16[8,128,1024]{2,1,0:T(8,128)(2,1)} %param.12) | copy-start | bytes 6291460
  58.3 9.8 %copy-start.4 = (s32[8]{0:T(128)S(1)}, s32[8]{0:T(128)}, u32[]{:S(2)}) copy-start(s32[8]{0:T(128)} %param.15) | copy-start | bytes 100
  59.6 15.2 %all-to-all-start.2 = ((bf16[64,8,128]{2,1,0:T(8,128)(2,1)}), bf16[64,8,128]{2,1,0:T(8,128)(2,1)S(1)}, u32[]{:S(2)}, u32[]{:S(2)}) async-start(bf16[64,8,128]{2,1,0:T(8,128)(2,1)} %bitcast.13), calls=%async_computation.2 | async-start | bytes 262144 | tf_op jit(solution)/shard_map/all_to_all | solution.py:406
  64.7 4.3 %collective-permute-start.2 = (bf16[80,1280]{1,0:T(8,128)(2,1)S(1)}, bf16[80,1280]{1,0:T(8,128)(2,1)S(1)}, u32[]{:S(2)}, u32[]{:S(2)}) collective-permute-start(bf16[80,1280]{1,0:T(8,128)(2,1)S(1)} %get-tuple-element.23.b0_ref.refs_4_), channel_id=1, source_target_pairs={{0,64},{64,0},{1,65},{65,1},{2,66},{66,2},{3,67},{67,3},{4,68},{68... | collective-permute-start | bytes 614408 | tf_op jit(solution)/shard_map/ppermute | solution.py:392
  68.0 1.5 %collective-permute-start.4 = (bf16[80,1280]{1,0:T(8,128)(2,1)S(1)}, bf16[80,1280]{1,0:T(8,128)(2,1)S(1)}, u32[]{:S(2)}, u32[]{:S(2)}) collective-permute-start(bf16[80,1280]{1,0:T(8,128)(2,1)S(1)} %collective-permute-done.3.b2_ref.refs_6_), channel_id=1, source_target_pairs={{0,64},{64,0},{1,65},{65,1},{2,66},{66,2},{3,67},{67,3},{4,68},{68... | collective-permute-start | bytes 614408 | tf_op jit(solution)/shard_map/ppermute | solution.py:392
  68.2 14.0 %collective-permute-start.5 = (bf16[80,1792]{1,0:T(8,128)(2,1)S(1)}, bf16[80,1792]{1,0:T(8,128)(2,1)S(1)}, u32[]{:S(2)}, u32[]{:S(2)}) collective-permute-start(bf16[80,1792]{1,0:T(8,128)(2,1)S(1)} %shard_map.119.refs_0_), channel_id=1, source_target_pairs={{0,64},{64,0},{1,65},{65,1},{2,66},{66,2},{3,67},{67,3},{4,68},{68... | collective-permute-start | bytes 860168 | tf_op jit(solution)/shard_map/ppermute | solution.py:392
  68.6 13.6 %collective-permute-start.7 = (bf16[80,1792]{1,0:T(8,128)(2,1)S(1)}, bf16[80,1792]{1,0:T(8,128)(2,1)S(1)}, u32[]{:S(2)}, u32[]{:S(2)}) collective-permute-start(bf16[80,1792]{1,0:T(8,128)(2,1)S(1)} %collective-permute-done.6.refs_2_), channel_id=1, source_target_pairs={{0,64},{64,0},{1,65},{65,1},{2,66},{66,2},{3,67},{67,3},{4,68},{68... | collective-permute-start | bytes 860168 | tf_op jit(solution)/shard_map/ppermute | solution.py:392
  76.1 15.7 %all-to-all-start.3 = ((bf16[64,8,128]{2,1,0:T(8,128)(2,1)}), bf16[64,8,128]{2,1,0:T(8,128)(2,1)S(1)}, u32[]{:S(2)}, u32[]{:S(2)}) async-start(bf16[64,8,128]{2,1,0:T(8,128)(2,1)} %bitcast.15), calls=%async_computation.3 | async-start | bytes 262144 | tf_op jit(solution)/shard_map/all_to_all | solution.py:406
  92.5 7.2 %collective-permute-start.10 = (f32[2,80]{1,0:T(2,128)S(1)}, f32[2,80]{1,0:T(2,128)S(1)}, u32[]{:S(2)}, u32[]{:S(2)}) collective-permute-start(f32[2,80]{1,0:T(2,128)S(1)} %get-tuple-element.28), channel_id=1, source_target_pairs={{0,64},{64,0},{1,65},{65,1},{2,66},{66,2},{3,67},{67,3},{4,68},{68... | collective-permute-start | bytes 1928 | tf_op jit(solution)/shard_map/ppermute | solution.py:492
  96.8 4.5 %collective-permute-start.8 = (f32[2,80]{1,0:T(2,128)S(1)}, f32[2,80]{1,0:T(2,128)S(1)}, u32[]{:S(2)}, u32[]{:S(2)}) collective-permute-start(f32[2,80]{1,0:T(2,128)S(1)} %get-tuple-element.26), channel_id=1, source_target_pairs={{0,192},{64,128},{128,64},{192,0},{1,193},{65,129},{129,65},{193,1... | collective-permute-start | bytes 1928 | tf_op jit(solution)/shard_map/ppermute | solution.py:494
  98.4 3.9 %collective-permute-start.9 = (f32[2,80]{1,0:T(2,128)S(1)}, f32[2,80]{1,0:T(2,128)S(1)}, u32[]{:S(2)}, u32[]{:S(2)}) collective-permute-start(f32[2,80]{1,0:T(2,128)S(1)} %get-tuple-element.27), channel_id=1, source_target_pairs={{0,128},{128,0},{1,129},{129,1},{2,130},{130,2},{3,131},{131,3},{4... | collective-permute-start | bytes 1928 | tf_op jit(solution)/shard_map/ppermute | solution.py:493
